TPU v7x, 32 devices: a whole 2x2x4 slice. The times are simulated.
32 devices in a mesh: slab: 4 (over y, x), mode: 8 (over z, core).
Axes of the slice: x: 2, y: 2, z: 4, core: 2. Of those that a mesh axis runs over, the one named last changes fastest.
Arguments:
- tensor: bfloat16 [512, 16384], P('mode', 'slab'), may hold values from -24 to 24, as said below
- start_block: float32 [512, 128], replicated, may hold values from -6 to 6
Outputs:
- basis_rows: float32 [512, 128], P('mode')
- core_coeffs: float32 [16384, 128], P(('slab', 'mode'))
Inputs may be any that keep to these rules, and one draw needn't show every extreme that they name: `tensor`: entries of the unfolding; each is a row factor times a column factor times a bounded random term.
All inputs are finite; a program needn't handle non-finite values.
Results may differ from a plain program's by a relative error of at most 0.0029.
Values may be sent and summed in bfloat16 or wider, within the bound.
No kernel may reach another device: no remote copies, remote signals or barrier semaphores. Data moves between devices by JAX's collectives and lax.ppermute only.
A program may use at most 64 MiB of HBM per device.

v0:
```python
import jax
import jax.numpy as jnp
from jax import lax
from jax.sharding import PartitionSpec as P

highest = lax.Precision.HIGHEST
contract_rows = (((0,), (0,)), ((), ()))


def orthonormal(image_block):
    small_gram = jnp.dot(image_block.T, image_block, precision=highest)
    factor = jnp.linalg.cholesky(small_gram)
    return lax.linalg.triangular_solve(
        factor, image_block, left_side=False, lower=True, transpose_a=True
    )


def shards(tensor, start_block):
    row_count = tensor.shape[0]
    mode_index = lax.axis_index("mode")
    regrouped = lax.all_to_all(tensor, "mode", split_axis=1, concat_axis=0, tiled=True)
    inner_block = jnp.dot(
        regrouped.T, start_block, precision=highest, preferred_element_type=jnp.float32
    )
    partial_image = jnp.dot(
        regrouped, inner_block, precision=highest, preferred_element_type=jnp.float32
    )
    image_block = lax.psum(partial_image, ("slab", "mode"))
    basis_full = orthonormal(image_block)
    basis_low = basis_full.astype(jnp.bfloat16)
    basis_rows = lax.dynamic_slice_in_dim(basis_full, mode_index * row_count, row_count, 0)
    core_coeffs = lax.dot_general(
        regrouped, basis_low, contract_rows, preferred_element_type=jnp.float32
    )
    return (basis_rows, core_coeffs)


def solution(mesh):
    placed = (P("mode", "slab"), P())
    return jax.shard_map(
        shards,
        mesh=mesh,
        in_specs=placed,
        out_specs=(P("mode", None), P(("slab", "mode"), None)),
        check_vma=False,
    )
```

profile of v0, /device:TPU:0, one launch (start us, length us, event | category | flops | bytes accessed | tf_op | source)
XLA Modules:
  0.0 189.7 jit_solution(16917536051712438762)
XLA Ops:
  7.2 0.0 copy-start
  7.2 0.0 all-reduce.2.cloned.1.call-start
  7.2 1.1 copy.16
  8.3 21.5 %all_to_all.19 = bf16[64,8,512]{2,0,1:T(8,128)(2,1)S(1)} all-to-all(bf16[64,8,512]{2,0,1:T(8,128)(2,1)S(1)} %bitcast.31), channel_id=1, replica_groups=mesh['slab'=4,'mode'=8] {'mode'}, dimensions={1} | all-to-all | bytes 1048576 | tf_op jit(solution)/shard_map/all_to_all | solution.py:21
  29.8 0.0 copy-done
  29.8 0.7 fusion.5
  30.5 1.4 convolution_bitcast_fusion.1
  32.0 0.0 all-reduce.2.cloned.1.call-update
  32.0 124.1 %all-reduce.2.cloned.1.call-done = f32[512,128]{0,1:T(8,128)} async-done(((f32[512,128]{0,1:T(8,128)}), f32[512,128]{0,1:T(8,128)}) %all-reduce.2.cloned.1.call-update) | async-done | bytes 262160 | tf_op jit(solution)/shard_map/psum | solution.py:28
  156.1 1.4 fusion.6
  157.5 0.0 copy-start.1
  157.5 0.1 copy.12
  157.6 11.7 %cholesky.16 = f32[128,128]{1,0:T(8,128)S(1)} custom-call(f32[128,128]{1,0:T(8,128)S(1)} %fusion.4), custom_call_target="Cholesky" | custom-call | tf_op jit(solution)/shard_map/jit(cholesky)/cholesky | solution.py:12
  169.4 0.6 compare_reduce_fusion
  170.0 0.7 fusion.1
  170.7 9.8 %custom-call.6 = f32[1,128,128]{1,2,0:T(8,128)S(1)} custom-call(f32[1,128,128]{2,1,0:T(8,128)S(1)} %fusion.1), custom_call_target="InvertDiagBlocksLowerTriangular" | custom-call | tf_op jit(solution)/shard_map/triangular_solve | solution.py:13
  180.5 0.0 copy-done.1
  180.5 0.6 fusion.2
  181.1 0.3 convolution_bitcast_fusion
  181.4 0.6 constant_dynamic-slice_fusion
  182.0 0.8 copy.13
  (2 shorter events, 0.0 us)
Async XLA Ops:
  7.2 22.7 %copy-start = (f32[512,128]{1,0:T(8,128)S(1)}, f32[512,128]{1,0:T(8,128)}, u32[]{:S(2)}) copy-start(f32[512,128]{1,0:T(8,128)} %param.3) | copy-start | bytes 786436
  7.2 148.9 %all-reduce.2.cloned.1.call-start = ((), (), s32[]{:S(2)}) async-start(), calls=%async_computation.1 | async-start | bytes 524288 | tf_op jit(solution)/shard_map/psum | solution.py:28
  157.5 23.0 %copy-start.1 = (f32[512,128]{0,1:T(8,128)S(1)}, f32[512,128]{0,1:T(8,128)}, u32[]{:S(2)}) copy-start(f32[512,128]{0,1:T(8,128)} %all-reduce.2.cloned.1.call-done) | copy-start | bytes 786436
Sparse Core Ops, SparseCore 0:
  32.1 123.9 all-reduce.1
where the time goes:
time: 190 us
  waiting for transfers between devices  124 us (65%)
  other arithmetic  22.9 us (12%)
  blocking collectives  21.5 us (11%)
  between operations  14.1 us (7%)
  matrix products  4.36 us (2%)
  local copies, waits for them, and re-layouts  2.67 us (1%)
    psum x1, waiting for transfers between devices, shards(): image_block = lax.psum(partial_image, ('slab', 'mode'))  124 us
    all_to_all x1, blocking collectives, shards(): lax.all_to_all(tensor, 'mode', split_axis=1, concat_axis=0, tiled=True)  21.5 us
    another operation x3, other arithmetic, orthonormal(): factor = jnp.linalg.cholesky(small_gram)  12.4 us
    another operation x2, other arithmetic, orthonormal(): lax.linalg.triangular_solve(factor, image_block, left_side=False, lower=T...  10.5 us
  transfers between devices with their start and end apart: 1, of which 1 were waited for; matrix products, arithmetic and copies ran while one was open for 0% of the time, Pallas kernels for 0%

commit v1 on v0

v1 whole, which is shorter than its diff:
```python
import functools

import jax
import jax.numpy as jnp
from jax import lax
from jax.experimental import pallas as pl
from jax.experimental.pallas import tpu as pltpu
from jax.sharding import PartitionSpec as P

highest = lax.Precision.HIGHEST
f32 = jnp.float32
bf16 = jnp.bfloat16
contract_rows = (((0,), (0,)), ((), ()))
contract_last = (((1,), (1,)), ((), ()))


def two_parts(value):
    high = value.astype(bf16)
    return high, (value - high.astype(f32)).astype(bf16)


def dot(lhs, rhs, dims):
    return lax.dot_general(lhs, rhs, dims, preferred_element_type=f32)


def in_vmem(count):
    return [pl.BlockSpec(memory_space=pltpu.VMEM)] * count


def inner_kernel(chips, start_ref, *refs):
    blocks, (inner_ref, held_ref) = refs[:chips], refs[chips:]
    mode_index = lax.axis_index("mode")
    chip, core = mode_index // 2, mode_index % 2
    rows = blocks[0].shape[0]
    starts = []
    for step in range(chips):
        source = lax.rem(chip + chips - step, chips)
        held_ref[pl.ds(pl.multiple_of(source * rows, rows), rows), :] = blocks[step][...]
        first = pl.multiple_of((source * 2 + core) * rows, rows)
        starts.append(start_ref[pl.ds(first, rows), :])
    ordered = jnp.concatenate([block[...] for block in blocks], axis=0)
    high, low = two_parts(jnp.concatenate(starts, axis=0))
    inner_ref[...] = dot(high, ordered, contract_rows) + dot(low, ordered, contract_rows)


def image_kernel(held_ref, own_ref, other_ref, image_ref):
    high, low = two_parts(own_ref[...] + other_ref[...])
    held = held_ref[...]
    image_ref[...] = dot(held, high, contract_last) + dot(held, low, contract_last)


def swap(value, axis, mask):
    count = lax.axis_size(axis)
    return lax.ppermute(value, axis, [(i, i ^ mask) for i in range(count)])


def add_four(value, axis, first, second):
    near = swap(value, axis, first)
    side = swap(value, axis, second)
    far = swap(value, axis, first ^ second)
    return (value + near) + (side + far)


def add_over(value, axis, masks):
    masks = list(masks)
    while len(masks) >= 2:
        value = add_four(value, axis, masks.pop(0), masks.pop(0))
    if masks:
        value = value + swap(value, axis, masks.pop())
    return value


def orthonormal(image_block):
    small_gram = jnp.dot(image_block.T, image_block, precision=highest)
    factor = jnp.linalg.cholesky(small_gram)
    return lax.linalg.triangular_solve(
        factor, image_block, left_side=False, lower=True, transpose_a=True
    )


def shards(tensor, start_block):
    row_count, slab_columns = tensor.shape
    slabs, modes = lax.axis_size("slab"), lax.axis_size("mode")
    chips = modes // 2
    chip_columns = slab_columns // chips
    own_columns = chip_columns // 2
    rank = start_block.shape[1]
    mode_index = lax.axis_index("mode")
    chip, core = mode_index // 2, mode_index % 2

    def chip_block(step):
        target = lax.rem(chip + step, chips)
        return lax.dynamic_slice_in_dim(tensor, target * chip_columns, chip_columns, 1)

    blocks = [chip_block(0)] + [None] * (chips - 1)
    for step in sorted(range(1, chips), key=lambda step: -min(step, chips - step)):
        pairs = [(i, (i + 2 * step) % modes) for i in range(modes)]
        blocks[step] = lax.ppermute(chip_block(step), "mode", pairs)

    held_rows = chips * row_count
    inner, held = pl.pallas_call(
        functools.partial(inner_kernel, chips),
        out_shape=(
            jax.ShapeDtypeStruct((rank, chip_columns), f32),
            jax.ShapeDtypeStruct((held_rows, chip_columns), bf16),
        ),
        in_specs=in_vmem(1 + chips),
        out_specs=tuple(in_vmem(2)),
    )(start_block, *blocks)
    inner_other = swap(inner, "mode", 1)
    own_half = lax.dynamic_slice_in_dim(held, core * own_columns, own_columns, 1)
    away_half = lax.dynamic_slice_in_dim(held, (1 - core) * own_columns, own_columns, 1)
    other_half = swap(away_half, "mode", 1)

    image = pl.pallas_call(
        image_kernel,
        out_shape=jax.ShapeDtypeStruct((held_rows, rank), f32),
        in_specs=in_vmem(3),
        out_specs=in_vmem(1)[0],
    )(held, inner, inner_other)
    slab_masks = [1 << bit for bit in range(slabs.bit_length() - 1)]
    chip_masks = [2 * ((2 << bit) - 1) for bit in range(chips.bit_length() - 1)]
    image = add_over(image, "slab", slab_masks)
    image = add_over(image, "mode", chip_masks)

    image_other = swap(image, "mode", 1)
    even = core == 0
    image_block = jnp.concatenate(
        [jnp.where(even, image, image_other), jnp.where(even, image_other, image)], axis=0
    )
    basis_full = orthonormal(image_block)
    basis_low = basis_full.astype(bf16)
    basis_rows = lax.dynamic_slice_in_dim(
        basis_full, core * held_rows + chip * row_count, row_count, 0
    )
    regrouped = jnp.concatenate(
        [jnp.where(even, own_half, other_half), jnp.where(even, other_half, own_half)], axis=0
    )
    core_coeffs = dot(regrouped, basis_low, contract_rows)
    return (basis_rows, core_coeffs)


def solution(mesh):
    placed = (P("mode", "slab"), P())
    return jax.shard_map(
        shards,
        mesh=mesh,
        in_specs=placed,
        out_specs=(P("mode", None), P(("slab", "mode"), None)),
        check_vma=False,
    )
```

time: 190 us -> 78.8 us (0.41)
  waiting for transfers between devices: 124 us -> 27.3 us
  blocking collectives: 21.5 us -> 0 us
  starting transfers between devices: 0.04 us -> 15.7 us
  between operations: 14.1 us -> 0.81 us
  Pallas kernels: 0 us -> 4.84 us
  matrix products: 4.36 us -> 2.01 us
    psum x1 -> x0, waiting for transfers between devices: 124 us -> none  [shards(): image_block = lax.psum(partial_image, ('slab', 'mode'))]
    ppermute x0 -> x12, waiting for transfers between devices: none -> 27.3 us  [the longest x9 20 us: swap(): return lax.ppermute(value, axis, [(i, i ^ mask) for i in range(count)])]
    all_to_all x1 -> x0, blocking collectives: 21.5 us -> none  [shards(): lax.all_to_all(tensor, 'mode', split_axis=1, concat_axis=0, tiled=True)]
    ppermute x0 -> x12, starting transfers between devices: none -> 15.7 us  [the longest x9 8.69 us: swap(): return lax.ppermute(value, axis, [(i, i ^ mask) for i in range(count)])]
    pallas_call x0 -> x2, Pallas kernels: none -> 4.84 us  [the longest x1 2.45 us: shards(): pl.pallas_call(image_kernel, out_shape=jax.ShapeDtypeStruct((held_rows, r...]
  transfers between devices with their start and end apart: 1 -> 12, of which waited for: 1 -> 9; matrix products, arithmetic and copies ran while one was open for 0% -> 0% of each run, Pallas kernels for 0% -> 0%
where the time goes in v1:
time: 78.8 us; the launch traced here: 78.6 us
  waiting for transfers between devices  27.3 us (35%)
  other arithmetic  24 us (30%)
  starting transfers between devices  15.7 us (20%)
  Pallas kernels  4.84 us (6%)
  local copies, waits for them, and re-layouts  4.05 us (5%)
  matrix products  2.01 us (3%)
  between operations  0.81 us (1%)
    ppermute x9, waiting for transfers between devices, swap(): return lax.ppermute(value, axis, [(i, i ^ mask) for i in range(count)])  20 us
    another operation x3, other arithmetic, orthonormal(): factor = jnp.linalg.cholesky(small_gram)  12.4 us
    another operation x2, other arithmetic, orthonormal(): lax.linalg.triangular_solve(factor, image_block, left_side=False, lower=T...  10.5 us
    ppermute x9, starting transfers between devices, swap(): return lax.ppermute(value, axis, [(i, i ^ mask) for i in range(count)])  8.69 us
    ppermute x3, waiting for transfers between devices, shards(): blocks[step] = lax.ppermute(chip_block(step), 'mode', pairs)  7.29 us
    ppermute x3, starting transfers between devices, shards(): blocks[step] = lax.ppermute(chip_block(step), 'mode', pairs)  6.96 us
    pallas_call x1, Pallas kernels, shards(): pl.pallas_call(image_kernel, out_shape=jax.ShapeDtypeStruct((held_rows, r...  2.45 us
    pallas_call x1, Pallas kernels, shards(): pl.pallas_call(functools.partial(inner_kernel, chips), out_shape=(jax.Sha...  2.39 us
  transfers between devices with their start and end apart: 12, of which 9 were waited for; matrix products, arithmetic and copies ran while one was open for 0% of the time, Pallas kernels for 0%

profile of v1, /device:TPU:0, one launch (start us, length us, event | category | flops | bytes accessed | tf_op | source)
XLA Modules:
  0.0 78.6 jit_solution(3442171040323771022)
XLA Ops:
  0.7 1.8 %constant_dynamic-slice_fusion.2 = (bf16[64,1024]{1,0:T(8,128)(2,1)S(1)}, bf16[64,1024]{1,0:T(8,128)(2,1)S(1)}, bf16[64,1024]{1,0:T(8,128)(2,1)}, bf16[64,1024]{1,0:T(8,128)(2,1)S(1)}) fusion(bf16[64,4096]{1,0:T(8,128)(2,1)} %param.2, s32[]{:T(128)S(6)} %select_n.66, s32[]{:T(128)S(6)} %select_n.64, s32[]{:T(128)S(6)} %select_n.63, s32[]{:T(128)S(6)} %select_n.65), kind=kLoop, calls=%fused_computation.25 | loop fusion | bytes 1048592 | tf_op jit(solution)/shard_map/dynamic_slice | solution.py:93
  2.5 3.0 %collective-permute-start = (bf16[64,1024]{1,0:T(8,128)(2,1)S(1)}, bf16[64,1024]{1,0:T(8,128)(2,1)S(1)}, u32[]{:S(2)}, u32[]{:S(2)}) collective-permute-start(bf16[64,1024]{1,0:T(8,128)(2,1)S(1)} %get-tuple-element.9), channel_id=1, source_target_pairs={{0,2},{1,3},{2,4},{3,5},{4,6},{5,7},{6,0},{7,1},{8,10},{9,11},{10,... | collective-permute-start | bytes 393224 | tf_op jit(solution)/shard_map/ppermute | solution.py:98
  5.5 2.6 %collective-permute-start.1 = (bf16[64,1024]{1,0:T(8,128)(2,1)S(1)}, bf16[64,1024]{1,0:T(8,128)(2,1)S(1)}, u32[]{:S(2)}, u32[]{:S(2)}) collective-permute-start(bf16[64,1024]{1,0:T(8,128)(2,1)S(1)} %get-tuple-element.11), channel_id=1, source_target_pairs={{0,4},{1,5},{2,6},{3,7},{4,0},{5,1},{6,2},{7,3},{8,12},{9,13},{10,... | collective-permute-start | bytes 393224 | tf_op jit(solution)/shard_map/ppermute | solution.py:98
  8.1 1.3 %collective-permute-start.2 = (bf16[64,1024]{1,0:T(8,128)(2,1)S(1)}, bf16[64,1024]{1,0:T(8,128)(2,1)S(1)}, u32[]{:S(2)}, u32[]{:S(2)}) collective-permute-start(bf16[64,1024]{1,0:T(8,128)(2,1)S(1)} %get-tuple-element.8), channel_id=1, source_target_pairs={{0,6},{1,7},{2,0},{3,1},{4,2},{5,3},{6,4},{7,5},{8,14},{9,15},{10,... | collective-permute-start | bytes 393224 | tf_op jit(solution)/shard_map/ppermute | solution.py:98
  9.5 2.5 %collective-permute-done.refs_1_ = bf16[64,1024]{1,0:T(8,128)(2,1)S(1)} collective-permute-done((bf16[64,1024]{1,0:T(8,128)(2,1)S(1)}, bf16[64,1024]{1,0:T(8,128)(2,1)S(1)}, u32[]{:S(2)}, u32[]{:S(2)}) %collective-permute-start) | collective-permute-done | bytes 131104 | tf_op jit(solution)/shard_map/ppermute | solution.py:98
  12.0 4.8 %collective-permute-done.1.refs_2_ = bf16[64,1024]{1,0:T(8,128)(2,1)S(1)} collective-permute-done((bf16[64,1024]{1,0:T(8,128)(2,1)S(1)}, bf16[64,1024]{1,0:T(8,128)(2,1)S(1)}, u32[]{:S(2)}, u32[]{:S(2)}) %collective-permute-start.1) | collective-permute-done | bytes 131104 | tf_op jit(solution)/shard_map/ppermute | solution.py:98
  17.4 2.4 %shard_map.41 = (f32[128,1024]{1,0:T(8,128)}, bf16[256,1024]{1,0:T(8,128)(2,1)}) custom-call(f32[512,128]{1,0:T(8,128)} %start_ref.1, bf16[64,1024]{1,0:T(8,128)(2,1)} %get-tuple-element.10.refs_0_, bf16[64,1024]{1,0:T(8,128)(2,1)} %copy-done.2, bf16[64,1024]{1,0:T(8,128)(2,1)} %copy-done.3, bf16[64,1024]{1,0:T(8,128)(2,1)} %copy-done.4), custom_call_target="tpu_custom_call" | custom-call | tf_op jit(solution)/shard_map/pallas_call | solution.py:101
  19.8 2.1 %collective-permute-done.3.other_ref = f32[128,1024]{1,0:T(8,128)S(1)} collective-permute-done((f32[128,1024]{1,0:T(8,128)}, f32[128,1024]{1,0:T(8,128)S(1)}, u32[]{:S(2)}, u32[]{:S(2)}) %collective-permute-start.3) | collective-permute-done | bytes 524320 | tf_op jit(solution)/shard_map/ppermute | solution.py:54
  22.0 0.8 %copy-done.1 = f32[128,1024]{1,0:T(8,128)} copy-done((f32[128,1024]{1,0:T(8,128)}, f32[128,1024]{1,0:T(8,128)S(1)}, u32[]{:S(2)}) %copy-start.1) | copy-done | bytes 524312
  22.8 2.5 %shard_map.42 = f32[256,128]{1,0:T(8,128)} custom-call(bf16[256,1024]{1,0:T(8,128)(2,1)} %get-tuple-element.4.held_ref, f32[128,1024]{1,0:T(8,128)} %get-tuple-element.5.own_ref, f32[128,1024]{1,0:T(8,128)} %copy-done.1), custom_call_target="tpu_custom_call" | custom-call | tf_op jit(solution)/shard_map/pallas_call | solution.py:115
  25.2 1.5 %collective-permute-start.5 = (f32[256,128]{1,0:T(8,128)}, f32[256,128]{1,0:T(8,128)S(1)}, u32[]{:S(2)}, u32[]{:S(2)}) collective-permute-start(f32[256,128]{1,0:T(8,128)} %shard_map.42), channel_id=1, source_target_pairs={{0,16},{8,24},{16,0},{24,8},{1,17},{9,25},{17,1},{25,9},{2,18},{10... | collective-permute-start | bytes 393224 | tf_op jit(solution)/shard_map/ppermute | solution.py:54
  26.8 1.4 %collective-permute-start.6 = (f32[256,128]{1,0:T(8,128)}, f32[256,128]{1,0:T(8,128)S(1)}, u32[]{:S(2)}, u32[]{:S(2)}) collective-permute-start(f32[256,128]{1,0:T(8,128)} %shard_map.42), channel_id=1, source_target_pairs={{0,24},{8,16},{16,8},{24,0},{1,25},{9,17},{17,9},{25,1},{2,26},{10... | collective-permute-start | bytes 393224 | tf_op jit(solution)/shard_map/ppermute | solution.py:54
  28.7 4.6 %collective-permute-done.5 = f32[256,128]{1,0:T(8,128)S(1)} collective-permute-done((f32[256,128]{1,0:T(8,128)}, f32[256,128]{1,0:T(8,128)S(1)}, u32[]{:S(2)}, u32[]{:S(2)}) %collective-permute-start.5) | collective-permute-done | bytes 131104 | tf_op jit(solution)/shard_map/ppermute | solution.py:54
  33.3 0.9 %collective-permute-done.6 = f32[256,128]{1,0:T(8,128)S(1)} collective-permute-done((f32[256,128]{1,0:T(8,128)}, f32[256,128]{1,0:T(8,128)S(1)}, u32[]{:S(2)}, u32[]{:S(2)}) %collective-permute-start.6) | collective-permute-done | bytes 131104 | tf_op jit(solution)/shard_map/ppermute | solution.py:54
  34.3 0.8 collective-permute-done.4
  35.0 0.9 %add_add_fusion.1 = f32[256,128]{1,0:T(8,128)S(1)} fusion(f32[256,128]{1,0:T(8,128)S(1)} %collective-permute-done.5, f32[256,128]{1,0:T(8,128)S(1)} %collective-permute-done.6, f32[256,128]{1,0:T(8,128)} %shard_map.42, f32[256,128]{1,0:T(8,128)S(1)} %collective-permute-done.4), kind=kLoop, calls=%fused_computation.11 | loop fusion | flops 98304 | bytes 655360 | tf_op jit(solution)/shard_map/add | solution.py:61
  36.0 4.4 %collective-permute-start.8 = (f32[256,128]{1,0:T(8,128)S(1)}, f32[256,128]{1,0:T(8,128)S(1)}, u32[]{:S(2)}, u32[]{:S(2)}) collective-permute-start(f32[256,128]{1,0:T(8,128)S(1)} %add_add_fusion.1), channel_id=1, source_target_pairs={{0,6},{1,7},{2,4},{3,5},{4,2},{5,3},{6,0},{7,1},{8,14},{9,15},{10,... | collective-permute-start | bytes 393224 | tf_op jit(solution)/shard_map/ppermute | solution.py:54
  41.1 3.7 %collective-permute-done.8 = f32[256,128]{1,0:T(8,128)S(1)} collective-permute-done((f32[256,128]{1,0:T(8,128)S(1)}, f32[256,128]{1,0:T(8,128)S(1)}, u32[]{:S(2)}, u32[]{:S(2)}) %collective-permute-start.8) | collective-permute-done | bytes 131104 | tf_op jit(solution)/shard_map/ppermute | solution.py:54
  44.8 6.7 %collective-permute-done.9 = f32[256,128]{1,0:T(8,128)S(1)} collective-permute-done((f32[256,128]{1,0:T(8,128)S(1)}, f32[256,128]{1,0:T(8,128)S(1)}, u32[]{:S(2)}, u32[]{:S(2)}) %collective-permute-start.9) | collective-permute-done | bytes 131104 | tf_op jit(solution)/shard_map/ppermute | solution.py:54
  51.8 1.2 %collective-permute-done.10 = f32[256,128]{1,0:T(8,128)S(1)} collective-permute-done((f32[256,128]{1,0:T(8,128)S(1)}, f32[256,128]{1,0:T(8,128)S(1)}, u32[]{:S(2)}, u32[]{:S(2)}) %collective-permute-start.10) | collective-permute-done | bytes 131104 | tf_op jit(solution)/shard_map/ppermute | solution.py:54
  53.7 11.7 %cholesky.16 = f32[128,128]{1,0:T(8,128)S(1)} custom-call(f32[128,128]{1,0:T(8,128)S(1)} %fusion.9), custom_call_target="Cholesky" | custom-call | tf_op jit(solution)/shard_map/jit(cholesky)/cholesky | solution.py:75
  66.1 0.7 fusion.7
  66.7 9.8 %custom-call.6 = f32[1,128,128]{1,2,0:T(8,128)S(1)} custom-call(f32[1,128,128]{2,1,0:T(8,128)S(1)} %fusion.7), custom_call_target="InvertDiagBlocksLowerTriangular" | custom-call | tf_op jit(solution)/shard_map/triangular_solve | solution.py:76
  77.5 1.1 %fusion = f32[512,128]{1,0:T(8,128)} fusion(bf16[256,512]{1,0:T(8,128)(2,1)S(1)} %get-tuple-element.7, bf16[256,512]{1,0:T(8,128)(2,1)S(1)} %get-tuple-element.6, f32[512,128]{1,0:T(8,128)S(1)} %fusion.4), kind=kOutput, calls=%fused_computation | convolution fusion | flops 68222976 | bytes 1048576 | tf_op jit(solution)/shard_map/dot_general | solution.py:23
  (29 shorter events, 4.6 us)
Async XLA Ops:
  2.5 9.5 %collective-permute-start = (bf16[64,1024]{1,0:T(8,128)(2,1)S(1)}, bf16[64,1024]{1,0:T(8,128)(2,1)S(1)}, u32[]{:S(2)}, u32[]{:S(2)}) collective-permute-start(bf16[64,1024]{1,0:T(8,128)(2,1)S(1)} %get-tuple-element.9), channel_id=1, source_target_pairs={{0,2},{1,3},{2,4},{3,5},{4,6},{5,7},{6,0},{7,1},{8,10},{9,11},{10,... | collective-permute-start | bytes 393224 | tf_op jit(solution)/shard_map/ppermute | solution.py:98
  5.5 11.2 %collective-permute-start.1 = (bf16[64,1024]{1,0:T(8,128)(2,1)S(1)}, bf16[64,1024]{1,0:T(8,128)(2,1)S(1)}, u32[]{:S(2)}, u32[]{:S(2)}) collective-permute-start(bf16[64,1024]{1,0:T(8,128)(2,1)S(1)} %get-tuple-element.11), channel_id=1, source_target_pairs={{0,4},{1,5},{2,6},{3,7},{4,0},{5,1},{6,2},{7,3},{8,12},{9,13},{10,... | collective-permute-start | bytes 393224 | tf_op jit(solution)/shard_map/ppermute | solution.py:98
  8.1 8.6 %collective-permute-start.2 = (bf16[64,1024]{1,0:T(8,128)(2,1)S(1)}, bf16[64,1024]{1,0:T(8,128)(2,1)S(1)}, u32[]{:S(2)}, u32[]{:S(2)}) collective-permute-start(bf16[64,1024]{1,0:T(8,128)(2,1)S(1)} %get-tuple-element.8), channel_id=1, source_target_pairs={{0,6},{1,7},{2,0},{3,1},{4,2},{5,3},{6,4},{7,5},{8,14},{9,15},{10,... | collective-permute-start | bytes 393224 | tf_op jit(solution)/shard_map/ppermute | solution.py:98
  12.0 4.8 %copy-start.2 = (bf16[64,1024]{1,0:T(8,128)(2,1)}, bf16[64,1024]{1,0:T(8,128)(2,1)S(1)}, u32[]{:S(2)}) copy-start(bf16[64,1024]{1,0:T(8,128)(2,1)S(1)} %collective-permute-done.refs_1_) | copy-start | bytes 393220
  16.8 0.7 copy-start.3
  16.8 0.7 copy-start.4
  19.8 2.1 %collective-permute-start.3 = (f32[128,1024]{1,0:T(8,128)}, f32[128,1024]{1,0:T(8,128)S(1)}, u32[]{:S(2)}, u32[]{:S(2)}) collective-permute-start(f32[128,1024]{1,0:T(8,128)} %get-tuple-element.5.own_ref), channel_id=1, source_target_pairs={{0,1},{1,0},{2,3},{3,2},{4,5},{5,4},{6,7},{7,6},{8,9},{9,8},{10,11... | collective-permute-start | bytes 1572872 | tf_op jit(solution)/shard_map/ppermute | solution.py:54
  22.0 0.8 %copy-start.1 = (f32[128,1024]{1,0:T(8,128)}, f32[128,1024]{1,0:T(8,128)S(1)}, u32[]{:S(2)}) copy-start(f32[128,1024]{1,0:T(8,128)S(1)} %collective-permute-done.3.other_ref) | copy-start | bytes 1572868
  25.2 15.8 %copy-start = (bf16[256,1024]{1,0:T(8,128)(2,1)S(1)}, bf16[256,1024]{1,0:T(8,128)(2,1)}, u32[]{:S(2)}) copy-start(bf16[256,1024]{1,0:T(8,128)(2,1)} %get-tuple-element.4.held_ref) | copy-start | bytes 1572868
  25.2 8.1 %collective-permute-start.5 = (f32[256,128]{1,0:T(8,128)}, f32[256,128]{1,0:T(8,128)S(1)}, u32[]{:S(2)}, u32[]{:S(2)}) collective-permute-start(f32[256,128]{1,0:T(8,128)} %shard_map.42), channel_id=1, source_target_pairs={{0,16},{8,24},{16,0},{24,8},{1,17},{9,25},{17,1},{25,9},{2,18},{10... | collective-permute-start | bytes 393224 | tf_op jit(solution)/shard_map/ppermute | solution.py:54
  26.8 7.5 %collective-permute-start.6 = (f32[256,128]{1,0:T(8,128)}, f32[256,128]{1,0:T(8,128)S(1)}, u32[]{:S(2)}, u32[]{:S(2)}) collective-permute-start(f32[256,128]{1,0:T(8,128)} %shard_map.42), channel_id=1, source_target_pairs={{0,24},{8,16},{16,8},{24,0},{1,25},{9,17},{17,9},{25,1},{2,26},{10... | collective-permute-start | bytes 393224 | tf_op jit(solution)/shard_map/ppermute | solution.py:54
  28.2 6.8 %collective-permute-start.4 = (f32[256,128]{1,0:T(8,128)}, f32[256,128]{1,0:T(8,128)S(1)}, u32[]{:S(2)}, u32[]{:S(2)}) collective-permute-start(f32[256,128]{1,0:T(8,128)} %shard_map.42), channel_id=1, source_target_pairs={{0,8},{8,0},{16,24},{24,16},{1,9},{9,1},{17,25},{25,17},{2,10},{10... | collective-permute-start | bytes 393224 | tf_op jit(solution)/shard_map/ppermute | solution.py:54
  36.0 8.9 %collective-permute-start.8 = (f32[256,128]{1,0:T(8,128)S(1)}, f32[256,128]{1,0:T(8,128)S(1)}, u32[]{:S(2)}, u32[]{:S(2)}) collective-permute-start(f32[256,128]{1,0:T(8,128)S(1)} %add_add_fusion.1), channel_id=1, source_target_pairs={{0,6},{1,7},{2,4},{3,5},{4,2},{5,3},{6,0},{7,1},{8,14},{9,15},{10,... | collective-permute-start | bytes 393224 | tf_op jit(solution)/shard_map/ppermute | solution.py:54
  40.4 11.1 %collective-permute-start.9 = (f32[256,128]{1,0:T(8,128)S(1)}, f32[256,128]{1,0:T(8,128)S(1)}, u32[]{:S(2)}, u32[]{:S(2)}) collective-permute-start(f32[256,128]{1,0:T(8,128)S(1)} %add_add_fusion.1), channel_id=1, source_target_pairs={{0,4},{1,5},{2,6},{3,7},{4,0},{5,1},{6,2},{7,3},{8,12},{9,13},{10,... | collective-permute-start | bytes 393224 | tf_op jit(solution)/shard_map/ppermute | solution.py:54
  40.7 10.8 %collective-permute-start.7 = (f32[256,128]{1,0:T(8,128)S(1)}, f32[256,128]{1,0:T(8,128)S(1)}, u32[]{:S(2)}, u32[]{:S(2)}) collective-permute-start(f32[256,128]{1,0:T(8,128)S(1)} %add_add_fusion.1), channel_id=1, source_target_pairs={{0,2},{1,3},{2,0},{3,1},{4,6},{5,7},{6,4},{7,5},{8,10},{9,11},{10,... | collective-permute-start | bytes 393224 | tf_op jit(solution)/shard_map/ppermute | solution.py:54
  41.0 10.6 %collective-permute-start.11 = (bf16[256,512]{1,0:T(8,128)(2,1)S(1)}, bf16[256,512]{1,0:T(8,128)(2,1)S(1)}, u32[]{:S(2)}, u32[]{:S(2)}) collective-permute-start(bf16[256,512]{1,0:T(8,128)(2,1)S(1)} %constant_dynamic-slice_fusion), channel_id=1, source_target_pairs={{0,1},{1,0},{2,3},{3,2},{4,5},{5,4},{6,7},{7,6},{8,9},{9,8},{10,11... | collective-permute-start | bytes 786440 | tf_op jit(solution)/shard_map/ppermute | solution.py:54
  51.5 1.4 %collective-permute-start.10 = (f32[256,128]{1,0:T(8,128)S(1)}, f32[256,128]{1,0:T(8,128)S(1)}, u32[]{:S(2)}, u32[]{:S(2)}) collective-permute-start(f32[256,128]{1,0:T(8,128)S(1)} %add_add_fusion), channel_id=1, source_target_pairs={{0,1},{1,0},{2,3},{3,2},{4,5},{5,4},{6,7},{7,6},{8,9},{9,8},{10,11... | collective-permute-start | bytes 393224 | tf_op jit(solution)/shard_map/ppermute | solution.py:54

commit v2 on v1

--- a/solution.py
+++ b/solution.py
@@ -70,11 +70,69 @@
     return value
 
 
-def orthonormal(image_block):
-    small_gram = jnp.dot(image_block.T, image_block, precision=highest)
-    factor = jnp.linalg.cholesky(small_gram)
-    return lax.linalg.triangular_solve(
-        factor, image_block, left_side=False, lower=True, transpose_a=True
+def inverse_factor(gram):
+    size, tile = gram.shape[0], 8
+    lane = lax.broadcasted_iota(jnp.int32, (tile, size), 1)
+    level = lax.broadcasted_iota(jnp.int32, (tile, size), 0)
+    def column(rows, index):
+        return jnp.broadcast_to(rows[:, index : index + 1], (tile, size))
+    def spread(rows, index):
+        return jnp.broadcast_to(rows[index : index + 1, :], (tile, size))
+    rows = [gram[first : first + tile, :] for first in range(0, size, tile)]
+    result = []
+    for block in range(size // tile):
+        base = block * tile
+        inside = (lane >= base) & (lane < base + tile)
+        columns = [column(rows[block], base + c) for c in range(tile)]
+        panel = jnp.where(inside, jnp.where(lane - base == level, 1.0, 0.0), rows[block])
+        pivots = jnp.ones((tile, size), f32)
+        inverses, known = [], {}
+        for t in range(tile):
+            pivot = spread(columns[t], t)
+            pivots = jnp.where(level == t, pivot, pivots)
+            inverses.append(1.0 / pivot)
+            ratio = jnp.where(level > t, columns[t], 0.0) * inverses[t]
+            panel = panel - ratio * spread(panel, t)
+            for c in range(t + 1, tile):
+                known[t, c] = spread(columns[c], t)
+                columns[c] = columns[c] - ratio * known[t, c]
+        result.append(jnp.where(lane <= base + level, panel, 0.0) * lax.rsqrt(pivots))
+        spreads = [spread(panel, t) for t in range(tile)]
+        for below in range(block + 1, size // tile):
+            columns = [column(rows[below], base + c) for c in range(tile)]
+            row = jnp.where(inside, 0.0, rows[below])
+            for t in range(tile):
+                ratio = columns[t] * inverses[t]
+                row = row - ratio * spreads[t]
+                for c in range(t + 1, tile):
+                    columns[c] = columns[c] - ratio * known[t, c]
+            rows[below] = row
+    return jnp.concatenate(result, axis=0)
+
+
+def outputs_kernel(rows, image_ref, image_other_ref, own_ref, other_ref, basis_ref, core_ref):
+    mode_index = lax.axis_index("mode")
+    chip, even = mode_index // 2, mode_index % 2 == 0
+    image, image_other = image_ref[...], image_other_ref[...]
+    image_block = jnp.concatenate(
+        [jnp.where(even, image, image_other), jnp.where(even, image_other, image)], axis=0
+    )
+    small_gram = lax.dot_general(
+        image_block, image_block, contract_rows, precision=highest, preferred_element_type=f32
+    )
+    inverse = inverse_factor(small_gram)
+    basis_full = lax.dot_general(
+        image_block, inverse, contract_last, precision=highest, preferred_element_type=f32
+    )
+    held = image.shape[0]
+    basis_own = jnp.where(even, basis_full[:held], basis_full[held:])
+    basis_other = jnp.where(even, basis_full[held:], basis_full[:held])
+    for place in range(held // rows):
+        @pl.when(chip == place)
+        def _():
+            basis_ref[...] = basis_own[place * rows : (place + 1) * rows]
+    core_ref[...] = dot(own_ref[...], basis_own.astype(bf16), contract_rows) + dot(
+        other_ref[...], basis_other.astype(bf16), contract_rows
     )
 
 
@@ -124,20 +182,15 @@
     image = add_over(image, "mode", chip_masks)
 
     image_other = swap(image, "mode", 1)
-    even = core == 0
-    image_block = jnp.concatenate(
-        [jnp.where(even, image, image_other), jnp.where(even, image_other, image)], axis=0
-    )
-    basis_full = orthonormal(image_block)
-    basis_low = basis_full.astype(bf16)
-    basis_rows = lax.dynamic_slice_in_dim(
-        basis_full, core * held_rows + chip * row_count, row_count, 0
-    )
-    regrouped = jnp.concatenate(
-        [jnp.where(even, own_half, other_half), jnp.where(even, other_half, own_half)], axis=0
-    )
-    core_coeffs = dot(regrouped, basis_low, contract_rows)
-    return (basis_rows, core_coeffs)
+    return pl.pallas_call(
+        functools.partial(outputs_kernel, row_count),
+        out_shape=(
+            jax.ShapeDtypeStruct((row_count, rank), f32),
+            jax.ShapeDtypeStruct((own_columns, rank), f32),
+        ),
+        in_specs=in_vmem(4),
+        out_specs=tuple(in_vmem(2)),
+    )(image, image_other, own_half, other_half)
 
 
 def solution(mesh):

time: 78.8 us -> 62 us (0.79)
  other arithmetic: 24 us -> 0.97 us
  Pallas kernels: 4.84 us -> 12.4 us
  matrix products: 2.01 us -> 0 us
    another operation x5 -> x0, other arithmetic: 22.9 us -> none  [the longest x3 12.4 us: orthonormal(): factor = jnp.linalg.cholesky(small_gram)]
    pallas_call x0 -> x1, Pallas kernels: none -> 7.54 us  [shards(): pl.pallas_call(functools.partial(outputs_kernel, row_count), out_shape=(j...]
    dot_general x2 -> x0, matrix products: 1.64 us -> none  [the longest x1 1.05 us: dot(): return lax.dot_general(lhs, rhs, dims, preferred_element_type=f32)]
    unnamed x10 -> x16, local copies, waits for them, and re-layouts: 1.52 us -> 2.15 us
  transfers between devices with their start and end apart: 12 -> 12, of which waited for: 9 -> 9; matrix products, arithmetic and copies ran while one was open for 0% -> 1% of each run, Pallas kernels for 0% -> 0%
where the time goes in v2:
time: 62 us; the launch traced here: 61.8 us
  waiting for transfers between devices  27.5 us (44%)
  starting transfers between devices  15.5 us (25%)
  Pallas kernels  12.4 us (20%)
  local copies, waits for them, and re-layouts  4.69 us (8%)
  other arithmetic  0.97 us (2%)
  between operations  0.75 us (1%)
    ppermute x9, waiting for transfers between devices, swap(): return lax.ppermute(value, axis, [(i, i ^ mask) for i in range(count)])  20.2 us
    ppermute x9, starting transfers between devices, swap(): return lax.ppermute(value, axis, [(i, i ^ mask) for i in range(count)])  8.54 us
    pallas_call x1, Pallas kernels, shards(): pl.pallas_call(functools.partial(outputs_kernel, row_count), out_shape=(j...  7.54 us
    ppermute x3, waiting for transfers between devices, shards(): blocks[step] = lax.ppermute(chip_block(step), 'mode', pairs)  7.29 us
    ppermute x3, starting transfers between devices, shards(): blocks[step] = lax.ppermute(chip_block(step), 'mode', pairs)  6.96 us
    pallas_call x1, Pallas kernels, shards(): pl.pallas_call(image_kernel, out_shape=jax.ShapeDtypeStruct((held_rows, r...  2.45 us
    pallas_call x1, Pallas kernels, shards(): pl.pallas_call(functools.partial(inner_kernel, chips), out_shape=(jax.Sha...  2.41 us
    unnamed x16, local copies, waits for them, and re-layouts  2.15 us
  transfers between devices with their start and end apart: 12, of which 9 were waited for; matrix products, arithmetic and copies ran while one was open for 1% of the time, Pallas kernels for 0%

profile of v2, /device:TPU:0, one launch (start us, length us, event | category | flops | bytes accessed | tf_op | source)
XLA Modules:
  0.0 61.8 jit_solution(15044064996331416060)
XLA Ops:
  0.7 1.8 %constant_dynamic-slice_fusion.2 = (bf16[64,1024]{1,0:T(8,128)(2,1)S(1)}, bf16[64,1024]{1,0:T(8,128)(2,1)S(1)}, bf16[64,1024]{1,0:T(8,128)(2,1)}, bf16[64,1024]{1,0:T(8,128)(2,1)S(1)}) fusion(bf16[64,4096]{1,0:T(8,128)(2,1)} %param.2, s32[]{:T(128)S(6)} %select_n.33, s32[]{:T(128)S(6)} %select_n.31, s32[]{:T(128)S(6)} %select_n.30, s32[]{:T(128)S(6)} %select_n.32), kind=kLoop, calls=%fused_computation.4 | loop fusion | bytes 1048592 | tf_op jit(solution)/shard_map/dynamic_slice | solution.py:151
  2.5 3.0 %collective-permute-start = (bf16[64,1024]{1,0:T(8,128)(2,1)S(1)}, bf16[64,1024]{1,0:T(8,128)(2,1)S(1)}, u32[]{:S(2)}, u32[]{:S(2)}) collective-permute-start(bf16[64,1024]{1,0:T(8,128)(2,1)S(1)} %get-tuple-element.9), channel_id=1, source_target_pairs={{0,2},{1,3},{2,4},{3,5},{4,6},{5,7},{6,0},{7,1},{8,10},{9,11},{10,... | collective-permute-start | bytes 393224 | tf_op jit(solution)/shard_map/ppermute | solution.py:156
  5.5 2.6 %collective-permute-start.1 = (bf16[64,1024]{1,0:T(8,128)(2,1)S(1)}, bf16[64,1024]{1,0:T(8,128)(2,1)S(1)}, u32[]{:S(2)}, u32[]{:S(2)}) collective-permute-start(bf16[64,1024]{1,0:T(8,128)(2,1)S(1)} %get-tuple-element.11), channel_id=1, source_target_pairs={{0,4},{1,5},{2,6},{3,7},{4,0},{5,1},{6,2},{7,3},{8,12},{9,13},{10,... | collective-permute-start | bytes 393224 | tf_op jit(solution)/shard_map/ppermute | solution.py:156
  8.1 1.3 %collective-permute-start.2 = (bf16[64,1024]{1,0:T(8,128)(2,1)S(1)}, bf16[64,1024]{1,0:T(8,128)(2,1)S(1)}, u32[]{:S(2)}, u32[]{:S(2)}) collective-permute-start(bf16[64,1024]{1,0:T(8,128)(2,1)S(1)} %get-tuple-element.8), channel_id=1, source_target_pairs={{0,6},{1,7},{2,0},{3,1},{4,2},{5,3},{6,4},{7,5},{8,14},{9,15},{10,... | collective-permute-start | bytes 393224 | tf_op jit(solution)/shard_map/ppermute | solution.py:156
  9.5 2.5 %collective-permute-done.refs_1_ = bf16[64,1024]{1,0:T(8,128)(2,1)S(1)} collective-permute-done((bf16[64,1024]{1,0:T(8,128)(2,1)S(1)}, bf16[64,1024]{1,0:T(8,128)(2,1)S(1)}, u32[]{:S(2)}, u32[]{:S(2)}) %collective-permute-start) | collective-permute-done | bytes 131104 | tf_op jit(solution)/shard_map/ppermute | solution.py:156
  12.0 4.8 %collective-permute-done.1.refs_2_ = bf16[64,1024]{1,0:T(8,128)(2,1)S(1)} collective-permute-done((bf16[64,1024]{1,0:T(8,128)(2,1)S(1)}, bf16[64,1024]{1,0:T(8,128)(2,1)S(1)}, u32[]{:S(2)}, u32[]{:S(2)}) %collective-permute-start.1) | collective-permute-done | bytes 131104 | tf_op jit(solution)/shard_map/ppermute | solution.py:156
  17.5 2.4 %shard_map.41 = (f32[128,1024]{1,0:T(8,128)}, bf16[256,1024]{1,0:T(8,128)(2,1)}) custom-call(f32[512,128]{1,0:T(8,128)} %start_ref.1, bf16[64,1024]{1,0:T(8,128)(2,1)} %get-tuple-element.10.refs_0_, bf16[64,1024]{1,0:T(8,128)(2,1)} %copy-done.4, bf16[64,1024]{1,0:T(8,128)(2,1)} %copy-done.5, bf16[64,1024]{1,0:T(8,128)(2,1)} %copy-done.6), custom_call_target="tpu_custom_call" | custom-call | tf_op jit(solution)/shard_map/pallas_call | solution.py:159
  19.9 2.1 %collective-permute-done.3.other_ref = f32[128,1024]{1,0:T(8,128)S(1)} collective-permute-done((f32[128,1024]{1,0:T(8,128)}, f32[128,1024]{1,0:T(8,128)S(1)}, u32[]{:S(2)}, u32[]{:S(2)}) %collective-permute-start.3) | collective-permute-done | bytes 524320 | tf_op jit(solution)/shard_map/ppermute | solution.py:54
  22.0 0.8 %copy-done.1 = f32[128,1024]{1,0:T(8,128)} copy-done((f32[128,1024]{1,0:T(8,128)}, f32[128,1024]{1,0:T(8,128)S(1)}, u32[]{:S(2)}) %copy-start.1) | copy-done | bytes 524312
  22.8 2.5 %shard_map.42 = f32[256,128]{1,0:T(8,128)} custom-call(bf16[256,1024]{1,0:T(8,128)(2,1)} %get-tuple-element.4.held_ref, f32[128,1024]{1,0:T(8,128)} %get-tuple-element.5.own_ref, f32[128,1024]{1,0:T(8,128)} %copy-done.1), custom_call_target="tpu_custom_call" | custom-call | tf_op jit(solution)/shard_map/pallas_call | solution.py:173
  25.2 1.5 %collective-permute-start.4 = (f32[256,128]{1,0:T(8,128)}, f32[256,128]{1,0:T(8,128)S(1)}, u32[]{:S(2)}, u32[]{:S(2)}) collective-permute-start(f32[256,128]{1,0:T(8,128)} %shard_map.42), channel_id=1, source_target_pairs={{0,8},{8,0},{16,24},{24,16},{1,9},{9,1},{17,25},{25,17},{2,10},{10... | collective-permute-start | bytes 393224 | tf_op jit(solution)/shard_map/ppermute | solution.py:54
  26.7 1.5 %collective-permute-start.5 = (f32[256,128]{1,0:T(8,128)}, f32[256,128]{1,0:T(8,128)S(1)}, u32[]{:S(2)}, u32[]{:S(2)}) collective-permute-start(f32[256,128]{1,0:T(8,128)} %shard_map.42), channel_id=1, source_target_pairs={{0,16},{8,24},{16,0},{24,8},{1,17},{9,25},{17,1},{25,9},{2,18},{10... | collective-permute-start | bytes 393224 | tf_op jit(solution)/shard_map/ppermute | solution.py:54
  28.7 2.6 %collective-permute-done.4 = f32[256,128]{1,0:T(8,128)S(1)} collective-permute-done((f32[256,128]{1,0:T(8,128)}, f32[256,128]{1,0:T(8,128)S(1)}, u32[]{:S(2)}, u32[]{:S(2)}) %collective-permute-start.4) | collective-permute-done | bytes 131104 | tf_op jit(solution)/shard_map/ppermute | solution.py:54
  31.4 3.7 %collective-permute-done.5 = f32[256,128]{1,0:T(8,128)S(1)} collective-permute-done((f32[256,128]{1,0:T(8,128)}, f32[256,128]{1,0:T(8,128)S(1)}, u32[]{:S(2)}, u32[]{:S(2)}) %collective-permute-start.5) | collective-permute-done | bytes 131104 | tf_op jit(solution)/shard_map/ppermute | solution.py:54
  35.0 0.9 %add_add_fusion.1 = f32[256,128]{1,0:T(8,128)S(1)} fusion(f32[256,128]{1,0:T(8,128)S(1)} %collective-permute-done.5, f32[256,128]{1,0:T(8,128)S(1)} %collective-permute-done.6, f32[256,128]{1,0:T(8,128)} %shard_map.42, f32[256,128]{1,0:T(8,128)S(1)} %collective-permute-done.4), kind=kLoop, calls=%fused_computation.1 | loop fusion | flops 98304 | bytes 655360 | tf_op jit(solution)/shard_map/add | solution.py:61
  36.0 3.3 %collective-permute-start.7 = (f32[256,128]{1,0:T(8,128)S(1)}, f32[256,128]{1,0:T(8,128)S(1)}, u32[]{:S(2)}, u32[]{:S(2)}) collective-permute-start(f32[256,128]{1,0:T(8,128)S(1)} %add_add_fusion.1), channel_id=1, source_target_pairs={{0,2},{1,3},{2,0},{3,1},{4,6},{5,7},{6,4},{7,5},{8,10},{9,11},{10,... | collective-permute-start | bytes 393224 | tf_op jit(solution)/shard_map/ppermute | solution.py:54
  39.2 1.2 %collective-permute-start.8 = (f32[256,128]{1,0:T(8,128)S(1)}, f32[256,128]{1,0:T(8,128)S(1)}, u32[]{:S(2)}, u32[]{:S(2)}) collective-permute-start(f32[256,128]{1,0:T(8,128)S(1)} %add_add_fusion.1), channel_id=1, source_target_pairs={{0,6},{1,7},{2,4},{3,5},{4,2},{5,3},{6,0},{7,1},{8,14},{9,15},{10,... | collective-permute-start | bytes 393224 | tf_op jit(solution)/shard_map/ppermute | solution.py:54
  40.9 0.7 %constant_dynamic-slice_fusion = (bf16[256,512]{1,0:T(8,128)(2,1)S(1)}, bf16[256,512]{1,0:T(8,128)(2,1)}) fusion(bf16[256,1024]{1,0:T(8,128)(2,1)S(1)} %copy-done, s32[]{:T(128)S(6)} %select_n.36, s32[]{:T(128)S(6)} %select_n.35), kind=kLoop, calls=%fused_computation.2 | loop fusion | bytes 1048584 | tf_op jit(solution)/shard_map/dynamic_slice | solution.py:170
  41.7 1.5 %collective-permute-done.7 = f32[256,128]{1,0:T(8,128)S(1)} collective-permute-done((f32[256,128]{1,0:T(8,128)S(1)}, f32[256,128]{1,0:T(8,128)S(1)}, u32[]{:S(2)}, u32[]{:S(2)}) %collective-permute-start.7) | collective-permute-done | bytes 131104 | tf_op jit(solution)/shard_map/ppermute | solution.py:54
  43.2 4.4 %collective-permute-done.8 = f32[256,128]{1,0:T(8,128)S(1)} collective-permute-done((f32[256,128]{1,0:T(8,128)S(1)}, f32[256,128]{1,0:T(8,128)S(1)}, u32[]{:S(2)}, u32[]{:S(2)}) %collective-permute-start.8) | collective-permute-done | bytes 131104 | tf_op jit(solution)/shard_map/ppermute | solution.py:54
  47.6 4.6 %collective-permute-done.9 = f32[256,128]{1,0:T(8,128)S(1)} collective-permute-done((f32[256,128]{1,0:T(8,128)S(1)}, f32[256,128]{1,0:T(8,128)S(1)}, u32[]{:S(2)}, u32[]{:S(2)}) %collective-permute-start.9) | collective-permute-done | bytes 131104 | tf_op jit(solution)/shard_map/ppermute | solution.py:54
  52.3 1.3 %collective-permute-done.10.image_other_ref = f32[256,128]{1,0:T(8,128)S(1)} collective-permute-done((f32[256,128]{1,0:T(8,128)S(1)}, f32[256,128]{1,0:T(8,128)S(1)}, u32[]{:S(2)}, u32[]{:S(2)}) %collective-permute-start.10) | collective-permute-done | bytes 131104 | tf_op jit(solution)/shard_map/ppermute | solution.py:54
  53.6 0.6 %copy-done.7 = f32[256,128]{1,0:T(8,128)} copy-done((f32[256,128]{1,0:T(8,128)}, f32[256,128]{1,0:T(8,128)S(1)}, u32[]{:S(2)}) %copy-start.7) | copy-done | bytes 131096
  54.3 7.5 %shard_map.43 = (f32[64,128]{1,0:T(8,128)}, f32[512,128]{1,0:T(8,128)}) custom-call(f32[256,128]{1,0:T(8,128)} %copy-done.2, f32[256,128]{1,0:T(8,128)} %copy-done.7, bf16[256,512]{1,0:T(8,128)(2,1)} %get-tuple-element.7.own_ref, bf16[256,512]{1,0:T(8,128)(2,1)} %copy-done.3), custom_call_target="tpu_custom_call" | custom-call | tf_op jit(solution)/shard_map/pallas_call | solution.py:185
  (23 shorter events, 1.8 us)
Async XLA Ops:
  2.5 9.5 %collective-permute-start = (bf16[64,1024]{1,0:T(8,128)(2,1)S(1)}, bf16[64,1024]{1,0:T(8,128)(2,1)S(1)}, u32[]{:S(2)}, u32[]{:S(2)}) collective-permute-start(bf16[64,1024]{1,0:T(8,128)(2,1)S(1)} %get-tuple-element.9), channel_id=1, source_target_pairs={{0,2},{1,3},{2,4},{3,5},{4,6},{5,7},{6,0},{7,1},{8,10},{9,11},{10,... | collective-permute-start | bytes 393224 | tf_op jit(solution)/shard_map/ppermute | solution.py:156
  5.5 11.2 %collective-permute-start.1 = (bf16[64,1024]{1,0:T(8,128)(2,1)S(1)}, bf16[64,1024]{1,0:T(8,128)(2,1)S(1)}, u32[]{:S(2)}, u32[]{:S(2)}) collective-permute-start(bf16[64,1024]{1,0:T(8,128)(2,1)S(1)} %get-tuple-element.11), channel_id=1, source_target_pairs={{0,4},{1,5},{2,6},{3,7},{4,0},{5,1},{6,2},{7,3},{8,12},{9,13},{10,... | collective-permute-start | bytes 393224 | tf_op jit(solution)/shard_map/ppermute | solution.py:156
  8.1 8.6 %collective-permute-start.2 = (bf16[64,1024]{1,0:T(8,128)(2,1)S(1)}, bf16[64,1024]{1,0:T(8,128)(2,1)S(1)}, u32[]{:S(2)}, u32[]{:S(2)}) collective-permute-start(bf16[64,1024]{1,0:T(8,128)(2,1)S(1)} %get-tuple-element.8), channel_id=1, source_target_pairs={{0,6},{1,7},{2,0},{3,1},{4,2},{5,3},{6,4},{7,5},{8,14},{9,15},{10,... | collective-permute-start | bytes 393224 | tf_op jit(solution)/shard_map/ppermute | solution.py:156
  12.0 4.8 %copy-start.4 = (bf16[64,1024]{1,0:T(8,128)(2,1)}, bf16[64,1024]{1,0:T(8,128)(2,1)S(1)}, u32[]{:S(2)}) copy-start(bf16[64,1024]{1,0:T(8,128)(2,1)S(1)} %collective-permute-done.refs_1_) | copy-start | bytes 393220
  16.8 0.7 %copy-start.5 = (bf16[64,1024]{1,0:T(8,128)(2,1)}, bf16[64,1024]{1,0:T(8,128)(2,1)S(1)}, u32[]{:S(2)}) copy-start(bf16[64,1024]{1,0:T(8,128)(2,1)S(1)} %collective-permute-done.1.refs_2_) | copy-start | bytes 393220
  16.8 0.7 %copy-start.6 = (bf16[64,1024]{1,0:T(8,128)(2,1)}, bf16[64,1024]{1,0:T(8,128)(2,1)S(1)}, u32[]{:S(2)}) copy-start(bf16[64,1024]{1,0:T(8,128)(2,1)S(1)} %collective-permute-done.2.refs_3_) | copy-start | bytes 393220
  19.9 2.1 %collective-permute-start.3 = (f32[128,1024]{1,0:T(8,128)}, f32[128,1024]{1,0:T(8,128)S(1)}, u32[]{:S(2)}, u32[]{:S(2)}) collective-permute-start(f32[128,1024]{1,0:T(8,128)} %get-tuple-element.5.own_ref), channel_id=1, source_target_pairs={{0,1},{1,0},{2,3},{3,2},{4,5},{5,4},{6,7},{7,6},{8,9},{9,8},{10,11... | collective-permute-start | bytes 1572872 | tf_op jit(solution)/shard_map/ppermute | solution.py:54
  22.0 0.8 %copy-start.1 = (f32[128,1024]{1,0:T(8,128)}, f32[128,1024]{1,0:T(8,128)S(1)}, u32[]{:S(2)}) copy-start(f32[128,1024]{1,0:T(8,128)S(1)} %collective-permute-done.3.other_ref) | copy-start | bytes 1572868
  25.2 15.7 %copy-start = (bf16[256,1024]{1,0:T(8,128)(2,1)S(1)}, bf16[256,1024]{1,0:T(8,128)(2,1)}, u32[]{:S(2)}) copy-start(bf16[256,1024]{1,0:T(8,128)(2,1)} %get-tuple-element.4.held_ref) | copy-start | bytes 1572868
  25.2 6.1 %collective-permute-start.4 = (f32[256,128]{1,0:T(8,128)}, f32[256,128]{1,0:T(8,128)S(1)}, u32[]{:S(2)}, u32[]{:S(2)}) collective-permute-start(f32[256,128]{1,0:T(8,128)} %shard_map.42), channel_id=1, source_target_pairs={{0,8},{8,0},{16,24},{24,16},{1,9},{9,1},{17,25},{25,17},{2,10},{10... | collective-permute-start | bytes 393224 | tf_op jit(solution)/shard_map/ppermute | solution.py:54
  26.7 8.3 %collective-permute-start.5 = (f32[256,128]{1,0:T(8,128)}, f32[256,128]{1,0:T(8,128)S(1)}, u32[]{:S(2)}, u32[]{:S(2)}) collective-permute-start(f32[256,128]{1,0:T(8,128)} %shard_map.42), channel_id=1, source_target_pairs={{0,16},{8,24},{16,0},{24,8},{1,17},{9,25},{17,1},{25,9},{2,18},{10... | collective-permute-start | bytes 393224 | tf_op jit(solution)/shard_map/ppermute | solution.py:54
  28.3 6.8 %collective-permute-start.6 = (f32[256,128]{1,0:T(8,128)}, f32[256,128]{1,0:T(8,128)S(1)}, u32[]{:S(2)}, u32[]{:S(2)}) collective-permute-start(f32[256,128]{1,0:T(8,128)} %shard_map.42), channel_id=1, source_target_pairs={{0,24},{8,16},{16,8},{24,0},{1,25},{9,17},{17,9},{25,1},{2,26},{10... | collective-permute-start | bytes 393224 | tf_op jit(solution)/shard_map/ppermute | solution.py:54
  36.0 7.2 %collective-permute-start.7 = (f32[256,128]{1,0:T(8,128)S(1)}, f32[256,128]{1,0:T(8,128)S(1)}, u32[]{:S(2)}, u32[]{:S(2)}) collective-permute-start(f32[256,128]{1,0:T(8,128)S(1)} %add_add_fusion.1), channel_id=1, source_target_pairs={{0,2},{1,3},{2,0},{3,1},{4,6},{5,7},{6,4},{7,5},{8,10},{9,11},{10,... | collective-permute-start | bytes 393224 | tf_op jit(solution)/shard_map/ppermute | solution.py:54
  39.2 8.3 %collective-permute-start.8 = (f32[256,128]{1,0:T(8,128)S(1)}, f32[256,128]{1,0:T(8,128)S(1)}, u32[]{:S(2)}, u32[]{:S(2)}) collective-permute-start(f32[256,128]{1,0:T(8,128)S(1)} %add_add_fusion.1), channel_id=1, source_target_pairs={{0,6},{1,7},{2,4},{3,5},{4,2},{5,3},{6,0},{7,1},{8,14},{9,15},{10,... | collective-permute-start | bytes 393224 | tf_op jit(solution)/shard_map/ppermute | solution.py:54
  40.4 11.7 %collective-permute-start.9 = (f32[256,128]{1,0:T(8,128)S(1)}, f32[256,128]{1,0:T(8,128)S(1)}, u32[]{:S(2)}, u32[]{:S(2)}) collective-permute-start(f32[256,128]{1,0:T(8,128)S(1)} %add_add_fusion.1), channel_id=1, source_target_pairs={{0,4},{1,5},{2,6},{3,7},{4,0},{5,1},{6,2},{7,3},{8,12},{9,13},{10,... | collective-permute-start | bytes 393224 | tf_op jit(solution)/shard_map/ppermute | solution.py:54
  41.7 10.6 %collective-permute-start.11 = (bf16[256,512]{1,0:T(8,128)(2,1)S(1)}, bf16[256,512]{1,0:T(8,128)(2,1)S(1)}, u32[]{:S(2)}, u32[]{:S(2)}) collective-permute-start(bf16[256,512]{1,0:T(8,128)(2,1)S(1)} %get-tuple-element.6), channel_id=1, source_target_pairs={{0,1},{1,0},{2,3},{3,2},{4,5},{5,4},{6,7},{7,6},{8,9},{9,8},{10,11... | collective-permute-start | bytes 786440 | tf_op jit(solution)/shard_map/ppermute | solution.py:54
  52.2 1.4 %copy-start.2 = (f32[256,128]{1,0:T(8,128)}, f32[256,128]{1,0:T(8,128)S(1)}, u32[]{:S(2)}) copy-start(f32[256,128]{1,0:T(8,128)S(1)} %add_add_fusion.image_ref) | copy-start | bytes 393220
  52.2 1.4 %collective-permute-start.10 = (f32[256,128]{1,0:T(8,128)S(1)}, f32[256,128]{1,0:T(8,128)S(1)}, u32[]{:S(2)}, u32[]{:S(2)}) collective-permute-start(f32[256,128]{1,0:T(8,128)S(1)} %add_add_fusion.image_ref), channel_id=1, source_target_pairs={{0,1},{1,0},{2,3},{3,2},{4,5},{5,4},{6,7},{7,6},{8,9},{9,8},{10,11... | collective-permute-start | bytes 393224 | tf_op jit(solution)/shard_map/ppermute | solution.py:54
  52.3 1.3 %copy-start.3 = (bf16[256,512]{1,0:T(8,128)(2,1)}, bf16[256,512]{1,0:T(8,128)(2,1)S(1)}, u32[]{:S(2)}) copy-start(bf16[256,512]{1,0:T(8,128)(2,1)S(1)} %collective-permute-done.11.other_ref) | copy-start | bytes 786436
  53.6 0.6 %copy-start.7 = (f32[256,128]{1,0:T(8,128)}, f32[256,128]{1,0:T(8,128)S(1)}, u32[]{:S(2)}) copy-start(f32[256,128]{1,0:T(8,128)S(1)} %collective-permute-done.10.image_other_ref) | copy-start | bytes 393220

commit v3 on v2

--- a/solution.py
+++ b/solution.py
@@ -23,19 +23,45 @@
     return lax.dot_general(lhs, rhs, dims, preferred_element_type=f32)
 
 
-def in_vmem(count):
+def in_vmem(*arrays):
+    return [pltpu.with_memory_space_constraint(array, pltpu.VMEM) for array in arrays]
+
+
+def vmem_specs(count):
     return [pl.BlockSpec(memory_space=pltpu.VMEM)] * count
 
 
+def split_kernel(tensor_ref, *refs):
+    blocks, semaphores = refs[:-1], refs[-1]
+    chips = len(blocks)
+    width = blocks[0].shape[1]
+    chip = lax.axis_index("mode") // 2
+    copies = []
+    for step, block in enumerate(blocks):
+        target = lax.rem(chip + step, chips)
+        columns = pl.ds(pl.multiple_of(target * width, width), width)
+        copies.append(
+            pltpu.make_async_copy(tensor_ref.at[:, columns], block, semaphores.at[step])
+        )
+    for copy in copies:
+        copy.start()
+    for copy in copies:
+        copy.wait()
+
+
 def inner_kernel(chips, start_ref, *refs):
-    blocks, (inner_ref, held_ref) = refs[:chips], refs[chips:]
+    blocks, (inner_ref, held_ref, own_ref, away_ref) = refs[:chips], refs[chips:]
     mode_index = lax.axis_index("mode")
     chip, core = mode_index // 2, mode_index % 2
-    rows = blocks[0].shape[0]
+    rows, width = blocks[0].shape
+    half = width // 2
     starts = []
     for step in range(chips):
         source = lax.rem(chip + chips - step, chips)
-        held_ref[pl.ds(pl.multiple_of(source * rows, rows), rows), :] = blocks[step][...]
+        place = pl.ds(pl.multiple_of(source * rows, rows), rows)
+        held_ref[place, :] = blocks[step][...]
+        own_ref[place, :] = blocks[step][:, pl.ds(pl.multiple_of(core * half, half), half)]
+        away_ref[place, :] = blocks[step][:, pl.ds(pl.multiple_of((1 - core) * half, half), half)]
         first = pl.multiple_of((source * 2 + core) * rows, rows)
         starts.append(start_ref[pl.ds(first, rows), :])
     ordered = jnp.concatenate([block[...] for block in blocks], axis=0)
@@ -49,24 +75,39 @@
     image_ref[...] = dot(held, high, contract_last) + dot(held, low, contract_last)
 
 
-def swap(value, axis, mask):
-    count = lax.axis_size(axis)
-    return lax.ppermute(value, axis, [(i, i ^ mask) for i in range(count)])
-
-
-def add_four(value, axis, first, second):
-    near = swap(value, axis, first)
-    side = swap(value, axis, second)
-    far = swap(value, axis, first ^ second)
-    return (value + near) + (side + far)
-
-
-def add_over(value, axis, masks):
-    masks = list(masks)
-    while len(masks) >= 2:
-        value = add_four(value, axis, masks.pop(0), masks.pop(0))
-    if masks:
-        value = value + swap(value, axis, masks.pop())
+def swap_cores(value):
+    return lax.ppermute(value, "mode", [(i, i ^ 1) for i in range(lax.axis_size("mode"))])
+
+
+def exchange(value, even_masks, odd_masks):
+    slabs, modes = lax.axis_size("slab"), lax.axis_size("mode")
+    pairs = []
+    for slab in range(slabs):
+        for mode in range(modes):
+            slab_mask, chip_mask = odd_masks if mode % 2 else even_masks
+            pairs.append((slab * modes + mode, (slab ^ slab_mask) * modes + (mode ^ 2 * chip_mask)))
+    return lax.ppermute(value, ("slab", "mode"), pairs)
+
+
+def both(first, second):
+    return (first[0] ^ second[0], first[1] ^ second[1])
+
+
+def sum_over_chips(value):
+    slab_bits = lax.axis_size("slab").bit_length() - 1
+    chip_bits = (lax.axis_size("mode") // 2).bit_length() - 1
+    along_slab = [(1 << bit, 0) for bit in range(slab_bits)]
+    along_mode = [(0, (2 << bit) - 1) for bit in range(chip_bits)]
+    even, odd = along_slab + along_mode, along_mode + along_slab
+    while len(even) >= 2:
+        (a, b), (c, d) = even[:2], odd[:2]
+        even, odd = even[2:], odd[2:]
+        far = exchange(value, both(a, b), both(c, d))
+        near = exchange(value, a, c)
+        side = exchange(value, b, d)
+        value = (value + near) + (side + far)
+    if even:
+        value = value + exchange(value, even[0], odd[0])
     return value
 
 
@@ -138,59 +179,56 @@
 
 def shards(tensor, start_block):
     row_count, slab_columns = tensor.shape
-    slabs, modes = lax.axis_size("slab"), lax.axis_size("mode")
+    modes = lax.axis_size("mode")
     chips = modes // 2
     chip_columns = slab_columns // chips
     own_columns = chip_columns // 2
+    held_rows = chips * row_count
     rank = start_block.shape[1]
-    mode_index = lax.axis_index("mode")
-    chip, core = mode_index // 2, mode_index % 2
-
-    def chip_block(step):
-        target = lax.rem(chip + step, chips)
-        return lax.dynamic_slice_in_dim(tensor, target * chip_columns, chip_columns, 1)
-
-    blocks = [chip_block(0)] + [None] * (chips - 1)
+
+    blocks = list(pl.pallas_call(
+        split_kernel,
+        out_shape=[pltpu.VMEM((row_count, chip_columns), bf16)] * chips,
+        in_specs=[pl.BlockSpec(memory_space=pl.ANY)],
+        out_specs=vmem_specs(chips),
+        scratch_shapes=[pltpu.SemaphoreType.DMA((chips,))],
+    )(tensor))
     for step in sorted(range(1, chips), key=lambda step: -min(step, chips - step)):
         pairs = [(i, (i + 2 * step) % modes) for i in range(modes)]
-        blocks[step] = lax.ppermute(chip_block(step), "mode", pairs)
-
-    held_rows = chips * row_count
-    inner, held = pl.pallas_call(
+        blocks[step] = lax.ppermute(blocks[step], "mode", pairs)
+
+    inner, held, own_half, away_half = pl.pallas_call(
         functools.partial(inner_kernel, chips),
         out_shape=(
-            jax.ShapeDtypeStruct((rank, chip_columns), f32),
-            jax.ShapeDtypeStruct((held_rows, chip_columns), bf16),
+            pltpu.VMEM((rank, chip_columns), f32),
+            pltpu.VMEM((held_rows, chip_columns), bf16),
+            pltpu.VMEM((held_rows, own_columns), bf16),
+            pltpu.VMEM((held_rows, own_columns), bf16),
         ),
-        in_specs=in_vmem(1 + chips),
-        out_specs=tuple(in_vmem(2)),
-    )(start_block, *blocks)
-    inner_other = swap(inner, "mode", 1)
-    own_half = lax.dynamic_slice_in_dim(held, core * own_columns, own_columns, 1)
-    away_half = lax.dynamic_slice_in_dim(held, (1 - core) * own_columns, own_columns, 1)
-    other_half = swap(away_half, "mode", 1)
+        in_specs=vmem_specs(1 + chips),
+        out_specs=tuple(vmem_specs(4)),
+    )(*in_vmem(start_block, *blocks))
+    inner_other = swap_cores(inner)
+    other_half = swap_cores(away_half)
 
     image = pl.pallas_call(
         image_kernel,
-        out_shape=jax.ShapeDtypeStruct((held_rows, rank), f32),
-        in_specs=in_vmem(3),
-        out_specs=in_vmem(1)[0],
-    )(held, inner, inner_other)
-    slab_masks = [1 << bit for bit in range(slabs.bit_length() - 1)]
-    chip_masks = [2 * ((2 << bit) - 1) for bit in range(chips.bit_length() - 1)]
-    image = add_over(image, "slab", slab_masks)
-    image = add_over(image, "mode", chip_masks)
-
-    image_other = swap(image, "mode", 1)
+        out_shape=pltpu.VMEM((held_rows, rank), f32),
+        in_specs=vmem_specs(3),
+        out_specs=vmem_specs(1)[0],
+    )(*in_vmem(held, inner, inner_other))
+    image = sum_over_chips(image)
+    image_other = swap_cores(image)
+
     return pl.pallas_call(
         functools.partial(outputs_kernel, row_count),
         out_shape=(
             jax.ShapeDtypeStruct((row_count, rank), f32),
             jax.ShapeDtypeStruct((own_columns, rank), f32),
         ),
-        in_specs=in_vmem(4),
-        out_specs=tuple(in_vmem(2)),
-    )(image, image_other, own_half, other_half)
+        in_specs=vmem_specs(4),
+        out_specs=tuple(vmem_specs(2)),
+    )(*in_vmem(image, image_other, own_half, other_half))
 
 
 def solution(mesh):

time: 62 us -> 46.5 us (0.75)
  waiting for transfers between devices: 27.5 us -> 20.8 us
  local copies, waits for them, and re-layouts: 4.69 us -> 0.01 us
  Pallas kernels: 12.4 us -> 8.42 us
  other arithmetic: 0.97 us -> 0.06 us
  starting transfers between devices: 15.5 us -> 16.4 us
    ppermute x12, waiting for transfers between devices: 27.5 us -> 20.8 us  [the longest x6 10.3 us: exchange(): return lax.ppermute(value, ('slab', 'mode'), pairs)]
    pallas_call x2 -> x3, Pallas kernels: 4.87 us -> 2.05 us  [the longest x1 1.19 us: shards(): pl.pallas_call(split_kernel, out_shape=[pltpu.VMEM((row_count, chip_colum...]
    dynamic_slice x2 -> x0, local copies, waits for them, and re-layouts: 2.54 us -> none  [the longest x1 1.8 us: chip_block(): lax.dynamic_slice_in_dim(tensor, target * chip_columns, chip_columns, 1)]
    unnamed x16 -> x2, local copies, waits for them, and re-layouts: 2.15 us -> 0.01 us
    pallas_call x1, Pallas kernels: 7.54 us -> 6.37 us  [shards(): pl.pallas_call(functools.partial(outputs_kernel, row_count), out_shape=(j...]
    ppermute x12, starting transfers between devices: 15.5 us -> 16.4 us  [the longest x6 9.26 us: exchange(): return lax.ppermute(value, ('slab', 'mode'), pairs)]
    add x2, other arithmetic: 0.97 us -> 0.06 us  [sum_over_chips(): value = value + near + (side + far)]
  transfers between devices with their start and end apart: 12 -> 12, of which waited for: 9 -> 10; matrix products, arithmetic and copies ran while one was open for 1% -> 0% of each run, Pallas kernels for 0% -> 0%
where the time goes in v3:
time: 46.5 us; the launch traced here: 46.4 us
  waiting for transfers between devices  20.8 us (45%)
  starting transfers between devices  16.4 us (35%)
  Pallas kernels  8.42 us (18%)
  between operations  0.7 us (2%)
    ppermute x6, waiting for transfers between devices, exchange(): return lax.ppermute(value, ('slab', 'mode'), pairs)  10.3 us
    ppermute x6, starting transfers between devices, exchange(): return lax.ppermute(value, ('slab', 'mode'), pairs)  9.26 us
    ppermute x3, waiting for transfers between devices, shards(): blocks[step] = lax.ppermute(blocks[step], 'mode', pairs)  7.3 us
    ppermute x3, starting transfers between devices, shards(): blocks[step] = lax.ppermute(blocks[step], 'mode', pairs)  7.01 us
    pallas_call x1, Pallas kernels, shards(): pl.pallas_call(functools.partial(outputs_kernel, row_count), out_shape=(j...  6.37 us
    ppermute x3, waiting for transfers between devices, swap_cores(): lax.ppermute(value, 'mode', [(i, i ^ 1) for i in range(lax.axis_size('mod...  3.22 us
    pallas_call x1, Pallas kernels, shards(): pl.pallas_call(split_kernel, out_shape=[pltpu.VMEM((row_count, chip_colum...  1.19 us
  transfers between devices with their start and end apart: 12, of which 10 were waited for; matrix products, arithmetic and copies ran while one was open for 0% of the time, Pallas kernels for 0%

profile of v3, /device:TPU:0, one launch (start us, length us, event | category | flops | bytes accessed | tf_op | source)
XLA Modules:
  0.0 46.4 jit_solution(1526015894127229532)
XLA Ops:
  0.6 1.2 %shard_map.41 = (bf16[64,1024]{1,0:T(8,128)(2,1)S(1)}, bf16[64,1024]{1,0:T(8,128)(2,1)S(1)}, bf16[64,1024]{1,0:T(8,128)(2,1)S(1)}, bf16[64,1024]{1,0:T(8,128)(2,1)S(1)}) custom-call(bf16[64,4096]{1,0:T(8,128)(2,1)} %tensor_ref.1), custom_call_target="tpu_custom_call" | custom-call | tf_op jit(solution)/shard_map/pallas_call | solution.py:189
  1.8 3.1 %collective-permute-start = (bf16[64,1024]{1,0:T(8,128)(2,1)S(1)}, bf16[64,1024]{1,0:T(8,128)(2,1)S(1)}, u32[]{:S(2)}, u32[]{:S(2)}) collective-permute-start(bf16[64,1024]{1,0:T(8,128)(2,1)S(1)} %get-tuple-element.11), channel_id=1, source_target_pairs={{0,2},{1,3},{2,4},{3,5},{4,6},{5,7},{6,0},{7,1},{8,10},{9,11},{10,... | collective-permute-start | bytes 393224 | tf_op jit(solution)/shard_map/ppermute | solution.py:198
  4.9 2.6 %collective-permute-start.1 = (bf16[64,1024]{1,0:T(8,128)(2,1)S(1)}, bf16[64,1024]{1,0:T(8,128)(2,1)S(1)}, u32[]{:S(2)}, u32[]{:S(2)}) collective-permute-start(bf16[64,1024]{1,0:T(8,128)(2,1)S(1)} %get-tuple-element.12), channel_id=1, source_target_pairs={{0,4},{1,5},{2,6},{3,7},{4,0},{5,1},{6,2},{7,3},{8,12},{9,13},{10,... | collective-permute-start | bytes 393224 | tf_op jit(solution)/shard_map/ppermute | solution.py:198
  7.5 1.3 %collective-permute-start.2 = (bf16[64,1024]{1,0:T(8,128)(2,1)S(1)}, bf16[64,1024]{1,0:T(8,128)(2,1)S(1)}, u32[]{:S(2)}, u32[]{:S(2)}) collective-permute-start(bf16[64,1024]{1,0:T(8,128)(2,1)S(1)} %get-tuple-element.13), channel_id=1, source_target_pairs={{0,6},{1,7},{2,0},{3,1},{4,2},{5,3},{6,4},{7,5},{8,14},{9,15},{10,... | collective-permute-start | bytes 393224 | tf_op jit(solution)/shard_map/ppermute | solution.py:198
  8.8 2.5 %collective-permute-done.refs_1_ = bf16[64,1024]{1,0:T(8,128)(2,1)S(1)} collective-permute-done((bf16[64,1024]{1,0:T(8,128)(2,1)S(1)}, bf16[64,1024]{1,0:T(8,128)(2,1)S(1)}, u32[]{:S(2)}, u32[]{:S(2)}) %collective-permute-start) | collective-permute-done | bytes 131104 | tf_op jit(solution)/shard_map/ppermute | solution.py:198
  11.4 4.8 %collective-permute-done.1.refs_2_ = bf16[64,1024]{1,0:T(8,128)(2,1)S(1)} collective-permute-done((bf16[64,1024]{1,0:T(8,128)(2,1)S(1)}, bf16[64,1024]{1,0:T(8,128)(2,1)S(1)}, u32[]{:S(2)}, u32[]{:S(2)}) %collective-permute-start.1) | collective-permute-done | bytes 131104 | tf_op jit(solution)/shard_map/ppermute | solution.py:198
  16.1 0.4 shard_map.42
  16.6 0.1 collective-permute-start.3
  16.7 1.9 %collective-permute-done.3.other_ref = f32[128,1024]{1,0:T(8,128)S(1)} collective-permute-done((f32[128,1024]{1,0:T(8,128)S(1)}, f32[128,1024]{1,0:T(8,128)S(1)}, u32[]{:S(2)}, u32[]{:S(2)}) %collective-permute-start.3) | collective-permute-done | bytes 524320 | tf_op jit(solution)/shard_map/ppermute | solution.py:79
  18.6 0.4 shard_map.43
  19.0 2.5 %collective-permute-start.6 = (f32[256,128]{1,0:T(8,128)S(1)}, f32[256,128]{1,0:T(8,128)S(1)}, u32[]{:S(2)}, u32[]{:S(2)}) collective-permute-start(f32[256,128]{1,0:T(8,128)S(1)} %shard_map.43), channel_id=1, source_target_pairs={{0,24},{1,5},{2,26},{3,7},{4,28},{5,1},{6,30},{7,3},{8,16},{9,13},... | collective-permute-start | bytes 393224 | tf_op jit(solution)/shard_map/ppermute | solution.py:89
  21.5 0.5 %collective-permute-start.5 = (f32[256,128]{1,0:T(8,128)S(1)}, f32[256,128]{1,0:T(8,128)S(1)}, u32[]{:S(2)}, u32[]{:S(2)}) collective-permute-start(f32[256,128]{1,0:T(8,128)S(1)} %shard_map.43), channel_id=1, source_target_pairs={{0,16},{1,7},{2,18},{3,5},{4,20},{5,3},{6,22},{7,1},{8,24},{9,15},... | collective-permute-start | bytes 393224 | tf_op jit(solution)/shard_map/ppermute | solution.py:89
  22.0 0.5 %collective-permute-start.4 = (f32[256,128]{1,0:T(8,128)S(1)}, f32[256,128]{1,0:T(8,128)S(1)}, u32[]{:S(2)}, u32[]{:S(2)}) collective-permute-start(f32[256,128]{1,0:T(8,128)S(1)} %shard_map.43), channel_id=1, source_target_pairs={{0,8},{1,3},{2,10},{3,1},{4,12},{5,7},{6,14},{7,5},{8,0},{9,11},{1... | collective-permute-start | bytes 393224 | tf_op jit(solution)/shard_map/ppermute | solution.py:89
  22.6 2.4 %collective-permute-done.6 = f32[256,128]{1,0:T(8,128)S(1)} collective-permute-done((f32[256,128]{1,0:T(8,128)S(1)}, f32[256,128]{1,0:T(8,128)S(1)}, u32[]{:S(2)}, u32[]{:S(2)}) %collective-permute-start.6) | collective-permute-done | bytes 131104 | tf_op jit(solution)/shard_map/ppermute | solution.py:89
  24.9 1.5 %collective-permute-done.5 = f32[256,128]{1,0:T(8,128)S(1)} collective-permute-done((f32[256,128]{1,0:T(8,128)S(1)}, f32[256,128]{1,0:T(8,128)S(1)}, u32[]{:S(2)}, u32[]{:S(2)}) %collective-permute-start.5) | collective-permute-done | bytes 131104 | tf_op jit(solution)/shard_map/ppermute | solution.py:89
  26.5 0.5 %collective-permute-done.4 = f32[256,128]{1,0:T(8,128)S(1)} collective-permute-done((f32[256,128]{1,0:T(8,128)S(1)}, f32[256,128]{1,0:T(8,128)S(1)}, u32[]{:S(2)}, u32[]{:S(2)}) %collective-permute-start.4) | collective-permute-done | bytes 131104 | tf_op jit(solution)/shard_map/ppermute | solution.py:89
  27.0 2.3 %collective-permute-start.9 = (f32[256,128]{1,0:T(8,128)S(1)}, f32[256,128]{1,0:T(8,128)S(1)}, u32[]{:S(2)}, u32[]{:S(2)}) collective-permute-start(f32[256,128]{1,0:T(8,128)S(1)} %add_add_fusion.1), channel_id=1, source_target_pairs={{0,4},{1,25},{2,6},{3,27},{4,0},{5,29},{6,2},{7,31},{8,12},{9,17},... | collective-permute-start | bytes 393224 | tf_op jit(solution)/shard_map/ppermute | solution.py:89
  29.3 3.4 %collective-permute-start.8 = (f32[256,128]{1,0:T(8,128)S(1)}, f32[256,128]{1,0:T(8,128)S(1)}, u32[]{:S(2)}, u32[]{:S(2)}) collective-permute-start(f32[256,128]{1,0:T(8,128)S(1)} %add_add_fusion.1), channel_id=1, source_target_pairs={{0,6},{1,17},{2,4},{3,19},{4,2},{5,21},{6,0},{7,23},{8,14},{9,25},... | collective-permute-start | bytes 393224 | tf_op jit(solution)/shard_map/ppermute | solution.py:89
  32.7 0.2 collective-permute-done.9
  33.0 4.3 %collective-permute-done.8 = f32[256,128]{1,0:T(8,128)S(1)} collective-permute-done((f32[256,128]{1,0:T(8,128)S(1)}, f32[256,128]{1,0:T(8,128)S(1)}, u32[]{:S(2)}, u32[]{:S(2)}) %collective-permute-start.8) | collective-permute-done | bytes 131104 | tf_op jit(solution)/shard_map/ppermute | solution.py:89
  37.3 1.3 %collective-permute-done.7 = f32[256,128]{1,0:T(8,128)S(1)} collective-permute-done((f32[256,128]{1,0:T(8,128)S(1)}, f32[256,128]{1,0:T(8,128)S(1)}, u32[]{:S(2)}, u32[]{:S(2)}) %collective-permute-start.7) | collective-permute-done | bytes 131104 | tf_op jit(solution)/shard_map/ppermute | solution.py:89
  38.6 0.1 collective-permute-start.10
  38.7 1.3 %collective-permute-done.10.image_other_ref = f32[256,128]{1,0:T(8,128)S(1)} collective-permute-done((f32[256,128]{1,0:T(8,128)S(1)}, f32[256,128]{1,0:T(8,128)S(1)}, u32[]{:S(2)}, u32[]{:S(2)}) %collective-permute-start.10) | collective-permute-done | bytes 131104 | tf_op jit(solution)/shard_map/ppermute | solution.py:79
  40.0 6.4 %shard_map.44 = (f32[64,128]{1,0:T(8,128)}, f32[512,128]{1,0:T(8,128)}) custom-call(f32[256,128]{1,0:T(8,128)S(1)} %add_add_fusion.image_ref, f32[256,128]{1,0:T(8,128)S(1)} %collective-permute-done.10.image_other_ref, bf16[256,512]{1,0:T(8,128)(2,1)S(1)} %get-tuple-element.16.own_ref, bf16[256,512]{1,0:T(8,128)(2,1)S(1)} %collective-permute-done.11.other_ref), custom_call_target="tpu_custom_call" | custom-call | tf_op jit(solution)/shard_map/pallas_call | solution.py:223
  (8 shorter events, 0.1 us)
Async XLA Ops:
  0.6 15.5 %copy-start = (f32[512,128]{1,0:T(8,128)S(1)}, f32[512,128]{1,0:T(8,128)}, u32[]{:S(2)}) copy-start(f32[512,128]{1,0:T(8,128)} %start_ref.1) | copy-start | bytes 786436
  1.8 9.5 %collective-permute-start = (bf16[64,1024]{1,0:T(8,128)(2,1)S(1)}, bf16[64,1024]{1,0:T(8,128)(2,1)S(1)}, u32[]{:S(2)}, u32[]{:S(2)}) collective-permute-start(bf16[64,1024]{1,0:T(8,128)(2,1)S(1)} %get-tuple-element.11), channel_id=1, source_target_pairs={{0,2},{1,3},{2,4},{3,5},{4,6},{5,7},{6,0},{7,1},{8,10},{9,11},{10,... | collective-permute-start | bytes 393224 | tf_op jit(solution)/shard_map/ppermute | solution.py:198
  4.9 11.2 %collective-permute-start.1 = (bf16[64,1024]{1,0:T(8,128)(2,1)S(1)}, bf16[64,1024]{1,0:T(8,128)(2,1)S(1)}, u32[]{:S(2)}, u32[]{:S(2)}) collective-permute-start(bf16[64,1024]{1,0:T(8,128)(2,1)S(1)} %get-tuple-element.12), channel_id=1, source_target_pairs={{0,4},{1,5},{2,6},{3,7},{4,0},{5,1},{6,2},{7,3},{8,12},{9,13},{10,... | collective-permute-start | bytes 393224 | tf_op jit(solution)/shard_map/ppermute | solution.py:198
  7.5 8.6 %collective-permute-start.2 = (bf16[64,1024]{1,0:T(8,128)(2,1)S(1)}, bf16[64,1024]{1,0:T(8,128)(2,1)S(1)}, u32[]{:S(2)}, u32[]{:S(2)}) collective-permute-start(bf16[64,1024]{1,0:T(8,128)(2,1)S(1)} %get-tuple-element.13), channel_id=1, source_target_pairs={{0,6},{1,7},{2,0},{3,1},{4,2},{5,3},{6,4},{7,5},{8,14},{9,15},{10,... | collective-permute-start | bytes 393224 | tf_op jit(solution)/shard_map/ppermute | solution.py:198
  16.6 2.0 %collective-permute-start.3 = (f32[128,1024]{1,0:T(8,128)S(1)}, f32[128,1024]{1,0:T(8,128)S(1)}, u32[]{:S(2)}, u32[]{:S(2)}) collective-permute-start(f32[128,1024]{1,0:T(8,128)S(1)} %get-tuple-element.15.own_ref), channel_id=1, source_target_pairs={{0,1},{1,0},{2,3},{3,2},{4,5},{5,4},{6,7},{7,6},{8,9},{9,8},{10,11... | collective-permute-start | bytes 1572872 | tf_op jit(solution)/shard_map/ppermute | solution.py:79
  19.0 5.9 %collective-permute-start.6 = (f32[256,128]{1,0:T(8,128)S(1)}, f32[256,128]{1,0:T(8,128)S(1)}, u32[]{:S(2)}, u32[]{:S(2)}) collective-permute-start(f32[256,128]{1,0:T(8,128)S(1)} %shard_map.43), channel_id=1, source_target_pairs={{0,24},{1,5},{2,26},{3,7},{4,28},{5,1},{6,30},{7,3},{8,16},{9,13},... | collective-permute-start | bytes 393224 | tf_op jit(solution)/shard_map/ppermute | solution.py:89
  21.5 5.0 %collective-permute-start.5 = (f32[256,128]{1,0:T(8,128)S(1)}, f32[256,128]{1,0:T(8,128)S(1)}, u32[]{:S(2)}, u32[]{:S(2)}) collective-permute-start(f32[256,128]{1,0:T(8,128)S(1)} %shard_map.43), channel_id=1, source_target_pairs={{0,16},{1,7},{2,18},{3,5},{4,20},{5,3},{6,22},{7,1},{8,24},{9,15},... | collective-permute-start | bytes 393224 | tf_op jit(solution)/shard_map/ppermute | solution.py:89
  22.0 5.0 %collective-permute-start.4 = (f32[256,128]{1,0:T(8,128)S(1)}, f32[256,128]{1,0:T(8,128)S(1)}, u32[]{:S(2)}, u32[]{:S(2)}) collective-permute-start(f32[256,128]{1,0:T(8,128)S(1)} %shard_map.43), channel_id=1, source_target_pairs={{0,8},{1,3},{2,10},{3,1},{4,12},{5,7},{6,14},{7,5},{8,0},{9,11},{1... | collective-permute-start | bytes 393224 | tf_op jit(solution)/shard_map/ppermute | solution.py:89
  27.0 5.9 %collective-permute-start.9 = (f32[256,128]{1,0:T(8,128)S(1)}, f32[256,128]{1,0:T(8,128)S(1)}, u32[]{:S(2)}, u32[]{:S(2)}) collective-permute-start(f32[256,128]{1,0:T(8,128)S(1)} %add_add_fusion.1), channel_id=1, source_target_pairs={{0,4},{1,25},{2,6},{3,27},{4,0},{5,29},{6,2},{7,31},{8,12},{9,17},... | collective-permute-start | bytes 393224 | tf_op jit(solution)/shard_map/ppermute | solution.py:89
  29.3 7.9 %collective-permute-start.8 = (f32[256,128]{1,0:T(8,128)S(1)}, f32[256,128]{1,0:T(8,128)S(1)}, u32[]{:S(2)}, u32[]{:S(2)}) collective-permute-start(f32[256,128]{1,0:T(8,128)S(1)} %add_add_fusion.1), channel_id=1, source_target_pairs={{0,6},{1,17},{2,4},{3,19},{4,2},{5,21},{6,0},{7,23},{8,14},{9,25},... | collective-permute-start | bytes 393224 | tf_op jit(solution)/shard_map/ppermute | solution.py:89
  32.7 5.8 %collective-permute-start.7 = (f32[256,128]{1,0:T(8,128)S(1)}, f32[256,128]{1,0:T(8,128)S(1)}, u32[]{:S(2)}, u32[]{:S(2)}) collective-permute-start(f32[256,128]{1,0:T(8,128)S(1)} %add_add_fusion.1), channel_id=1, source_target_pairs={{0,2},{1,9},{2,0},{3,11},{4,6},{5,13},{6,4},{7,15},{8,10},{9,1},{1... | collective-permute-start | bytes 393224 | tf_op jit(solution)/shard_map/ppermute | solution.py:89
  32.7 6.0 %collective-permute-start.11 = (bf16[256,512]{1,0:T(8,128)(2,1)S(1)}, bf16[256,512]{1,0:T(8,128)(2,1)S(1)}, u32[]{:S(2)}, u32[]{:S(2)}) collective-permute-start(bf16[256,512]{1,0:T(8,128)(2,1)S(1)} %get-tuple-element.17), channel_id=1, source_target_pairs={{0,1},{1,0},{2,3},{3,2},{4,5},{5,4},{6,7},{7,6},{8,9},{9,8},{10,11... | collective-permute-start | bytes 786440 | tf_op jit(solution)/shard_map/ppermute | solution.py:79
  38.6 1.4 %collective-permute-start.10 = (f32[256,128]{1,0:T(8,128)S(1)}, f32[256,128]{1,0:T(8,128)S(1)}, u32[]{:S(2)}, u32[]{:S(2)}) collective-permute-start(f32[256,128]{1,0:T(8,128)S(1)} %add_add_fusion.image_ref), channel_id=1, source_target_pairs={{0,1},{1,0},{2,3},{3,2},{4,5},{5,4},{6,7},{7,6},{8,9},{9,8},{10,11... | collective-permute-start | bytes 393224 | tf_op jit(solution)/shard_map/ppermute | solution.py:79

commit v4 on v3

--- a/solution.py
+++ b/solution.py
@@ -113,42 +113,89 @@
 
 def inverse_factor(gram):
     size, tile = gram.shape[0], 8
+    count = size // tile
+    span = max(count // 2, 1)
     lane = lax.broadcasted_iota(jnp.int32, (tile, size), 1)
     level = lax.broadcasted_iota(jnp.int32, (tile, size), 0)
-    def column(rows, index):
-        return jnp.broadcast_to(rows[:, index : index + 1], (tile, size))
+
+    def columns(rows, base):
+        return [jnp.broadcast_to(rows[:, c : c + 1], (tile, size)) for c in range(base, base + tile)]
+
     def spread(rows, index):
         return jnp.broadcast_to(rows[index : index + 1, :], (tile, size))
+
     rows = [gram[first : first + tile, :] for first in range(0, size, tile)]
-    result = []
-    for block in range(size // tile):
-        base = block * tile
-        inside = (lane >= base) & (lane < base + tile)
-        columns = [column(rows[block], base + c) for c in range(tile)]
-        panel = jnp.where(inside, jnp.where(lane - base == level, 1.0, 0.0), rows[block])
-        pivots = jnp.ones((tile, size), f32)
-        inverses, known = [], {}
-        for t in range(tile):
-            pivot = spread(columns[t], t)
-            pivots = jnp.where(level == t, pivot, pivots)
-            inverses.append(1.0 / pivot)
-            ratio = jnp.where(level > t, columns[t], 0.0) * inverses[t]
-            panel = panel - ratio * spread(panel, t)
-            for c in range(t + 1, tile):
-                known[t, c] = spread(columns[c], t)
-                columns[c] = columns[c] - ratio * known[t, c]
-        result.append(jnp.where(lane <= base + level, panel, 0.0) * lax.rsqrt(pivots))
-        spreads = [spread(panel, t) for t in range(tile)]
-        for below in range(block + 1, size // tile):
-            columns = [column(rows[below], base + c) for c in range(tile)]
-            row = jnp.where(inside, 0.0, rows[below])
+    panels, scales = [None] * count, [None] * count
+    ahead = None
+    for start in range(0, count, span):
+        stop = min(start + span, count)
+        for block in range(start, stop):
+            base = block * tile
+            inside = (lane >= base) & (lane < base + tile)
+            diagonal = ahead if block > start else columns(rows[block], base)
+            follow = block + 1 < stop
+            if follow:
+                beside = columns(rows[block], base + tile)
+                under = columns(rows[block + 1], base)
+                ahead = columns(rows[block + 1], base + tile)
+            pivots = jnp.ones((tile, size), f32)
+            inverses, ratios, known = [], [], {}
             for t in range(tile):
-                ratio = columns[t] * inverses[t]
-                row = row - ratio * spreads[t]
+                pivot = spread(diagonal[t], t)
+                pivots = jnp.where(level == t, pivot, pivots)
+                inverses.append(1.0 / pivot)
+                ratios.append(jnp.where(level > t, diagonal[t], 0.0) * inverses[t])
                 for c in range(t + 1, tile):
-                    columns[c] = columns[c] - ratio * known[t, c]
-            rows[below] = row
-    return jnp.concatenate(result, axis=0)
+                    known[t, c] = spread(diagonal[c], t)
+                    diagonal[c] = diagonal[c] - ratios[t] * known[t, c]
+            if follow:
+                for t in range(tile):
+                    ratio = under[t] * inverses[t]
+                    for c in range(t + 1, tile):
+                        under[c] = under[c] - ratio * known[t, c]
+                    for c in range(tile):
+                        across = spread(beside[c], t)
+                        ahead[c] = ahead[c] - ratio * across
+                        beside[c] = beside[c] - ratios[t] * across
+            panel = jnp.where(inside, jnp.where(lane - base == level, 1.0, 0.0), rows[block])
+            spreads = []
+            for t in range(tile):
+                spreads.append(spread(panel, t))
+                panel = panel - ratios[t] * spreads[t]
+            panels[block], scales[block] = panel, pivots
+            for below in range(block + 1, stop):
+                multiples = columns(rows[below], base)
+                row = jnp.where(inside, 0.0, rows[below])
+                for t in range(tile):
+                    ratio = multiples[t] * inverses[t]
+                    row = row - ratio * spreads[t]
+                    for c in range(t + 1, tile):
+                        multiples[c] = multiples[c] - ratio * known[t, c]
+                rows[below] = row
+        if stop < count:
+            first, last = start * tile, stop * tile
+            done = range(start, stop)
+            wide = [
+                jnp.where((lane < last) & (lane > b * tile + level), 0.0, panels[b]) for b in done
+            ]
+            scaled = [panels[b] / scales[b] for b in done]
+            change = lax.dot_general(
+                jnp.concatenate(scaled, axis=0),
+                jnp.concatenate(wide, axis=0),
+                contract_rows,
+                precision=highest,
+                preferred_element_type=f32,
+            )
+            for below in range(stop, count):
+                kept = jnp.where((lane >= first) & (lane < last), 0.0, rows[below])
+                rows[below] = kept - change[below * tile : (below + 1) * tile]
+    return jnp.concatenate(
+        [
+            jnp.where(lane <= b * tile + level, panels[b], 0.0) * lax.rsqrt(scales[b])
+            for b in range(count)
+        ],
+        axis=0,
+    )
 
 
 def outputs_kernel(rows, image_ref, image_other_ref, own_ref, other_ref, basis_ref, core_ref):

time: 46.5 us -> 45.1 us (0.970)
  Pallas kernels: 8.42 us -> 6.96 us
    pallas_call x1, Pallas kernels: 6.37 us -> 4.92 us  [shards(): pl.pallas_call(functools.partial(outputs_kernel, row_count), out_shape=(j...]
where the time goes in v4:
time: 45.1 us; the launch traced here: 44.9 us
  waiting for transfers between devices  20.8 us (46%)
  starting transfers between devices  16.4 us (36%)
  Pallas kernels  6.96 us (15%)
  between operations  0.7 us (2%)
    ppermute x6, waiting for transfers between devices, exchange(): return lax.ppermute(value, ('slab', 'mode'), pairs)  10.3 us
    ppermute x6, starting transfers between devices, exchange(): return lax.ppermute(value, ('slab', 'mode'), pairs)  9.26 us
    ppermute x3, waiting for transfers between devices, shards(): blocks[step] = lax.ppermute(blocks[step], 'mode', pairs)  7.3 us
    ppermute x3, starting transfers between devices, shards(): blocks[step] = lax.ppermute(blocks[step], 'mode', pairs)  7.01 us
    pallas_call x1, Pallas kernels, shards(): pl.pallas_call(functools.partial(outputs_kernel, row_count), out_shape=(j...  4.92 us
    ppermute x3, waiting for transfers between devices, swap_cores(): lax.ppermute(value, 'mode', [(i, i ^ 1) for i in range(lax.axis_size('mod...  3.22 us
    pallas_call x1, Pallas kernels, shards(): pl.pallas_call(split_kernel, out_shape=[pltpu.VMEM((row_count, chip_colum...  1.19 us
  transfers between devices with their start and end apart: 12, of which 10 were waited for; matrix products, arithmetic and copies ran while one was open for 0% of the time, Pallas kernels for 0%

profile of v4, /device:TPU:0, one launch (start us, length us, event | category | flops | bytes accessed | tf_op | source)
XLA Modules:
  0.0 44.9 jit_solution(1615825807850151054)
XLA Ops:
  0.6 1.2 %shard_map.41 = (bf16[64,1024]{1,0:T(8,128)(2,1)S(1)}, bf16[64,1024]{1,0:T(8,128)(2,1)S(1)}, bf16[64,1024]{1,0:T(8,128)(2,1)S(1)}, bf16[64,1024]{1,0:T(8,128)(2,1)S(1)}) custom-call(bf16[64,4096]{1,0:T(8,128)(2,1)} %tensor_ref.1), custom_call_target="tpu_custom_call" | custom-call | tf_op jit(solution)/shard_map/pallas_call | solution.py:236
  1.8 3.1 %collective-permute-start = (bf16[64,1024]{1,0:T(8,128)(2,1)S(1)}, bf16[64,1024]{1,0:T(8,128)(2,1)S(1)}, u32[]{:S(2)}, u32[]{:S(2)}) collective-permute-start(bf16[64,1024]{1,0:T(8,128)(2,1)S(1)} %get-tuple-element.11), channel_id=1, source_target_pairs={{0,2},{1,3},{2,4},{3,5},{4,6},{5,7},{6,0},{7,1},{8,10},{9,11},{10,... | collective-permute-start | bytes 393224 | tf_op jit(solution)/shard_map/ppermute | solution.py:245
  4.9 2.6 %collective-permute-start.1 = (bf16[64,1024]{1,0:T(8,128)(2,1)S(1)}, bf16[64,1024]{1,0:T(8,128)(2,1)S(1)}, u32[]{:S(2)}, u32[]{:S(2)}) collective-permute-start(bf16[64,1024]{1,0:T(8,128)(2,1)S(1)} %get-tuple-element.12), channel_id=1, source_target_pairs={{0,4},{1,5},{2,6},{3,7},{4,0},{5,1},{6,2},{7,3},{8,12},{9,13},{10,... | collective-permute-start | bytes 393224 | tf_op jit(solution)/shard_map/ppermute | solution.py:245
  7.5 1.3 %collective-permute-start.2 = (bf16[64,1024]{1,0:T(8,128)(2,1)S(1)}, bf16[64,1024]{1,0:T(8,128)(2,1)S(1)}, u32[]{:S(2)}, u32[]{:S(2)}) collective-permute-start(bf16[64,1024]{1,0:T(8,128)(2,1)S(1)} %get-tuple-element.13), channel_id=1, source_target_pairs={{0,6},{1,7},{2,0},{3,1},{4,2},{5,3},{6,4},{7,5},{8,14},{9,15},{10,... | collective-permute-start | bytes 393224 | tf_op jit(solution)/shard_map/ppermute | solution.py:245
  8.8 2.5 %collective-permute-done.refs_1_ = bf16[64,1024]{1,0:T(8,128)(2,1)S(1)} collective-permute-done((bf16[64,1024]{1,0:T(8,128)(2,1)S(1)}, bf16[64,1024]{1,0:T(8,128)(2,1)S(1)}, u32[]{:S(2)}, u32[]{:S(2)}) %collective-permute-start) | collective-permute-done | bytes 131104 | tf_op jit(solution)/shard_map/ppermute | solution.py:245
  11.4 4.8 %collective-permute-done.1.refs_2_ = bf16[64,1024]{1,0:T(8,128)(2,1)S(1)} collective-permute-done((bf16[64,1024]{1,0:T(8,128)(2,1)S(1)}, bf16[64,1024]{1,0:T(8,128)(2,1)S(1)}, u32[]{:S(2)}, u32[]{:S(2)}) %collective-permute-start.1) | collective-permute-done | bytes 131104 | tf_op jit(solution)/shard_map/ppermute | solution.py:245
  16.1 0.4 shard_map.42
  16.6 0.1 collective-permute-start.3
  16.7 1.9 %collective-permute-done.3.other_ref = f32[128,1024]{1,0:T(8,128)S(1)} collective-permute-done((f32[128,1024]{1,0:T(8,128)S(1)}, f32[128,1024]{1,0:T(8,128)S(1)}, u32[]{:S(2)}, u32[]{:S(2)}) %collective-permute-start.3) | collective-permute-done | bytes 524320 | tf_op jit(solution)/shard_map/ppermute | solution.py:79
  18.6 0.4 shard_map.43
  19.0 2.5 %collective-permute-start.6 = (f32[256,128]{1,0:T(8,128)S(1)}, f32[256,128]{1,0:T(8,128)S(1)}, u32[]{:S(2)}, u32[]{:S(2)}) collective-permute-start(f32[256,128]{1,0:T(8,128)S(1)} %shard_map.43), channel_id=1, source_target_pairs={{0,24},{1,5},{2,26},{3,7},{4,28},{5,1},{6,30},{7,3},{8,16},{9,13},... | collective-permute-start | bytes 393224 | tf_op jit(solution)/shard_map/ppermute | solution.py:89
  21.5 0.5 %collective-permute-start.5 = (f32[256,128]{1,0:T(8,128)S(1)}, f32[256,128]{1,0:T(8,128)S(1)}, u32[]{:S(2)}, u32[]{:S(2)}) collective-permute-start(f32[256,128]{1,0:T(8,128)S(1)} %shard_map.43), channel_id=1, source_target_pairs={{0,16},{1,7},{2,18},{3,5},{4,20},{5,3},{6,22},{7,1},{8,24},{9,15},... | collective-permute-start | bytes 393224 | tf_op jit(solution)/shard_map/ppermute | solution.py:89
  22.0 0.5 %collective-permute-start.4 = (f32[256,128]{1,0:T(8,128)S(1)}, f32[256,128]{1,0:T(8,128)S(1)}, u32[]{:S(2)}, u32[]{:S(2)}) collective-permute-start(f32[256,128]{1,0:T(8,128)S(1)} %shard_map.43), channel_id=1, source_target_pairs={{0,8},{1,3},{2,10},{3,1},{4,12},{5,7},{6,14},{7,5},{8,0},{9,11},{1... | collective-permute-start | bytes 393224 | tf_op jit(solution)/shard_map/ppermute | solution.py:89
  22.6 2.4 %collective-permute-done.6 = f32[256,128]{1,0:T(8,128)S(1)} collective-permute-done((f32[256,128]{1,0:T(8,128)S(1)}, f32[256,128]{1,0:T(8,128)S(1)}, u32[]{:S(2)}, u32[]{:S(2)}) %collective-permute-start.6) | collective-permute-done | bytes 131104 | tf_op jit(solution)/shard_map/ppermute | solution.py:89
  24.9 1.5 %collective-permute-done.5 = f32[256,128]{1,0:T(8,128)S(1)} collective-permute-done((f32[256,128]{1,0:T(8,128)S(1)}, f32[256,128]{1,0:T(8,128)S(1)}, u32[]{:S(2)}, u32[]{:S(2)}) %collective-permute-start.5) | collective-permute-done | bytes 131104 | tf_op jit(solution)/shard_map/ppermute | solution.py:89
  26.5 0.5 %collective-permute-done.4 = f32[256,128]{1,0:T(8,128)S(1)} collective-permute-done((f32[256,128]{1,0:T(8,128)S(1)}, f32[256,128]{1,0:T(8,128)S(1)}, u32[]{:S(2)}, u32[]{:S(2)}) %collective-permute-start.4) | collective-permute-done | bytes 131104 | tf_op jit(solution)/shard_map/ppermute | solution.py:89
  27.0 2.3 %collective-permute-start.9 = (f32[256,128]{1,0:T(8,128)S(1)}, f32[256,128]{1,0:T(8,128)S(1)}, u32[]{:S(2)}, u32[]{:S(2)}) collective-permute-start(f32[256,128]{1,0:T(8,128)S(1)} %add_add_fusion.1), channel_id=1, source_target_pairs={{0,4},{1,25},{2,6},{3,27},{4,0},{5,29},{6,2},{7,31},{8,12},{9,17},... | collective-permute-start | bytes 393224 | tf_op jit(solution)/shard_map/ppermute | solution.py:89
  29.3 3.4 %collective-permute-start.8 = (f32[256,128]{1,0:T(8,128)S(1)}, f32[256,128]{1,0:T(8,128)S(1)}, u32[]{:S(2)}, u32[]{:S(2)}) collective-permute-start(f32[256,128]{1,0:T(8,128)S(1)} %add_add_fusion.1), channel_id=1, source_target_pairs={{0,6},{1,17},{2,4},{3,19},{4,2},{5,21},{6,0},{7,23},{8,14},{9,25},... | collective-permute-start | bytes 393224 | tf_op jit(solution)/shard_map/ppermute | solution.py:89
  32.7 0.2 collective-permute-done.9
  33.0 4.3 %collective-permute-done.8 = f32[256,128]{1,0:T(8,128)S(1)} collective-permute-done((f32[256,128]{1,0:T(8,128)S(1)}, f32[256,128]{1,0:T(8,128)S(1)}, u32[]{:S(2)}, u32[]{:S(2)}) %collective-permute-start.8) | collective-permute-done | bytes 131104 | tf_op jit(solution)/shard_map/ppermute | solution.py:89
  37.3 1.3 %collective-permute-done.7 = f32[256,128]{1,0:T(8,128)S(1)} collective-permute-done((f32[256,128]{1,0:T(8,128)S(1)}, f32[256,128]{1,0:T(8,128)S(1)}, u32[]{:S(2)}, u32[]{:S(2)}) %collective-permute-start.7) | collective-permute-done | bytes 131104 | tf_op jit(solution)/shard_map/ppermute | solution.py:89
  38.6 0.1 collective-permute-start.10
  38.7 1.3 %collective-permute-done.10.image_other_ref = f32[256,128]{1,0:T(8,128)S(1)} collective-permute-done((f32[256,128]{1,0:T(8,128)S(1)}, f32[256,128]{1,0:T(8,128)S(1)}, u32[]{:S(2)}, u32[]{:S(2)}) %collective-permute-start.10) | collective-permute-done | bytes 131104 | tf_op jit(solution)/shard_map/ppermute | solution.py:79
  40.0 4.9 %shard_map.44 = (f32[64,128]{1,0:T(8,128)}, f32[512,128]{1,0:T(8,128)}) custom-call(f32[256,128]{1,0:T(8,128)S(1)} %add_add_fusion.image_ref, f32[256,128]{1,0:T(8,128)S(1)} %collective-permute-done.10.image_other_ref, bf16[256,512]{1,0:T(8,128)(2,1)S(1)} %get-tuple-element.16.own_ref, bf16[256,512]{1,0:T(8,128)(2,1)S(1)} %collective-permute-done.11.other_ref), custom_call_target="tpu_custom_call" | custom-call | tf_op jit(solution)/shard_map/pallas_call | solution.py:270
  (8 shorter events, 0.1 us)
Async XLA Ops:
  0.6 15.5 %copy-start = (f32[512,128]{1,0:T(8,128)S(1)}, f32[512,128]{1,0:T(8,128)}, u32[]{:S(2)}) copy-start(f32[512,128]{1,0:T(8,128)} %start_ref.1) | copy-start | bytes 786436
  1.8 9.5 %collective-permute-start = (bf16[64,1024]{1,0:T(8,128)(2,1)S(1)}, bf16[64,1024]{1,0:T(8,128)(2,1)S(1)}, u32[]{:S(2)}, u32[]{:S(2)}) collective-permute-start(bf16[64,1024]{1,0:T(8,128)(2,1)S(1)} %get-tuple-element.11), channel_id=1, source_target_pairs={{0,2},{1,3},{2,4},{3,5},{4,6},{5,7},{6,0},{7,1},{8,10},{9,11},{10,... | collective-permute-start | bytes 393224 | tf_op jit(solution)/shard_map/ppermute | solution.py:245
  4.9 11.2 %collective-permute-start.1 = (bf16[64,1024]{1,0:T(8,128)(2,1)S(1)}, bf16[64,1024]{1,0:T(8,128)(2,1)S(1)}, u32[]{:S(2)}, u32[]{:S(2)}) collective-permute-start(bf16[64,1024]{1,0:T(8,128)(2,1)S(1)} %get-tuple-element.12), channel_id=1, source_target_pairs={{0,4},{1,5},{2,6},{3,7},{4,0},{5,1},{6,2},{7,3},{8,12},{9,13},{10,... | collective-permute-start | bytes 393224 | tf_op jit(solution)/shard_map/ppermute | solution.py:245
  7.5 8.6 %collective-permute-start.2 = (bf16[64,1024]{1,0:T(8,128)(2,1)S(1)}, bf16[64,1024]{1,0:T(8,128)(2,1)S(1)}, u32[]{:S(2)}, u32[]{:S(2)}) collective-permute-start(bf16[64,1024]{1,0:T(8,128)(2,1)S(1)} %get-tuple-element.13), channel_id=1, source_target_pairs={{0,6},{1,7},{2,0},{3,1},{4,2},{5,3},{6,4},{7,5},{8,14},{9,15},{10,... | collective-permute-start | bytes 393224 | tf_op jit(solution)/shard_map/ppermute | solution.py:245
  16.6 2.0 %collective-permute-start.3 = (f32[128,1024]{1,0:T(8,128)S(1)}, f32[128,1024]{1,0:T(8,128)S(1)}, u32[]{:S(2)}, u32[]{:S(2)}) collective-permute-start(f32[128,1024]{1,0:T(8,128)S(1)} %get-tuple-element.15.own_ref), channel_id=1, source_target_pairs={{0,1},{1,0},{2,3},{3,2},{4,5},{5,4},{6,7},{7,6},{8,9},{9,8},{10,11... | collective-permute-start | bytes 1572872 | tf_op jit(solution)/shard_map/ppermute | solution.py:79
  19.0 5.9 %collective-permute-start.6 = (f32[256,128]{1,0:T(8,128)S(1)}, f32[256,128]{1,0:T(8,128)S(1)}, u32[]{:S(2)}, u32[]{:S(2)}) collective-permute-start(f32[256,128]{1,0:T(8,128)S(1)} %shard_map.43), channel_id=1, source_target_pairs={{0,24},{1,5},{2,26},{3,7},{4,28},{5,1},{6,30},{7,3},{8,16},{9,13},... | collective-permute-start | bytes 393224 | tf_op jit(solution)/shard_map/ppermute | solution.py:89
  21.5 5.0 %collective-permute-start.5 = (f32[256,128]{1,0:T(8,128)S(1)}, f32[256,128]{1,0:T(8,128)S(1)}, u32[]{:S(2)}, u32[]{:S(2)}) collective-permute-start(f32[256,128]{1,0:T(8,128)S(1)} %shard_map.43), channel_id=1, source_target_pairs={{0,16},{1,7},{2,18},{3,5},{4,20},{5,3},{6,22},{7,1},{8,24},{9,15},... | collective-permute-start | bytes 393224 | tf_op jit(solution)/shard_map/ppermute | solution.py:89
  22.0 5.0 %collective-permute-start.4 = (f32[256,128]{1,0:T(8,128)S(1)}, f32[256,128]{1,0:T(8,128)S(1)}, u32[]{:S(2)}, u32[]{:S(2)}) collective-permute-start(f32[256,128]{1,0:T(8,128)S(1)} %shard_map.43), channel_id=1, source_target_pairs={{0,8},{1,3},{2,10},{3,1},{4,12},{5,7},{6,14},{7,5},{8,0},{9,11},{1... | collective-permute-start | bytes 393224 | tf_op jit(solution)/shard_map/ppermute | solution.py:89
  27.0 5.9 %collective-permute-start.9 = (f32[256,128]{1,0:T(8,128)S(1)}, f32[256,128]{1,0:T(8,128)S(1)}, u32[]{:S(2)}, u32[]{:S(2)}) collective-permute-start(f32[256,128]{1,0:T(8,128)S(1)} %add_add_fusion.1), channel_id=1, source_target_pairs={{0,4},{1,25},{2,6},{3,27},{4,0},{5,29},{6,2},{7,31},{8,12},{9,17},... | collective-permute-start | bytes 393224 | tf_op jit(solution)/shard_map/ppermute | solution.py:89
  29.3 7.9 %collective-permute-start.8 = (f32[256,128]{1,0:T(8,128)S(1)}, f32[256,128]{1,0:T(8,128)S(1)}, u32[]{:S(2)}, u32[]{:S(2)}) collective-permute-start(f32[256,128]{1,0:T(8,128)S(1)} %add_add_fusion.1), channel_id=1, source_target_pairs={{0,6},{1,17},{2,4},{3,19},{4,2},{5,21},{6,0},{7,23},{8,14},{9,25},... | collective-permute-start | bytes 393224 | tf_op jit(solution)/shard_map/ppermute | solution.py:89
  32.7 5.8 %collective-permute-start.7 = (f32[256,128]{1,0:T(8,128)S(1)}, f32[256,128]{1,0:T(8,128)S(1)}, u32[]{:S(2)}, u32[]{:S(2)}) collective-permute-start(f32[256,128]{1,0:T(8,128)S(1)} %add_add_fusion.1), channel_id=1, source_target_pairs={{0,2},{1,9},{2,0},{3,11},{4,6},{5,13},{6,4},{7,15},{8,10},{9,1},{1... | collective-permute-start | bytes 393224 | tf_op jit(solution)/shard_map/ppermute | solution.py:89
  32.7 6.0 %collective-permute-start.11 = (bf16[256,512]{1,0:T(8,128)(2,1)S(1)}, bf16[256,512]{1,0:T(8,128)(2,1)S(1)}, u32[]{:S(2)}, u32[]{:S(2)}) collective-permute-start(bf16[256,512]{1,0:T(8,128)(2,1)S(1)} %get-tuple-element.17), channel_id=1, source_target_pairs={{0,1},{1,0},{2,3},{3,2},{4,5},{5,4},{6,7},{7,6},{8,9},{9,8},{10,11... | collective-permute-start | bytes 786440 | tf_op jit(solution)/shard_map/ppermute | solution.py:79
  38.6 1.4 %collective-permute-start.10 = (f32[256,128]{1,0:T(8,128)S(1)}, f32[256,128]{1,0:T(8,128)S(1)}, u32[]{:S(2)}, u32[]{:S(2)}) collective-permute-start(f32[256,128]{1,0:T(8,128)S(1)} %add_add_fusion.image_ref), channel_id=1, source_target_pairs={{0,1},{1,0},{2,3},{3,2},{4,5},{5,4},{6,7},{7,6},{8,9},{9,8},{10,11... | collective-permute-start | bytes 393224 | tf_op jit(solution)/shard_map/ppermute | solution.py:79

commit v5 on v4

--- a/solution.py
+++ b/solution.py
@@ -31,17 +31,15 @@
     return [pl.BlockSpec(memory_space=pltpu.VMEM)] * count
 
 
-def split_kernel(tensor_ref, *refs):
+def split_kernel(masks, tensor_ref, *refs):
     blocks, semaphores = refs[:-1], refs[-1]
-    chips = len(blocks)
     width = blocks[0].shape[1]
     chip = lax.axis_index("mode") // 2
     copies = []
-    for step, block in enumerate(blocks):
-        target = lax.rem(chip + step, chips)
-        columns = pl.ds(pl.multiple_of(target * width, width), width)
+    for place, (mask, block) in enumerate(zip(masks, blocks)):
+        columns = pl.ds(pl.multiple_of((chip ^ mask) * width, width), width)
         copies.append(
-            pltpu.make_async_copy(tensor_ref.at[:, columns], block, semaphores.at[step])
+            pltpu.make_async_copy(tensor_ref.at[:, columns], block, semaphores.at[place])
         )
     for copy in copies:
         copy.start()
@@ -49,20 +47,20 @@
         copy.wait()
 
 
-def inner_kernel(chips, start_ref, *refs):
-    blocks, (inner_ref, held_ref, own_ref, away_ref) = refs[:chips], refs[chips:]
+def inner_kernel(masks, start_ref, *refs):
+    blocks, (inner_ref, held_ref, own_ref, away_ref) = refs[: len(masks)], refs[len(masks) :]
     mode_index = lax.axis_index("mode")
     chip, core = mode_index // 2, mode_index % 2
     rows, width = blocks[0].shape
     half = width // 2
     starts = []
-    for step in range(chips):
-        source = lax.rem(chip + chips - step, chips)
+    for mask, block in zip(masks, blocks):
+        source = chip ^ mask
         place = pl.ds(pl.multiple_of(source * rows, rows), rows)
-        held_ref[place, :] = blocks[step][...]
-        own_ref[place, :] = blocks[step][:, pl.ds(pl.multiple_of(core * half, half), half)]
-        away_ref[place, :] = blocks[step][:, pl.ds(pl.multiple_of((1 - core) * half, half), half)]
-        first = pl.multiple_of((source * 2 + core) * rows, rows)
+        held_ref[place, :] = block[...]
+        own_ref[place, :] = block[:, pl.ds(pl.multiple_of(core * half, half), half)]
+        away_ref[place, :] = block[:, pl.ds(pl.multiple_of((1 - core) * half, half), half)]
+        first = pl.multiple_of((source * 2 + (core ^ (mask & 1))) * rows, rows)
         starts.append(start_ref[pl.ds(first, rows), :])
     ordered = jnp.concatenate([block[...] for block in blocks], axis=0)
     high, low = two_parts(jnp.concatenate(starts, axis=0))
@@ -84,8 +82,10 @@
     pairs = []
     for slab in range(slabs):
         for mode in range(modes):
-            slab_mask, chip_mask = odd_masks if mode % 2 else even_masks
-            pairs.append((slab * modes + mode, (slab ^ slab_mask) * modes + (mode ^ 2 * chip_mask)))
+            half = (mode % 2) ^ (mode // 2) % 2
+            slab_mask, chip_mask = odd_masks if half else even_masks
+            target = (slab ^ slab_mask) * modes + (mode ^ (2 * chip_mask + chip_mask % 2))
+            pairs.append((slab * modes + mode, target))
     return lax.ppermute(value, ("slab", "mode"), pairs)
 
 
@@ -198,29 +198,34 @@
     )
 
 
-def outputs_kernel(rows, image_ref, image_other_ref, own_ref, other_ref, basis_ref, core_ref):
+def outputs_kernel(image_ref, image_other_ref, own_ref, other_ref, basis_ref, core_ref, basis_own_ref):
     mode_index = lax.axis_index("mode")
-    chip, even = mode_index // 2, mode_index % 2 == 0
+    first = mode_index % 2 == mode_index // 2 % 2
     image, image_other = image_ref[...], image_other_ref[...]
     image_block = jnp.concatenate(
-        [jnp.where(even, image, image_other), jnp.where(even, image_other, image)], axis=0
+        [jnp.where(first, image, image_other), jnp.where(first, image_other, image)], axis=0
     )
     small_gram = lax.dot_general(
         image_block, image_block, contract_rows, precision=highest, preferred_element_type=f32
     )
     inverse = inverse_factor(small_gram)
-    basis_full = lax.dot_general(
-        image_block, inverse, contract_last, precision=highest, preferred_element_type=f32
-    )
-    held = image.shape[0]
-    basis_own = jnp.where(even, basis_full[:held], basis_full[held:])
-    basis_other = jnp.where(even, basis_full[held:], basis_full[:held])
-    for place in range(held // rows):
-        @pl.when(chip == place)
-        def _():
-            basis_ref[...] = basis_own[place * rows : (place + 1) * rows]
+    basis_own, basis_other = [
+        lax.dot_general(part, inverse, contract_last, precision=highest, preferred_element_type=f32)
+        for part in (image, image_other)
+    ]
+    basis_own_ref[...] = basis_own
+    rows = basis_ref.shape[0]
+    place = pl.multiple_of(mode_index // 2 * rows, rows)
+    basis_ref[...] = basis_own_ref[pl.ds(place, rows), :]
     core_ref[...] = dot(own_ref[...], basis_own.astype(bf16), contract_rows) + dot(
         other_ref[...], basis_other.astype(bf16), contract_rows
+    )
+
+
+def in_chips(value, mask):
+    flipped = 2 * mask + (mask & 1)
+    return lax.ppermute(
+        value, "mode", [(i, i ^ flipped) for i in range(lax.axis_size("mode"))]
     )
 
 
@@ -228,24 +233,25 @@
     row_count, slab_columns = tensor.shape
     modes = lax.axis_size("mode")
     chips = modes // 2
+    far_mask = chips // 2
     chip_columns = slab_columns // chips
     own_columns = chip_columns // 2
     held_rows = chips * row_count
     rank = start_block.shape[1]
 
+    masks = [0, far_mask] + [mask for mask in reversed(range(1, chips)) if mask != far_mask]
     blocks = list(pl.pallas_call(
-        split_kernel,
+        functools.partial(split_kernel, masks),
         out_shape=[pltpu.VMEM((row_count, chip_columns), bf16)] * chips,
         in_specs=[pl.BlockSpec(memory_space=pl.ANY)],
         out_specs=vmem_specs(chips),
         scratch_shapes=[pltpu.SemaphoreType.DMA((chips,))],
     )(tensor))
-    for step in sorted(range(1, chips), key=lambda step: -min(step, chips - step)):
-        pairs = [(i, (i + 2 * step) % modes) for i in range(modes)]
-        blocks[step] = lax.ppermute(blocks[step], "mode", pairs)
+    for place in range(1, chips):
+        blocks[place] = in_chips(blocks[place], masks[place])
 
     inner, held, own_half, away_half = pl.pallas_call(
-        functools.partial(inner_kernel, chips),
+        functools.partial(inner_kernel, masks),
         out_shape=(
             pltpu.VMEM((rank, chip_columns), f32),
             pltpu.VMEM((held_rows, chip_columns), bf16),
@@ -268,13 +274,14 @@
     image_other = swap_cores(image)
 
     return pl.pallas_call(
-        functools.partial(outputs_kernel, row_count),
+        outputs_kernel,
         out_shape=(
             jax.ShapeDtypeStruct((row_count, rank), f32),
             jax.ShapeDtypeStruct((own_columns, rank), f32),
         ),
         in_specs=vmem_specs(4),
         out_specs=tuple(vmem_specs(2)),
+        scratch_shapes=[pltpu.VMEM((held_rows, rank), f32)],
     )(*in_vmem(image, image_other, own_half, other_half))
 
 

time: 45.1 us -> 43.8 us (0.971)
  starting transfers between devices: 16.4 us -> 14.5 us
  waiting for transfers between devices: 20.8 us -> 21.7 us
    ppermute x3, starting transfers between devices: 7.01 us -> 4.84 us  [in_chips(): lax.ppermute(value, 'mode', [(i, i ^ flipped) for i in range(lax.axis_siz...]
    ppermute x3, waiting for transfers between devices: 7.3 us -> 9.25 us  [in_chips(): lax.ppermute(value, 'mode', [(i, i ^ flipped) for i in range(lax.axis_siz...]
    ppermute x3, starting transfers between devices: 0.14 us -> 1.55 us  [swap_cores(): lax.ppermute(value, 'mode', [(i, i ^ 1) for i in range(lax.axis_size('mod...]
    ppermute x6, starting transfers between devices: 9.26 us -> 8.11 us  [exchange(): return lax.ppermute(value, ('slab', 'mode'), pairs)]
    ppermute x6, waiting for transfers between devices: 10.3 us -> 9.56 us  [exchange(): return lax.ppermute(value, ('slab', 'mode'), pairs)]
  transfers between devices with their start and end apart: 12 -> 12, of which waited for: 10 -> 8; matrix products, arithmetic and copies ran while one was open for 0% -> 0% of each run, Pallas kernels for 0% -> 0%
where the time goes in v5:
time: 43.8 us; the launch traced here: 43.6 us
  waiting for transfers between devices  21.7 us (50%)
  starting transfers between devices  14.5 us (33%)
  Pallas kernels  6.68 us (15%)
  between operations  0.7 us (2%)
    ppermute x6, waiting for transfers between devices, exchange(): return lax.ppermute(value, ('slab', 'mode'), pairs)  9.56 us
    ppermute x3, waiting for transfers between devices, in_chips(): lax.ppermute(value, 'mode', [(i, i ^ flipped) for i in range(lax.axis_siz...  9.25 us
    ppermute x6, starting transfers between devices, exchange(): return lax.ppermute(value, ('slab', 'mode'), pairs)  8.11 us
    ppermute x3, starting transfers between devices, in_chips(): lax.ppermute(value, 'mode', [(i, i ^ flipped) for i in range(lax.axis_siz...  4.84 us
    pallas_call x1, Pallas kernels, shards(): pl.pallas_call(outputs_kernel, out_shape=(jax.ShapeDtypeStruct((row_count...  4.64 us
    ppermute x3, waiting for transfers between devices, swap_cores(): lax.ppermute(value, 'mode', [(i, i ^ 1) for i in range(lax.axis_size('mod...  2.86 us
    ppermute x3, starting transfers between devices, swap_cores(): lax.ppermute(value, 'mode', [(i, i ^ 1) for i in range(lax.axis_size('mod...  1.55 us
    pallas_call x1, Pallas kernels, shards(): pl.pallas_call(functools.partial(split_kernel, masks), out_shape=[pltpu.V...  1.18 us
  transfers between devices with their start and end apart: 12, of which 8 were waited for; matrix products, arithmetic and copies ran while one was open for 0% of the time, Pallas kernels for 0%

profile of v5, /device:TPU:0, one launch (start us, length us, event | category | flops | bytes accessed | tf_op | source)
XLA Modules:
  0.0 43.6 jit_solution(1163236314664969880)
XLA Ops:
  0.6 1.2 %shard_map.41 = (bf16[64,1024]{1,0:T(8,128)(2,1)S(1)}, bf16[64,1024]{1,0:T(8,128)(2,1)S(1)}, bf16[64,1024]{1,0:T(8,128)(2,1)S(1)}, bf16[64,1024]{1,0:T(8,128)(2,1)S(1)}) custom-call(bf16[64,4096]{1,0:T(8,128)(2,1)} %tensor_ref.1), custom_call_target="tpu_custom_call" | custom-call | tf_op jit(solution)/shard_map/pallas_call | solution.py:243
  1.8 4.1 %collective-permute-start = (bf16[64,1024]{1,0:T(8,128)(2,1)S(1)}, bf16[64,1024]{1,0:T(8,128)(2,1)S(1)}, u32[]{:S(2)}, u32[]{:S(2)}) collective-permute-start(bf16[64,1024]{1,0:T(8,128)(2,1)S(1)} %get-tuple-element.11), channel_id=1, source_target_pairs={{0,4},{1,5},{2,6},{3,7},{4,0},{5,1},{6,2},{7,3},{8,12},{9,13},{10,... | collective-permute-start | bytes 393224 | tf_op jit(solution)/shard_map/ppermute | solution.py:227
  5.9 0.5 %collective-permute-start.1 = (bf16[64,1024]{1,0:T(8,128)(2,1)S(1)}, bf16[64,1024]{1,0:T(8,128)(2,1)S(1)}, u32[]{:S(2)}, u32[]{:S(2)}) collective-permute-start(bf16[64,1024]{1,0:T(8,128)(2,1)S(1)} %get-tuple-element.12), channel_id=1, source_target_pairs={{0,7},{1,6},{2,5},{3,4},{4,3},{5,2},{6,1},{7,0},{8,15},{9,14},{10,... | collective-permute-start | bytes 393224 | tf_op jit(solution)/shard_map/ppermute | solution.py:227
  6.5 0.2 collective-permute-start.2
  6.7 9.2 %collective-permute-done.refs_1_ = bf16[64,1024]{1,0:T(8,128)(2,1)S(1)} collective-permute-done((bf16[64,1024]{1,0:T(8,128)(2,1)S(1)}, bf16[64,1024]{1,0:T(8,128)(2,1)S(1)}, u32[]{:S(2)}, u32[]{:S(2)}) %collective-permute-start) | collective-permute-done | bytes 131104 | tf_op jit(solution)/shard_map/ppermute | solution.py:227
  15.9 0.0 collective-permute-done.1.refs_2_
  15.9 0.4 shard_map.42
  16.4 0.7 %collective-permute-start.3 = (f32[128,1024]{1,0:T(8,128)S(1)}, f32[128,1024]{1,0:T(8,128)S(1)}, u32[]{:S(2)}, u32[]{:S(2)}) collective-permute-start(f32[128,1024]{1,0:T(8,128)S(1)} %get-tuple-element.15.own_ref), channel_id=1, source_target_pairs={{0,1},{1,0},{2,3},{3,2},{4,5},{5,4},{6,7},{7,6},{8,9},{9,8},{10,11... | collective-permute-start | bytes 1572872 | tf_op jit(solution)/shard_map/ppermute | solution.py:77
  17.0 1.5 %collective-permute-done.3.other_ref = f32[128,1024]{1,0:T(8,128)S(1)} collective-permute-done((f32[128,1024]{1,0:T(8,128)S(1)}, f32[128,1024]{1,0:T(8,128)S(1)}, u32[]{:S(2)}, u32[]{:S(2)}) %collective-permute-start.3) | collective-permute-done | bytes 524320 | tf_op jit(solution)/shard_map/ppermute | solution.py:77
  18.6 0.4 %shard_map.43 = f32[256,128]{1,0:T(8,128)S(1)} custom-call(bf16[256,1024]{1,0:T(8,128)(2,1)S(1)} %get-tuple-element.14.held_ref, f32[128,1024]{1,0:T(8,128)S(1)} %get-tuple-element.15.own_ref, f32[128,1024]{1,0:T(8,128)S(1)} %collective-permute-done.3.other_ref), custom_call_target="tpu_custom_call" | custom-call | tf_op jit(solution)/shard_map/pallas_call | solution.py:267
  19.0 2.6 %collective-permute-start.6 = (f32[256,128]{1,0:T(8,128)S(1)}, f32[256,128]{1,0:T(8,128)S(1)}, u32[]{:S(2)}, u32[]{:S(2)}) collective-permute-start(f32[256,128]{1,0:T(8,128)S(1)} %shard_map.43), channel_id=1, source_target_pairs={{0,24},{1,5},{2,6},{3,27},{4,28},{5,1},{6,2},{7,31},{8,16},{9,13},... | collective-permute-start | bytes 393224 | tf_op jit(solution)/shard_map/ppermute | solution.py:89
  21.6 0.5 %collective-permute-start.5 = (f32[256,128]{1,0:T(8,128)S(1)}, f32[256,128]{1,0:T(8,128)S(1)}, u32[]{:S(2)}, u32[]{:S(2)}) collective-permute-start(f32[256,128]{1,0:T(8,128)S(1)} %shard_map.43), channel_id=1, source_target_pairs={{0,16},{1,6},{2,5},{3,19},{4,20},{5,2},{6,1},{7,23},{8,24},{9,14},... | collective-permute-start | bytes 393224 | tf_op jit(solution)/shard_map/ppermute | solution.py:89
  22.1 0.4 collective-permute-start.4
  22.6 2.4 %collective-permute-done.6 = f32[256,128]{1,0:T(8,128)S(1)} collective-permute-done((f32[256,128]{1,0:T(8,128)S(1)}, f32[256,128]{1,0:T(8,128)S(1)}, u32[]{:S(2)}, u32[]{:S(2)}) %collective-permute-start.6) | collective-permute-done | bytes 131104 | tf_op jit(solution)/shard_map/ppermute | solution.py:89
  24.9 1.7 %collective-permute-done.5 = f32[256,128]{1,0:T(8,128)S(1)} collective-permute-done((f32[256,128]{1,0:T(8,128)S(1)}, f32[256,128]{1,0:T(8,128)S(1)}, u32[]{:S(2)}, u32[]{:S(2)}) %collective-permute-start.5) | collective-permute-done | bytes 131104 | tf_op jit(solution)/shard_map/ppermute | solution.py:89
  26.6 0.5 %collective-permute-done.4 = f32[256,128]{1,0:T(8,128)S(1)} collective-permute-done((f32[256,128]{1,0:T(8,128)S(1)}, f32[256,128]{1,0:T(8,128)S(1)}, u32[]{:S(2)}, u32[]{:S(2)}) %collective-permute-start.4) | collective-permute-done | bytes 131104 | tf_op jit(solution)/shard_map/ppermute | solution.py:89
  27.1 4.2 %collective-permute-start.9 = (f32[256,128]{1,0:T(8,128)S(1)}, f32[256,128]{1,0:T(8,128)S(1)}, u32[]{:S(2)}, u32[]{:S(2)}) collective-permute-start(f32[256,128]{1,0:T(8,128)S(1)} %add_add_fusion.1), channel_id=1, source_target_pairs={{0,4},{1,25},{2,26},{3,7},{4,0},{5,29},{6,30},{7,3},{8,12},{9,17},... | collective-permute-start | bytes 393224 | tf_op jit(solution)/shard_map/ppermute | solution.py:89
  31.3 0.4 collective-permute-start.7
  31.7 0.8 %collective-permute-start.11 = (bf16[256,512]{1,0:T(8,128)(2,1)S(1)}, bf16[256,512]{1,0:T(8,128)(2,1)S(1)}, u32[]{:S(2)}, u32[]{:S(2)}) collective-permute-start(bf16[256,512]{1,0:T(8,128)(2,1)S(1)} %get-tuple-element.17), channel_id=1, source_target_pairs={{0,1},{1,0},{2,3},{3,2},{4,5},{5,4},{6,7},{7,6},{8,9},{9,8},{10,11... | collective-permute-start | bytes 786440 | tf_op jit(solution)/shard_map/ppermute | solution.py:77
  32.5 1.8 %collective-permute-done.9 = f32[256,128]{1,0:T(8,128)S(1)} collective-permute-done((f32[256,128]{1,0:T(8,128)S(1)}, f32[256,128]{1,0:T(8,128)S(1)}, u32[]{:S(2)}, u32[]{:S(2)}) %collective-permute-start.9) | collective-permute-done | bytes 131104 | tf_op jit(solution)/shard_map/ppermute | solution.py:89
  34.3 3.2 %collective-permute-done.8 = f32[256,128]{1,0:T(8,128)S(1)} collective-permute-done((f32[256,128]{1,0:T(8,128)S(1)}, f32[256,128]{1,0:T(8,128)S(1)}, u32[]{:S(2)}, u32[]{:S(2)}) %collective-permute-start.8) | collective-permute-done | bytes 131104 | tf_op jit(solution)/shard_map/ppermute | solution.py:89
  37.6 0.1 collective-permute-start.10
  37.6 1.3 %collective-permute-done.10.image_other_ref = f32[256,128]{1,0:T(8,128)S(1)} collective-permute-done((f32[256,128]{1,0:T(8,128)S(1)}, f32[256,128]{1,0:T(8,128)S(1)}, u32[]{:S(2)}, u32[]{:S(2)}) %collective-permute-start.10) | collective-permute-done | bytes 131104 | tf_op jit(solution)/shard_map/ppermute | solution.py:77
  39.0 4.6 %shard_map.44 = (f32[64,128]{1,0:T(8,128)}, f32[512,128]{1,0:T(8,128)}) custom-call(f32[256,128]{1,0:T(8,128)S(1)} %add_add_fusion.image_ref, f32[256,128]{1,0:T(8,128)S(1)} %collective-permute-done.10.image_other_ref, bf16[256,512]{1,0:T(8,128)(2,1)S(1)} %get-tuple-element.16.own_ref, bf16[256,512]{1,0:T(8,128)(2,1)S(1)} %collective-permute-done.11.other_ref), custom_call_target="tpu_custom_call" | custom-call | tf_op jit(solution)/shard_map/pallas_call | solution.py:276
  (8 shorter events, 0.1 us)
Async XLA Ops:
  0.6 15.3 %copy-start = (f32[512,128]{1,0:T(8,128)S(1)}, f32[512,128]{1,0:T(8,128)}, u32[]{:S(2)}) copy-start(f32[512,128]{1,0:T(8,128)} %start_ref.1) | copy-start | bytes 786436
  1.8 14.1 %collective-permute-start = (bf16[64,1024]{1,0:T(8,128)(2,1)S(1)}, bf16[64,1024]{1,0:T(8,128)(2,1)S(1)}, u32[]{:S(2)}, u32[]{:S(2)}) collective-permute-start(bf16[64,1024]{1,0:T(8,128)(2,1)S(1)} %get-tuple-element.11), channel_id=1, source_target_pairs={{0,4},{1,5},{2,6},{3,7},{4,0},{5,1},{6,2},{7,3},{8,12},{9,13},{10,... | collective-permute-start | bytes 393224 | tf_op jit(solution)/shard_map/ppermute | solution.py:227
  5.9 10.0 %collective-permute-start.1 = (bf16[64,1024]{1,0:T(8,128)(2,1)S(1)}, bf16[64,1024]{1,0:T(8,128)(2,1)S(1)}, u32[]{:S(2)}, u32[]{:S(2)}) collective-permute-start(bf16[64,1024]{1,0:T(8,128)(2,1)S(1)} %get-tuple-element.12), channel_id=1, source_target_pairs={{0,7},{1,6},{2,5},{3,4},{4,3},{5,2},{6,1},{7,0},{8,15},{9,14},{10,... | collective-permute-start | bytes 393224 | tf_op jit(solution)/shard_map/ppermute | solution.py:227
  6.5 9.5 %collective-permute-start.2 = (bf16[64,1024]{1,0:T(8,128)(2,1)S(1)}, bf16[64,1024]{1,0:T(8,128)(2,1)S(1)}, u32[]{:S(2)}, u32[]{:S(2)}) collective-permute-start(bf16[64,1024]{1,0:T(8,128)(2,1)S(1)} %get-tuple-element.13), channel_id=1, source_target_pairs={{0,3},{1,2},{2,1},{3,0},{4,7},{5,6},{6,5},{7,4},{8,11},{9,10},{10,... | collective-permute-start | bytes 393224 | tf_op jit(solution)/shard_map/ppermute | solution.py:227
  16.4 2.2 %collective-permute-start.3 = (f32[128,1024]{1,0:T(8,128)S(1)}, f32[128,1024]{1,0:T(8,128)S(1)}, u32[]{:S(2)}, u32[]{:S(2)}) collective-permute-start(f32[128,1024]{1,0:T(8,128)S(1)} %get-tuple-element.15.own_ref), channel_id=1, source_target_pairs={{0,1},{1,0},{2,3},{3,2},{4,5},{5,4},{6,7},{7,6},{8,9},{9,8},{10,11... | collective-permute-start | bytes 1572872 | tf_op jit(solution)/shard_map/ppermute | solution.py:77
  19.0 5.9 %collective-permute-start.6 = (f32[256,128]{1,0:T(8,128)S(1)}, f32[256,128]{1,0:T(8,128)S(1)}, u32[]{:S(2)}, u32[]{:S(2)}) collective-permute-start(f32[256,128]{1,0:T(8,128)S(1)} %shard_map.43), channel_id=1, source_target_pairs={{0,24},{1,5},{2,6},{3,27},{4,28},{5,1},{6,2},{7,31},{8,16},{9,13},... | collective-permute-start | bytes 393224 | tf_op jit(solution)/shard_map/ppermute | solution.py:89
  21.6 5.0 %collective-permute-start.5 = (f32[256,128]{1,0:T(8,128)S(1)}, f32[256,128]{1,0:T(8,128)S(1)}, u32[]{:S(2)}, u32[]{:S(2)}) collective-permute-start(f32[256,128]{1,0:T(8,128)S(1)} %shard_map.43), channel_id=1, source_target_pairs={{0,16},{1,6},{2,5},{3,19},{4,20},{5,2},{6,1},{7,23},{8,24},{9,14},... | collective-permute-start | bytes 393224 | tf_op jit(solution)/shard_map/ppermute | solution.py:89
  22.1 5.0 %collective-permute-start.4 = (f32[256,128]{1,0:T(8,128)S(1)}, f32[256,128]{1,0:T(8,128)S(1)}, u32[]{:S(2)}, u32[]{:S(2)}) collective-permute-start(f32[256,128]{1,0:T(8,128)S(1)} %shard_map.43), channel_id=1, source_target_pairs={{0,8},{1,2},{2,1},{3,11},{4,12},{5,6},{6,5},{7,15},{8,0},{9,10},{1... | collective-permute-start | bytes 393224 | tf_op jit(solution)/shard_map/ppermute | solution.py:89
  27.1 7.1 %collective-permute-start.9 = (f32[256,128]{1,0:T(8,128)S(1)}, f32[256,128]{1,0:T(8,128)S(1)}, u32[]{:S(2)}, u32[]{:S(2)}) collective-permute-start(f32[256,128]{1,0:T(8,128)S(1)} %add_add_fusion.1), channel_id=1, source_target_pairs={{0,4},{1,25},{2,26},{3,7},{4,0},{5,29},{6,30},{7,3},{8,12},{9,17},... | collective-permute-start | bytes 393224 | tf_op jit(solution)/shard_map/ppermute | solution.py:89
  31.3 6.2 %collective-permute-start.8 = (f32[256,128]{1,0:T(8,128)S(1)}, f32[256,128]{1,0:T(8,128)S(1)}, u32[]{:S(2)}, u32[]{:S(2)}) collective-permute-start(f32[256,128]{1,0:T(8,128)S(1)} %add_add_fusion.1), channel_id=1, source_target_pairs={{0,7},{1,17},{2,18},{3,4},{4,3},{5,21},{6,22},{7,0},{8,15},{9,25},... | collective-permute-start | bytes 393224 | tf_op jit(solution)/shard_map/ppermute | solution.py:89
  31.3 6.2 %collective-permute-start.7 = (f32[256,128]{1,0:T(8,128)S(1)}, f32[256,128]{1,0:T(8,128)S(1)}, u32[]{:S(2)}, u32[]{:S(2)}) collective-permute-start(f32[256,128]{1,0:T(8,128)S(1)} %add_add_fusion.1), channel_id=1, source_target_pairs={{0,3},{1,9},{2,10},{3,0},{4,7},{5,13},{6,14},{7,4},{8,11},{9,1},{1... | collective-permute-start | bytes 393224 | tf_op jit(solution)/shard_map/ppermute | solution.py:89
  31.7 5.9 %collective-permute-start.11 = (bf16[256,512]{1,0:T(8,128)(2,1)S(1)}, bf16[256,512]{1,0:T(8,128)(2,1)S(1)}, u32[]{:S(2)}, u32[]{:S(2)}) collective-permute-start(bf16[256,512]{1,0:T(8,128)(2,1)S(1)} %get-tuple-element.17), channel_id=1, source_target_pairs={{0,1},{1,0},{2,3},{3,2},{4,5},{5,4},{6,7},{7,6},{8,9},{9,8},{10,11... | collective-permute-start | bytes 786440 | tf_op jit(solution)/shard_map/ppermute | solution.py:77
  37.6 1.4 %collective-permute-start.10 = (f32[256,128]{1,0:T(8,128)S(1)}, f32[256,128]{1,0:T(8,128)S(1)}, u32[]{:S(2)}, u32[]{:S(2)}) collective-permute-start(f32[256,128]{1,0:T(8,128)S(1)} %add_add_fusion.image_ref), channel_id=1, source_target_pairs={{0,1},{1,0},{2,3},{3,2},{4,5},{5,4},{6,7},{7,6},{8,9},{9,8},{10,11... | collective-permute-start | bytes 393224 | tf_op jit(solution)/shard_map/ppermute | solution.py:77

commit v6 on v5

--- a/solution.py
+++ b/solution.py
@@ -240,13 +240,19 @@
     rank = start_block.shape[1]
 
     masks = [0, far_mask] + [mask for mask in reversed(range(1, chips)) if mask != far_mask]
-    blocks = list(pl.pallas_call(
-        functools.partial(split_kernel, masks),
-        out_shape=[pltpu.VMEM((row_count, chip_columns), bf16)] * chips,
-        in_specs=[pl.BlockSpec(memory_space=pl.ANY)],
-        out_specs=vmem_specs(chips),
-        scratch_shapes=[pltpu.SemaphoreType.DMA((chips,))],
-    )(tensor))
+    def split(source, some):
+        return pl.pallas_call(
+            functools.partial(split_kernel, some),
+            out_shape=[pltpu.VMEM((row_count, chip_columns), bf16)] * len(some),
+            in_specs=[pl.BlockSpec(memory_space=pl.ANY)],
+            out_specs=vmem_specs(len(some)),
+            scratch_shapes=[pltpu.SemaphoreType.DMA((len(some),))],
+        )(source)
+
+    (far,) = split(tensor, [far_mask])
+    far, tensor = lax.optimization_barrier((far, tensor))
+    rest = split(tensor, [mask for mask in masks if mask != far_mask])
+    blocks = [rest[0], far, *rest[1:]]
     for place in range(1, chips):
         blocks[place] = in_chips(blocks[place], masks[place])
 

time: 43.8 us -> 43.5 us (level)
  starting transfers between devices: 14.5 us -> 13.2 us
  Pallas kernels: 6.68 us -> 7.47 us
    ppermute x6, starting transfers between devices: 8.11 us -> 6.85 us  [exchange(): return lax.ppermute(value, ('slab', 'mode'), pairs)]
    pallas_call x1 -> x2, Pallas kernels: 1.18 us -> 1.98 us  [split(): pl.pallas_call(functools.partial(split_kernel, some), out_shape=[pltpu.VM...]
    ppermute x6, waiting for transfers between devices: 9.56 us -> 9.04 us  [exchange(): return lax.ppermute(value, ('slab', 'mode'), pairs)]
    ppermute x3, waiting for transfers between devices: 9.25 us -> 9.77 us  [in_chips(): lax.ppermute(value, 'mode', [(i, i ^ flipped) for i in range(lax.axis_siz...]
  transfers between devices with their start and end apart: 12 -> 12, of which waited for: 8 -> 9; matrix products, arithmetic and copies ran while one was open for 0% -> 0% of each run, Pallas kernels for 0% -> 2%
where the time goes in v6:
time: 43.5 us; the launch traced here: 43.4 us
  waiting for transfers between devices  21.9 us (50%)
  starting transfers between devices  13.2 us (30%)
  Pallas kernels  7.47 us (17%)
  between operations  0.7 us (2%)
    ppermute x3, waiting for transfers between devices, in_chips(): lax.ppermute(value, 'mode', [(i, i ^ flipped) for i in range(lax.axis_siz...  9.77 us
    ppermute x6, waiting for transfers between devices, exchange(): return lax.ppermute(value, ('slab', 'mode'), pairs)  9.04 us
    ppermute x6, starting transfers between devices, exchange(): return lax.ppermute(value, ('slab', 'mode'), pairs)  6.85 us
    ppermute x3, starting transfers between devices, in_chips(): lax.ppermute(value, 'mode', [(i, i ^ flipped) for i in range(lax.axis_siz...  4.98 us
    pallas_call x1, Pallas kernels, shards(): pl.pallas_call(outputs_kernel, out_shape=(jax.ShapeDtypeStruct((row_count...  4.64 us
    ppermute x3, waiting for transfers between devices, swap_cores(): lax.ppermute(value, 'mode', [(i, i ^ 1) for i in range(lax.axis_size('mod...  3.13 us
    pallas_call x2, Pallas kernels, split(): pl.pallas_call(functools.partial(split_kernel, some), out_shape=[pltpu.VM...  1.98 us
    ppermute x3, starting transfers between devices, swap_cores(): lax.ppermute(value, 'mode', [(i, i ^ 1) for i in range(lax.axis_size('mod...  1.39 us
  transfers between devices with their start and end apart: 12, of which 9 were waited for; matrix products, arithmetic and copies ran while one was open for 0% of the time, Pallas kernels for 2%

profile of v6, /device:TPU:0, one launch (start us, length us, event | category | flops | bytes accessed | tf_op | source)
XLA Modules:
  0.0 43.4 jit_solution(14192542950726093832)
XLA Ops:
  0.6 0.9 %shard_map.41 = bf16[64,1024]{1,0:T(8,128)(2,1)S(1)} custom-call(bf16[64,4096]{1,0:T(8,128)(2,1)} %tensor_ref.2), custom_call_target="tpu_custom_call" | custom-call | tf_op jit(solution)/shard_map/pallas_call | solution.py:244
  1.6 4.1 %collective-permute-start = (bf16[64,1024]{1,0:T(8,128)(2,1)S(1)}, bf16[64,1024]{1,0:T(8,128)(2,1)S(1)}, u32[]{:S(2)}, u32[]{:S(2)}) collective-permute-start(bf16[64,1024]{1,0:T(8,128)(2,1)S(1)} %shard_map.41), channel_id=1, source_target_pairs={{0,4},{1,5},{2,6},{3,7},{4,0},{5,1},{6,2},{7,3},{8,12},{9,13},{10,... | collective-permute-start | bytes 393224 | tf_op jit(solution)/shard_map/ppermute | solution.py:227
  5.7 1.1 %shard_map.42 = (bf16[64,1024]{1,0:T(8,128)(2,1)S(1)}, bf16[64,1024]{1,0:T(8,128)(2,1)S(1)}, bf16[64,1024]{1,0:T(8,128)(2,1)S(1)}) custom-call(bf16[64,4096]{1,0:T(8,128)(2,1)} %tensor_ref.2), custom_call_target="tpu_custom_call" | custom-call | tf_op jit(solution)/shard_map/pallas_call | solution.py:244
  6.7 0.6 %collective-permute-start.1 = (bf16[64,1024]{1,0:T(8,128)(2,1)S(1)}, bf16[64,1024]{1,0:T(8,128)(2,1)S(1)}, u32[]{:S(2)}, u32[]{:S(2)}) collective-permute-start(bf16[64,1024]{1,0:T(8,128)(2,1)S(1)} %get-tuple-element.14), channel_id=1, source_target_pairs={{0,7},{1,6},{2,5},{3,4},{4,3},{5,2},{6,1},{7,0},{8,15},{9,14},{10,... | collective-permute-start | bytes 393224 | tf_op jit(solution)/shard_map/ppermute | solution.py:227
  7.3 0.3 collective-permute-start.2
  7.6 8.0 %collective-permute-done.refs_1_ = bf16[64,1024]{1,0:T(8,128)(2,1)S(1)} collective-permute-done((bf16[64,1024]{1,0:T(8,128)(2,1)S(1)}, bf16[64,1024]{1,0:T(8,128)(2,1)S(1)}, u32[]{:S(2)}, u32[]{:S(2)}) %collective-permute-start) | collective-permute-done | bytes 131104 | tf_op jit(solution)/shard_map/ppermute | solution.py:227
  15.6 1.8 %collective-permute-done.2.refs_3_ = bf16[64,1024]{1,0:T(8,128)(2,1)S(1)} collective-permute-done((bf16[64,1024]{1,0:T(8,128)(2,1)S(1)}, bf16[64,1024]{1,0:T(8,128)(2,1)S(1)}, u32[]{:S(2)}, u32[]{:S(2)}) %collective-permute-start.2) | collective-permute-done | bytes 131104 | tf_op jit(solution)/shard_map/ppermute | solution.py:227
  17.4 0.4 shard_map.43
  17.8 0.2 collective-permute-start.3
  18.0 1.8 %collective-permute-done.3.other_ref = f32[128,1024]{1,0:T(8,128)S(1)} collective-permute-done((f32[128,1024]{1,0:T(8,128)S(1)}, f32[128,1024]{1,0:T(8,128)S(1)}, u32[]{:S(2)}, u32[]{:S(2)}) %collective-permute-start.3) | collective-permute-done | bytes 524320 | tf_op jit(solution)/shard_map/ppermute | solution.py:77
  19.8 0.4 %shard_map.44 = f32[256,128]{1,0:T(8,128)S(1)} custom-call(bf16[256,1024]{1,0:T(8,128)(2,1)S(1)} %get-tuple-element.16.held_ref, f32[128,1024]{1,0:T(8,128)S(1)} %get-tuple-element.17.own_ref, f32[128,1024]{1,0:T(8,128)S(1)} %collective-permute-done.3.other_ref), custom_call_target="tpu_custom_call" | custom-call | tf_op jit(solution)/shard_map/pallas_call | solution.py:273
  20.2 2.4 %collective-permute-start.6 = (f32[256,128]{1,0:T(8,128)S(1)}, f32[256,128]{1,0:T(8,128)S(1)}, u32[]{:S(2)}, u32[]{:S(2)}) collective-permute-start(f32[256,128]{1,0:T(8,128)S(1)} %shard_map.44), channel_id=1, source_target_pairs={{0,24},{1,5},{2,6},{3,27},{4,28},{5,1},{6,2},{7,31},{8,16},{9,13},... | collective-permute-start | bytes 393224 | tf_op jit(solution)/shard_map/ppermute | solution.py:89
  22.7 0.5 %collective-permute-start.5 = (f32[256,128]{1,0:T(8,128)S(1)}, f32[256,128]{1,0:T(8,128)S(1)}, u32[]{:S(2)}, u32[]{:S(2)}) collective-permute-start(f32[256,128]{1,0:T(8,128)S(1)} %shard_map.44), channel_id=1, source_target_pairs={{0,16},{1,6},{2,5},{3,19},{4,20},{5,2},{6,1},{7,23},{8,24},{9,14},... | collective-permute-start | bytes 393224 | tf_op jit(solution)/shard_map/ppermute | solution.py:89
  23.2 0.6 %collective-permute-start.4 = (f32[256,128]{1,0:T(8,128)S(1)}, f32[256,128]{1,0:T(8,128)S(1)}, u32[]{:S(2)}, u32[]{:S(2)}) collective-permute-start(f32[256,128]{1,0:T(8,128)S(1)} %shard_map.44), channel_id=1, source_target_pairs={{0,8},{1,2},{2,1},{3,11},{4,12},{5,6},{6,5},{7,15},{8,0},{9,10},{1... | collective-permute-start | bytes 393224 | tf_op jit(solution)/shard_map/ppermute | solution.py:89
  23.8 2.4 %collective-permute-done.6 = f32[256,128]{1,0:T(8,128)S(1)} collective-permute-done((f32[256,128]{1,0:T(8,128)S(1)}, f32[256,128]{1,0:T(8,128)S(1)}, u32[]{:S(2)}, u32[]{:S(2)}) %collective-permute-start.6) | collective-permute-done | bytes 131104 | tf_op jit(solution)/shard_map/ppermute | solution.py:89
  26.2 1.5 %collective-permute-done.5 = f32[256,128]{1,0:T(8,128)S(1)} collective-permute-done((f32[256,128]{1,0:T(8,128)S(1)}, f32[256,128]{1,0:T(8,128)S(1)}, u32[]{:S(2)}, u32[]{:S(2)}) %collective-permute-start.5) | collective-permute-done | bytes 131104 | tf_op jit(solution)/shard_map/ppermute | solution.py:89
  27.6 0.5 %collective-permute-done.4 = f32[256,128]{1,0:T(8,128)S(1)} collective-permute-done((f32[256,128]{1,0:T(8,128)S(1)}, f32[256,128]{1,0:T(8,128)S(1)}, u32[]{:S(2)}, u32[]{:S(2)}) %collective-permute-start.4) | collective-permute-done | bytes 131104 | tf_op jit(solution)/shard_map/ppermute | solution.py:89
  28.2 2.9 %collective-permute-start.9 = (f32[256,128]{1,0:T(8,128)S(1)}, f32[256,128]{1,0:T(8,128)S(1)}, u32[]{:S(2)}, u32[]{:S(2)}) collective-permute-start(f32[256,128]{1,0:T(8,128)S(1)} %add_add_fusion.1), channel_id=1, source_target_pairs={{0,4},{1,25},{2,26},{3,7},{4,0},{5,29},{6,30},{7,3},{8,12},{9,17},... | collective-permute-start | bytes 393224 | tf_op jit(solution)/shard_map/ppermute | solution.py:89
  31.1 0.4 collective-permute-start.7
  31.5 1.1 %collective-permute-start.11 = (bf16[256,512]{1,0:T(8,128)(2,1)S(1)}, bf16[256,512]{1,0:T(8,128)(2,1)S(1)}, u32[]{:S(2)}, u32[]{:S(2)}) collective-permute-start(bf16[256,512]{1,0:T(8,128)(2,1)S(1)} %get-tuple-element.19), channel_id=1, source_target_pairs={{0,1},{1,0},{2,3},{3,2},{4,5},{5,4},{6,7},{7,6},{8,9},{9,8},{10,11... | collective-permute-start | bytes 786440 | tf_op jit(solution)/shard_map/ppermute | solution.py:77
  32.6 1.7 %collective-permute-done.9 = f32[256,128]{1,0:T(8,128)S(1)} collective-permute-done((f32[256,128]{1,0:T(8,128)S(1)}, f32[256,128]{1,0:T(8,128)S(1)}, u32[]{:S(2)}, u32[]{:S(2)}) %collective-permute-start.9) | collective-permute-done | bytes 131104 | tf_op jit(solution)/shard_map/ppermute | solution.py:89
  34.3 3.0 %collective-permute-done.8 = f32[256,128]{1,0:T(8,128)S(1)} collective-permute-done((f32[256,128]{1,0:T(8,128)S(1)}, f32[256,128]{1,0:T(8,128)S(1)}, u32[]{:S(2)}, u32[]{:S(2)}) %collective-permute-start.8) | collective-permute-done | bytes 131104 | tf_op jit(solution)/shard_map/ppermute | solution.py:89
  37.4 1.3 %collective-permute-done.10.image_other_ref = f32[256,128]{1,0:T(8,128)S(1)} collective-permute-done((f32[256,128]{1,0:T(8,128)S(1)}, f32[256,128]{1,0:T(8,128)S(1)}, u32[]{:S(2)}, u32[]{:S(2)}) %collective-permute-start.10) | collective-permute-done | bytes 131104 | tf_op jit(solution)/shard_map/ppermute | solution.py:77
  38.8 4.6 %shard_map.45 = (f32[64,128]{1,0:T(8,128)}, f32[512,128]{1,0:T(8,128)}) custom-call(f32[256,128]{1,0:T(8,128)S(1)} %add_add_fusion.image_ref, f32[256,128]{1,0:T(8,128)S(1)} %collective-permute-done.10.image_other_ref, bf16[256,512]{1,0:T(8,128)(2,1)S(1)} %get-tuple-element.18.own_ref, bf16[256,512]{1,0:T(8,128)(2,1)S(1)} %collective-permute-done.11.other_ref), custom_call_target="tpu_custom_call" | custom-call | tf_op jit(solution)/shard_map/pallas_call | solution.py:282
  (9 shorter events, 0.1 us)
Async XLA Ops:
  1.6 15.8 %copy-start = (f32[512,128]{1,0:T(8,128)S(1)}, f32[512,128]{1,0:T(8,128)}, u32[]{:S(2)}) copy-start(f32[512,128]{1,0:T(8,128)} %start_ref.1) | copy-start | bytes 786436
  1.6 14.0 %collective-permute-start = (bf16[64,1024]{1,0:T(8,128)(2,1)S(1)}, bf16[64,1024]{1,0:T(8,128)(2,1)S(1)}, u32[]{:S(2)}, u32[]{:S(2)}) collective-permute-start(bf16[64,1024]{1,0:T(8,128)(2,1)S(1)} %shard_map.41), channel_id=1, source_target_pairs={{0,4},{1,5},{2,6},{3,7},{4,0},{5,1},{6,2},{7,3},{8,12},{9,13},{10,... | collective-permute-start | bytes 393224 | tf_op jit(solution)/shard_map/ppermute | solution.py:227
  6.7 8.9 %collective-permute-start.1 = (bf16[64,1024]{1,0:T(8,128)(2,1)S(1)}, bf16[64,1024]{1,0:T(8,128)(2,1)S(1)}, u32[]{:S(2)}, u32[]{:S(2)}) collective-permute-start(bf16[64,1024]{1,0:T(8,128)(2,1)S(1)} %get-tuple-element.14), channel_id=1, source_target_pairs={{0,7},{1,6},{2,5},{3,4},{4,3},{5,2},{6,1},{7,0},{8,15},{9,14},{10,... | collective-permute-start | bytes 393224 | tf_op jit(solution)/shard_map/ppermute | solution.py:227
  7.3 10.1 %collective-permute-start.2 = (bf16[64,1024]{1,0:T(8,128)(2,1)S(1)}, bf16[64,1024]{1,0:T(8,128)(2,1)S(1)}, u32[]{:S(2)}, u32[]{:S(2)}) collective-permute-start(bf16[64,1024]{1,0:T(8,128)(2,1)S(1)} %get-tuple-element.15), channel_id=1, source_target_pairs={{0,3},{1,2},{2,1},{3,0},{4,7},{5,6},{6,5},{7,4},{8,11},{9,10},{10,... | collective-permute-start | bytes 393224 | tf_op jit(solution)/shard_map/ppermute | solution.py:227
  17.8 2.0 %collective-permute-start.3 = (f32[128,1024]{1,0:T(8,128)S(1)}, f32[128,1024]{1,0:T(8,128)S(1)}, u32[]{:S(2)}, u32[]{:S(2)}) collective-permute-start(f32[128,1024]{1,0:T(8,128)S(1)} %get-tuple-element.17.own_ref), channel_id=1, source_target_pairs={{0,1},{1,0},{2,3},{3,2},{4,5},{5,4},{6,7},{7,6},{8,9},{9,8},{10,11... | collective-permute-start | bytes 1572872 | tf_op jit(solution)/shard_map/ppermute | solution.py:77
  20.2 5.9 %collective-permute-start.6 = (f32[256,128]{1,0:T(8,128)S(1)}, f32[256,128]{1,0:T(8,128)S(1)}, u32[]{:S(2)}, u32[]{:S(2)}) collective-permute-start(f32[256,128]{1,0:T(8,128)S(1)} %shard_map.44), channel_id=1, source_target_pairs={{0,24},{1,5},{2,6},{3,27},{4,28},{5,1},{6,2},{7,31},{8,16},{9,13},... | collective-permute-start | bytes 393224 | tf_op jit(solution)/shard_map/ppermute | solution.py:89
  22.7 5.0 %collective-permute-start.5 = (f32[256,128]{1,0:T(8,128)S(1)}, f32[256,128]{1,0:T(8,128)S(1)}, u32[]{:S(2)}, u32[]{:S(2)}) collective-permute-start(f32[256,128]{1,0:T(8,128)S(1)} %shard_map.44), channel_id=1, source_target_pairs={{0,16},{1,6},{2,5},{3,19},{4,20},{5,2},{6,1},{7,23},{8,24},{9,14},... | collective-permute-start | bytes 393224 | tf_op jit(solution)/shard_map/ppermute | solution.py:89
  23.2 5.0 %collective-permute-start.4 = (f32[256,128]{1,0:T(8,128)S(1)}, f32[256,128]{1,0:T(8,128)S(1)}, u32[]{:S(2)}, u32[]{:S(2)}) collective-permute-start(f32[256,128]{1,0:T(8,128)S(1)} %shard_map.44), channel_id=1, source_target_pairs={{0,8},{1,2},{2,1},{3,11},{4,12},{5,6},{6,5},{7,15},{8,0},{9,10},{1... | collective-permute-start | bytes 393224 | tf_op jit(solution)/shard_map/ppermute | solution.py:89
  28.2 6.1 %collective-permute-start.9 = (f32[256,128]{1,0:T(8,128)S(1)}, f32[256,128]{1,0:T(8,128)S(1)}, u32[]{:S(2)}, u32[]{:S(2)}) collective-permute-start(f32[256,128]{1,0:T(8,128)S(1)} %add_add_fusion.1), channel_id=1, source_target_pairs={{0,4},{1,25},{2,26},{3,7},{4,0},{5,29},{6,30},{7,3},{8,12},{9,17},... | collective-permute-start | bytes 393224 | tf_op jit(solution)/shard_map/ppermute | solution.py:89
  31.1 6.2 %collective-permute-start.8 = (f32[256,128]{1,0:T(8,128)S(1)}, f32[256,128]{1,0:T(8,128)S(1)}, u32[]{:S(2)}, u32[]{:S(2)}) collective-permute-start(f32[256,128]{1,0:T(8,128)S(1)} %add_add_fusion.1), channel_id=1, source_target_pairs={{0,7},{1,17},{2,18},{3,4},{4,3},{5,21},{6,22},{7,0},{8,15},{9,25},... | collective-permute-start | bytes 393224 | tf_op jit(solution)/shard_map/ppermute | solution.py:89
  31.1 6.2 %collective-permute-start.7 = (f32[256,128]{1,0:T(8,128)S(1)}, f32[256,128]{1,0:T(8,128)S(1)}, u32[]{:S(2)}, u32[]{:S(2)}) collective-permute-start(f32[256,128]{1,0:T(8,128)S(1)} %add_add_fusion.1), channel_id=1, source_target_pairs={{0,3},{1,9},{2,10},{3,0},{4,7},{5,13},{6,14},{7,4},{8,11},{9,1},{1... | collective-permute-start | bytes 393224 | tf_op jit(solution)/shard_map/ppermute | solution.py:89
  31.5 5.9 %collective-permute-start.11 = (bf16[256,512]{1,0:T(8,128)(2,1)S(1)}, bf16[256,512]{1,0:T(8,128)(2,1)S(1)}, u32[]{:S(2)}, u32[]{:S(2)}) collective-permute-start(bf16[256,512]{1,0:T(8,128)(2,1)S(1)} %get-tuple-element.19), channel_id=1, source_target_pairs={{0,1},{1,0},{2,3},{3,2},{4,5},{5,4},{6,7},{7,6},{8,9},{9,8},{10,11... | collective-permute-start | bytes 786440 | tf_op jit(solution)/shard_map/ppermute | solution.py:77
  37.3 1.4 %collective-permute-start.10 = (f32[256,128]{1,0:T(8,128)S(1)}, f32[256,128]{1,0:T(8,128)S(1)}, u32[]{:S(2)}, u32[]{:S(2)}) collective-permute-start(f32[256,128]{1,0:T(8,128)S(1)} %add_add_fusion.image_ref), channel_id=1, source_target_pairs={{0,1},{1,0},{2,3},{3,2},{4,5},{5,4},{6,7},{7,6},{8,9},{9,8},{10,11... | collective-permute-start | bytes 393224 | tf_op jit(solution)/shard_map/ppermute | solution.py:77

commit v7 on v6

--- a/solution.py
+++ b/solution.py
@@ -48,7 +48,7 @@
 
 
 def inner_kernel(masks, start_ref, *refs):
-    blocks, (inner_ref, held_ref, own_ref, away_ref) = refs[: len(masks)], refs[len(masks) :]
+    blocks, (inner_ref, inner_low_ref, held_ref, own_ref, away_ref) = refs[: len(masks)], refs[len(masks) :]
     mode_index = lax.axis_index("mode")
     chip, core = mode_index // 2, mode_index % 2
     rows, width = blocks[0].shape
@@ -64,13 +64,16 @@
         starts.append(start_ref[pl.ds(first, rows), :])
     ordered = jnp.concatenate([block[...] for block in blocks], axis=0)
     high, low = two_parts(jnp.concatenate(starts, axis=0))
-    inner_ref[...] = dot(high, ordered, contract_rows) + dot(low, ordered, contract_rows)
+    inner = dot(high, ordered, contract_rows) + dot(low, ordered, contract_rows)
+    inner_ref[...] = inner
+    inner_low_ref[...] = inner.astype(bf16)
 
 
 def image_kernel(held_ref, own_ref, other_ref, image_ref):
-    high, low = two_parts(own_ref[...] + other_ref[...])
+    high, low = two_parts(own_ref[...] + other_ref[...].astype(f32))
     held = held_ref[...]
-    image_ref[...] = dot(held, high, contract_last) + dot(held, low, contract_last)
+    image = dot(held, high, contract_last) + dot(held, low, contract_last)
+    image_ref[...] = image.astype(image_ref.dtype)
 
 
 def swap_cores(value):
@@ -102,12 +105,12 @@
     while len(even) >= 2:
         (a, b), (c, d) = even[:2], odd[:2]
         even, odd = even[2:], odd[2:]
-        far = exchange(value, both(a, b), both(c, d))
-        near = exchange(value, a, c)
-        side = exchange(value, b, d)
-        value = (value + near) + (side + far)
+        far = exchange(value, both(a, b), both(c, d)).astype(f32)
+        near = exchange(value, a, c).astype(f32)
+        side = exchange(value, b, d).astype(f32)
+        value = (value.astype(f32) + near) + (side + far)
     if even:
-        value = value + exchange(value, even[0], odd[0])
+        value = value.astype(f32) + exchange(value, even[0], odd[0]).astype(f32)
     return value
 
 
@@ -198,27 +201,36 @@
     )
 
 
-def outputs_kernel(image_ref, image_other_ref, own_ref, other_ref, basis_ref, core_ref, basis_own_ref):
+def gram_of(rows):
+    return lax.dot_general(
+        rows, rows, contract_rows, precision=highest, preferred_element_type=f32
+    )
+
+
+def gram_kernel(image_ref, gram_ref):
+    gram_ref[...] = gram_of(image_ref[...])
+
+
+def outputs_kernel(
+    gram_ref, image_ref, image_other_ref, own_ref, other_ref, basis_ref, core_ref, basis_own_ref
+):
     mode_index = lax.axis_index("mode")
-    first = mode_index % 2 == mode_index // 2 % 2
-    image, image_other = image_ref[...], image_other_ref[...]
-    image_block = jnp.concatenate(
-        [jnp.where(first, image, image_other), jnp.where(first, image_other, image)], axis=0
-    )
-    small_gram = lax.dot_general(
-        image_block, image_block, contract_rows, precision=highest, preferred_element_type=f32
-    )
-    inverse = inverse_factor(small_gram)
-    basis_own, basis_other = [
-        lax.dot_general(part, inverse, contract_last, precision=highest, preferred_element_type=f32)
-        for part in (image, image_other)
-    ]
+    image_other = image_other_ref[...]
+    inverse = inverse_factor(gram_ref[...] + gram_of(image_other))
+    inverse_high, inverse_low = two_parts(inverse)
+
+    def basis_of(image):
+        high, low = two_parts(image)
+        small = dot(high, inverse_low, contract_last) + dot(low, inverse_high, contract_last)
+        return dot(high, inverse_high, contract_last) + small
+
+    basis_own = basis_of(image_ref[...])
     basis_own_ref[...] = basis_own
     rows = basis_ref.shape[0]
     place = pl.multiple_of(mode_index // 2 * rows, rows)
     basis_ref[...] = basis_own_ref[pl.ds(place, rows), :]
     core_ref[...] = dot(own_ref[...], basis_own.astype(bf16), contract_rows) + dot(
-        other_ref[...], basis_other.astype(bf16), contract_rows
+        other_ref[...], basis_of(image_other).astype(bf16), contract_rows
     )
 
 
@@ -256,28 +268,35 @@
     for place in range(1, chips):
         blocks[place] = in_chips(blocks[place], masks[place])
 
-    inner, held, own_half, away_half = pl.pallas_call(
+    inner, inner_low, held, own_half, away_half = pl.pallas_call(
         functools.partial(inner_kernel, masks),
         out_shape=(
             pltpu.VMEM((rank, chip_columns), f32),
+            pltpu.VMEM((rank, chip_columns), bf16),
             pltpu.VMEM((held_rows, chip_columns), bf16),
             pltpu.VMEM((held_rows, own_columns), bf16),
             pltpu.VMEM((held_rows, own_columns), bf16),
         ),
         in_specs=vmem_specs(1 + chips),
-        out_specs=tuple(vmem_specs(4)),
+        out_specs=tuple(vmem_specs(5)),
     )(*in_vmem(start_block, *blocks))
-    inner_other = swap_cores(inner)
+    inner_other = swap_cores(inner_low)
     other_half = swap_cores(away_half)
 
     image = pl.pallas_call(
         image_kernel,
-        out_shape=pltpu.VMEM((held_rows, rank), f32),
+        out_shape=pltpu.VMEM((held_rows, rank), bf16),
         in_specs=vmem_specs(3),
         out_specs=vmem_specs(1)[0],
     )(*in_vmem(held, inner, inner_other))
     image = sum_over_chips(image)
     image_other = swap_cores(image)
+    gram = pl.pallas_call(
+        gram_kernel,
+        out_shape=pltpu.VMEM((rank, rank), f32),
+        in_specs=vmem_specs(1),
+        out_specs=vmem_specs(1)[0],
+    )(*in_vmem(image))
 
     return pl.pallas_call(
         outputs_kernel,
@@ -285,10 +304,10 @@
             jax.ShapeDtypeStruct((row_count, rank), f32),
             jax.ShapeDtypeStruct((own_columns, rank), f32),
         ),
-        in_specs=vmem_specs(4),
+        in_specs=vmem_specs(5),
         out_specs=tuple(vmem_specs(2)),
         scratch_shapes=[pltpu.VMEM((held_rows, rank), f32)],
-    )(*in_vmem(image, image_other, own_half, other_half))
+    )(*in_vmem(gram, image, image_other, own_half, other_half))
 
 
 def solution(mesh):

time: 43.5 us -> 42.3 us (0.972)
  starting transfers between devices: 13.2 us -> 12.5 us
  waiting for transfers between devices: 21.9 us -> 21.2 us
    ppermute x3, starting transfers between devices: 1.39 us -> 0.69 us  [swap_cores(): lax.ppermute(value, 'mode', [(i, i ^ 1) for i in range(lax.axis_size('mod...]
    ppermute x3, waiting for transfers between devices: 3.13 us -> 2.43 us  [swap_cores(): lax.ppermute(value, 'mode', [(i, i ^ 1) for i in range(lax.axis_size('mod...]
  transfers between devices with their start and end apart: 12 -> 12, of which waited for: 9 -> 9; matrix products, arithmetic and copies ran while one was open for 0% -> 0% of each run, Pallas kernels for 2% -> 3%
where the time goes in v7:
time: 42.3 us; the launch traced here: 42.2 us
  waiting for transfers between devices  21.2 us (50%)
  starting transfers between devices  12.5 us (30%)
  Pallas kernels  7.63 us (18%)
  between operations  0.71 us (2%)
    ppermute x3, waiting for transfers between devices, in_chips(): lax.ppermute(value, 'mode', [(i, i ^ flipped) for i in range(lax.axis_siz...  9.77 us
    ppermute x6, waiting for transfers between devices, exchange(): return lax.ppermute(value, ('slab', 'mode'), pairs)  9.05 us
    ppermute x6, starting transfers between devices, exchange(): return lax.ppermute(value, ('slab', 'mode'), pairs)  6.85 us
    ppermute x3, starting transfers between devices, in_chips(): lax.ppermute(value, 'mode', [(i, i ^ flipped) for i in range(lax.axis_siz...  4.98 us
    pallas_call x1, Pallas kernels, shards(): pl.pallas_call(outputs_kernel, out_shape=(jax.ShapeDtypeStruct((row_count...  4.47 us
    ppermute x3, waiting for transfers between devices, swap_cores(): lax.ppermute(value, 'mode', [(i, i ^ 1) for i in range(lax.axis_size('mod...  2.43 us
    pallas_call x2, Pallas kernels, split(): pl.pallas_call(functools.partial(split_kernel, some), out_shape=[pltpu.VM...  1.98 us
  transfers between devices with their start and end apart: 12, of which 9 were waited for; matrix products, arithmetic and copies ran while one was open for 0% of the time, Pallas kernels for 3%

profile of v7, /device:TPU:0, one launch (start us, length us, event | category | flops | bytes accessed | tf_op | source)
XLA Modules:
  0.0 42.2 jit_solution(14628774783194016000)
XLA Ops:
  0.6 0.9 %shard_map.41 = bf16[64,1024]{1,0:T(8,128)(2,1)S(1)} custom-call(bf16[64,4096]{1,0:T(8,128)(2,1)} %tensor_ref.2), custom_call_target="tpu_custom_call" | custom-call | tf_op jit(solution)/shard_map/pallas_call | solution.py:256
  1.6 4.1 %collective-permute-start = (bf16[64,1024]{1,0:T(8,128)(2,1)S(1)}, bf16[64,1024]{1,0:T(8,128)(2,1)S(1)}, u32[]{:S(2)}, u32[]{:S(2)}) collective-permute-start(bf16[64,1024]{1,0:T(8,128)(2,1)S(1)} %shard_map.41), channel_id=1, source_target_pairs={{0,4},{1,5},{2,6},{3,7},{4,0},{5,1},{6,2},{7,3},{8,12},{9,13},{10,... | collective-permute-start | bytes 393224 | tf_op jit(solution)/shard_map/ppermute | solution.py:239
  5.7 1.1 %shard_map.42 = (bf16[64,1024]{1,0:T(8,128)(2,1)S(1)}, bf16[64,1024]{1,0:T(8,128)(2,1)S(1)}, bf16[64,1024]{1,0:T(8,128)(2,1)S(1)}) custom-call(bf16[64,4096]{1,0:T(8,128)(2,1)} %tensor_ref.2), custom_call_target="tpu_custom_call" | custom-call | tf_op jit(solution)/shard_map/pallas_call | solution.py:256
  6.7 0.6 %collective-permute-start.1 = (bf16[64,1024]{1,0:T(8,128)(2,1)S(1)}, bf16[64,1024]{1,0:T(8,128)(2,1)S(1)}, u32[]{:S(2)}, u32[]{:S(2)}) collective-permute-start(bf16[64,1024]{1,0:T(8,128)(2,1)S(1)} %get-tuple-element.15), channel_id=1, source_target_pairs={{0,7},{1,6},{2,5},{3,4},{4,3},{5,2},{6,1},{7,0},{8,15},{9,14},{10,... | collective-permute-start | bytes 393224 | tf_op jit(solution)/shard_map/ppermute | solution.py:239
  7.3 0.3 collective-permute-start.2
  7.6 8.0 %collective-permute-done.refs_1_ = bf16[64,1024]{1,0:T(8,128)(2,1)S(1)} collective-permute-done((bf16[64,1024]{1,0:T(8,128)(2,1)S(1)}, bf16[64,1024]{1,0:T(8,128)(2,1)S(1)}, u32[]{:S(2)}, u32[]{:S(2)}) %collective-permute-start) | collective-permute-done | bytes 131104 | tf_op jit(solution)/shard_map/ppermute | solution.py:239
  15.6 1.8 %collective-permute-done.2.refs_3_ = bf16[64,1024]{1,0:T(8,128)(2,1)S(1)} collective-permute-done((bf16[64,1024]{1,0:T(8,128)(2,1)S(1)}, bf16[64,1024]{1,0:T(8,128)(2,1)S(1)}, u32[]{:S(2)}, u32[]{:S(2)}) %collective-permute-start.2) | collective-permute-done | bytes 131104 | tf_op jit(solution)/shard_map/ppermute | solution.py:239
  17.4 0.4 shard_map.43
  18.0 1.4 %collective-permute-done.3.other_ref = bf16[128,1024]{1,0:T(8,128)(2,1)S(1)} collective-permute-done((bf16[128,1024]{1,0:T(8,128)(2,1)S(1)}, bf16[128,1024]{1,0:T(8,128)(2,1)S(1)}, u32[]{:S(2)}, u32[]{:S(2)}) %collective-permute-start.3) | collective-permute-done | bytes 262176 | tf_op jit(solution)/shard_map/ppermute | solution.py:80
  19.4 0.5 %shard_map.44 = bf16[256,128]{1,0:T(8,128)(2,1)S(1)} custom-call(bf16[256,1024]{1,0:T(8,128)(2,1)S(1)} %get-tuple-element.17.held_ref, f32[128,1024]{1,0:T(8,128)S(1)} %get-tuple-element.18.own_ref, bf16[128,1024]{1,0:T(8,128)(2,1)S(1)} %collective-permute-done.3.other_ref), custom_call_target="tpu_custom_call" | custom-call | tf_op jit(solution)/shard_map/pallas_call | solution.py:286
  19.9 2.4 %collective-permute-start.6 = (bf16[256,128]{1,0:T(8,128)(2,1)S(1)}, bf16[256,128]{1,0:T(8,128)(2,1)S(1)}, u32[]{:S(2)}, u32[]{:S(2)}) collective-permute-start(bf16[256,128]{1,0:T(8,128)(2,1)S(1)} %shard_map.44), channel_id=1, source_target_pairs={{0,24},{1,5},{2,6},{3,27},{4,28},{5,1},{6,2},{7,31},{8,16},{9,13},... | collective-permute-start | bytes 196616 | tf_op jit(solution)/shard_map/ppermute | solution.py:92
  22.3 0.5 %collective-permute-start.5 = (bf16[256,128]{1,0:T(8,128)(2,1)S(1)}, bf16[256,128]{1,0:T(8,128)(2,1)S(1)}, u32[]{:S(2)}, u32[]{:S(2)}) collective-permute-start(bf16[256,128]{1,0:T(8,128)(2,1)S(1)} %shard_map.44), channel_id=1, source_target_pairs={{0,16},{1,6},{2,5},{3,19},{4,20},{5,2},{6,1},{7,23},{8,24},{9,14},... | collective-permute-start | bytes 196616 | tf_op jit(solution)/shard_map/ppermute | solution.py:92
  22.8 0.6 %collective-permute-start.4 = (bf16[256,128]{1,0:T(8,128)(2,1)S(1)}, bf16[256,128]{1,0:T(8,128)(2,1)S(1)}, u32[]{:S(2)}, u32[]{:S(2)}) collective-permute-start(bf16[256,128]{1,0:T(8,128)(2,1)S(1)} %shard_map.44), channel_id=1, source_target_pairs={{0,8},{1,2},{2,1},{3,11},{4,12},{5,6},{6,5},{7,15},{8,0},{9,10},{1... | collective-permute-start | bytes 196616 | tf_op jit(solution)/shard_map/ppermute | solution.py:92
  23.4 1.7 %collective-permute-done.6 = bf16[256,128]{1,0:T(8,128)(2,1)S(1)} collective-permute-done((bf16[256,128]{1,0:T(8,128)(2,1)S(1)}, bf16[256,128]{1,0:T(8,128)(2,1)S(1)}, u32[]{:S(2)}, u32[]{:S(2)}) %collective-permute-start.6) | collective-permute-done | bytes 65568 | tf_op jit(solution)/shard_map/ppermute | solution.py:92
  25.1 1.5 %collective-permute-done.5 = bf16[256,128]{1,0:T(8,128)(2,1)S(1)} collective-permute-done((bf16[256,128]{1,0:T(8,128)(2,1)S(1)}, bf16[256,128]{1,0:T(8,128)(2,1)S(1)}, u32[]{:S(2)}, u32[]{:S(2)}) %collective-permute-start.5) | collective-permute-done | bytes 65568 | tf_op jit(solution)/shard_map/ppermute | solution.py:92
  26.6 0.5 %collective-permute-done.4 = bf16[256,128]{1,0:T(8,128)(2,1)S(1)} collective-permute-done((bf16[256,128]{1,0:T(8,128)(2,1)S(1)}, bf16[256,128]{1,0:T(8,128)(2,1)S(1)}, u32[]{:S(2)}, u32[]{:S(2)}) %collective-permute-start.4) | collective-permute-done | bytes 65568 | tf_op jit(solution)/shard_map/ppermute | solution.py:92
  27.1 2.9 %collective-permute-start.9 = (f32[256,128]{1,0:T(8,128)S(1)}, f32[256,128]{1,0:T(8,128)S(1)}, u32[]{:S(2)}, u32[]{:S(2)}) collective-permute-start(f32[256,128]{1,0:T(8,128)S(1)} %add_add_fusion.1), channel_id=1, source_target_pairs={{0,4},{1,25},{2,26},{3,7},{4,0},{5,29},{6,30},{7,3},{8,12},{9,17},... | collective-permute-start | bytes 393224 | tf_op jit(solution)/shard_map/ppermute | solution.py:92
  30.1 0.4 collective-permute-start.7
  30.4 0.4 %collective-permute-start.11 = (bf16[256,512]{1,0:T(8,128)(2,1)S(1)}, bf16[256,512]{1,0:T(8,128)(2,1)S(1)}, u32[]{:S(2)}, u32[]{:S(2)}) collective-permute-start(bf16[256,512]{1,0:T(8,128)(2,1)S(1)} %get-tuple-element.21), channel_id=1, source_target_pairs={{0,1},{1,0},{2,3},{3,2},{4,5},{5,4},{6,7},{7,6},{8,9},{9,8},{10,11... | collective-permute-start | bytes 786440 | tf_op jit(solution)/shard_map/ppermute | solution.py:80
  30.9 2.4 %collective-permute-done.9 = f32[256,128]{1,0:T(8,128)S(1)} collective-permute-done((f32[256,128]{1,0:T(8,128)S(1)}, f32[256,128]{1,0:T(8,128)S(1)}, u32[]{:S(2)}, u32[]{:S(2)}) %collective-permute-start.9) | collective-permute-done | bytes 131104 | tf_op jit(solution)/shard_map/ppermute | solution.py:92
  33.2 3.0 %collective-permute-done.8 = f32[256,128]{1,0:T(8,128)S(1)} collective-permute-done((f32[256,128]{1,0:T(8,128)S(1)}, f32[256,128]{1,0:T(8,128)S(1)}, u32[]{:S(2)}, u32[]{:S(2)}) %collective-permute-start.8) | collective-permute-done | bytes 131104 | tf_op jit(solution)/shard_map/ppermute | solution.py:92
  36.4 0.3 shard_map.45.gram_ref
  36.7 1.0 %collective-permute-done.10.image_other_ref = f32[256,128]{1,0:T(8,128)S(1)} collective-permute-done((f32[256,128]{1,0:T(8,128)S(1)}, f32[256,128]{1,0:T(8,128)S(1)}, u32[]{:S(2)}, u32[]{:S(2)}) %collective-permute-start.10) | collective-permute-done | bytes 131104 | tf_op jit(solution)/shard_map/ppermute | solution.py:80
  37.7 4.5 %shard_map.46 = (f32[64,128]{1,0:T(8,128)}, f32[512,128]{1,0:T(8,128)}) custom-call(f32[128,128]{1,0:T(8,128)S(1)} %shard_map.45.gram_ref, f32[256,128]{1,0:T(8,128)S(1)} %add_add_fusion.image_ref, f32[256,128]{1,0:T(8,128)S(1)} %collective-permute-done.10.image_other_ref, bf16[256,512]{1,0:T(8,128)(2,1)S(1)} %get-tuple-element.20.own_ref, ...), custom_call_target="tpu_custom_call" | custom-call | tf_op jit(solution)/shard_map/pallas_call | solution.py:301
  (10 shorter events, 0.3 us)
Async XLA Ops:
  1.6 15.8 %copy-start = (f32[512,128]{1,0:T(8,128)S(1)}, f32[512,128]{1,0:T(8,128)}, u32[]{:S(2)}) copy-start(f32[512,128]{1,0:T(8,128)} %start_ref.1) | copy-start | bytes 786436
  1.6 14.0 %collective-permute-start = (bf16[64,1024]{1,0:T(8,128)(2,1)S(1)}, bf16[64,1024]{1,0:T(8,128)(2,1)S(1)}, u32[]{:S(2)}, u32[]{:S(2)}) collective-permute-start(bf16[64,1024]{1,0:T(8,128)(2,1)S(1)} %shard_map.41), channel_id=1, source_target_pairs={{0,4},{1,5},{2,6},{3,7},{4,0},{5,1},{6,2},{7,3},{8,12},{9,13},{10,... | collective-permute-start | bytes 393224 | tf_op jit(solution)/shard_map/ppermute | solution.py:239
  6.7 8.9 %collective-permute-start.1 = (bf16[64,1024]{1,0:T(8,128)(2,1)S(1)}, bf16[64,1024]{1,0:T(8,128)(2,1)S(1)}, u32[]{:S(2)}, u32[]{:S(2)}) collective-permute-start(bf16[64,1024]{1,0:T(8,128)(2,1)S(1)} %get-tuple-element.15), channel_id=1, source_target_pairs={{0,7},{1,6},{2,5},{3,4},{4,3},{5,2},{6,1},{7,0},{8,15},{9,14},{10,... | collective-permute-start | bytes 393224 | tf_op jit(solution)/shard_map/ppermute | solution.py:239
  7.3 10.1 %collective-permute-start.2 = (bf16[64,1024]{1,0:T(8,128)(2,1)S(1)}, bf16[64,1024]{1,0:T(8,128)(2,1)S(1)}, u32[]{:S(2)}, u32[]{:S(2)}) collective-permute-start(bf16[64,1024]{1,0:T(8,128)(2,1)S(1)} %get-tuple-element.16), channel_id=1, source_target_pairs={{0,3},{1,2},{2,1},{3,0},{4,7},{5,6},{6,5},{7,4},{8,11},{9,10},{10,... | collective-permute-start | bytes 393224 | tf_op jit(solution)/shard_map/ppermute | solution.py:239
  17.8 1.6 %collective-permute-start.3 = (bf16[128,1024]{1,0:T(8,128)(2,1)S(1)}, bf16[128,1024]{1,0:T(8,128)(2,1)S(1)}, u32[]{:S(2)}, u32[]{:S(2)}) collective-permute-start(bf16[128,1024]{1,0:T(8,128)(2,1)S(1)} %get-tuple-element.19), channel_id=1, source_target_pairs={{0,1},{1,0},{2,3},{3,2},{4,5},{5,4},{6,7},{7,6},{8,9},{9,8},{10,11... | collective-permute-start | bytes 786440 | tf_op jit(solution)/shard_map/ppermute | solution.py:80
  19.9 5.2 %collective-permute-start.6 = (bf16[256,128]{1,0:T(8,128)(2,1)S(1)}, bf16[256,128]{1,0:T(8,128)(2,1)S(1)}, u32[]{:S(2)}, u32[]{:S(2)}) collective-permute-start(bf16[256,128]{1,0:T(8,128)(2,1)S(1)} %shard_map.44), channel_id=1, source_target_pairs={{0,24},{1,5},{2,6},{3,27},{4,28},{5,1},{6,2},{7,31},{8,16},{9,13},... | collective-permute-start | bytes 196616 | tf_op jit(solution)/shard_map/ppermute | solution.py:92
  22.3 4.3 %collective-permute-start.5 = (bf16[256,128]{1,0:T(8,128)(2,1)S(1)}, bf16[256,128]{1,0:T(8,128)(2,1)S(1)}, u32[]{:S(2)}, u32[]{:S(2)}) collective-permute-start(bf16[256,128]{1,0:T(8,128)(2,1)S(1)} %shard_map.44), channel_id=1, source_target_pairs={{0,16},{1,6},{2,5},{3,19},{4,20},{5,2},{6,1},{7,23},{8,24},{9,14},... | collective-permute-start | bytes 196616 | tf_op jit(solution)/shard_map/ppermute | solution.py:92
  22.8 4.3 %collective-permute-start.4 = (bf16[256,128]{1,0:T(8,128)(2,1)S(1)}, bf16[256,128]{1,0:T(8,128)(2,1)S(1)}, u32[]{:S(2)}, u32[]{:S(2)}) collective-permute-start(bf16[256,128]{1,0:T(8,128)(2,1)S(1)} %shard_map.44), channel_id=1, source_target_pairs={{0,8},{1,2},{2,1},{3,11},{4,12},{5,6},{6,5},{7,15},{8,0},{9,10},{1... | collective-permute-start | bytes 196616 | tf_op jit(solution)/shard_map/ppermute | solution.py:92
  27.1 6.1 %collective-permute-start.9 = (f32[256,128]{1,0:T(8,128)S(1)}, f32[256,128]{1,0:T(8,128)S(1)}, u32[]{:S(2)}, u32[]{:S(2)}) collective-permute-start(f32[256,128]{1,0:T(8,128)S(1)} %add_add_fusion.1), channel_id=1, source_target_pairs={{0,4},{1,25},{2,26},{3,7},{4,0},{5,29},{6,30},{7,3},{8,12},{9,17},... | collective-permute-start | bytes 393224 | tf_op jit(solution)/shard_map/ppermute | solution.py:92
  30.1 6.2 %collective-permute-start.8 = (f32[256,128]{1,0:T(8,128)S(1)}, f32[256,128]{1,0:T(8,128)S(1)}, u32[]{:S(2)}, u32[]{:S(2)}) collective-permute-start(f32[256,128]{1,0:T(8,128)S(1)} %add_add_fusion.1), channel_id=1, source_target_pairs={{0,7},{1,17},{2,18},{3,4},{4,3},{5,21},{6,22},{7,0},{8,15},{9,25},... | collective-permute-start | bytes 393224 | tf_op jit(solution)/shard_map/ppermute | solution.py:92
  30.1 6.2 %collective-permute-start.7 = (f32[256,128]{1,0:T(8,128)S(1)}, f32[256,128]{1,0:T(8,128)S(1)}, u32[]{:S(2)}, u32[]{:S(2)}) collective-permute-start(f32[256,128]{1,0:T(8,128)S(1)} %add_add_fusion.1), channel_id=1, source_target_pairs={{0,3},{1,9},{2,10},{3,0},{4,7},{5,13},{6,14},{7,4},{8,11},{9,1},{1... | collective-permute-start | bytes 393224 | tf_op jit(solution)/shard_map/ppermute | solution.py:92
  30.4 6.3 %collective-permute-start.11 = (bf16[256,512]{1,0:T(8,128)(2,1)S(1)}, bf16[256,512]{1,0:T(8,128)(2,1)S(1)}, u32[]{:S(2)}, u32[]{:S(2)}) collective-permute-start(bf16[256,512]{1,0:T(8,128)(2,1)S(1)} %get-tuple-element.21), channel_id=1, source_target_pairs={{0,1},{1,0},{2,3},{3,2},{4,5},{5,4},{6,7},{7,6},{8,9},{9,8},{10,11... | collective-permute-start | bytes 786440 | tf_op jit(solution)/shard_map/ppermute | solution.py:80
  36.3 1.4 %collective-permute-start.10 = (f32[256,128]{1,0:T(8,128)S(1)}, f32[256,128]{1,0:T(8,128)S(1)}, u32[]{:S(2)}, u32[]{:S(2)}) collective-permute-start(f32[256,128]{1,0:T(8,128)S(1)} %add_add_fusion.image_ref), channel_id=1, source_target_pairs={{0,1},{1,0},{2,3},{3,2},{4,5},{5,4},{6,7},{7,6},{8,9},{9,8},{10,11... | collective-permute-start | bytes 393224 | tf_op jit(solution)/shard_map/ppermute | solution.py:80

commit v8 on v7

--- a/solution.py
+++ b/solution.py
@@ -31,13 +31,19 @@
     return [pl.BlockSpec(memory_space=pltpu.VMEM)] * count
 
 
+def chosen(masks):
+    mode_index = lax.axis_index("mode")
+    half = (mode_index // 2 + mode_index) % 2
+    return masks[0] if masks[0] == masks[1] else jnp.where(half == 0, masks[0], masks[1])
+
+
 def split_kernel(masks, tensor_ref, *refs):
     blocks, semaphores = refs[:-1], refs[-1]
     width = blocks[0].shape[1]
     chip = lax.axis_index("mode") // 2
     copies = []
     for place, (mask, block) in enumerate(zip(masks, blocks)):
-        columns = pl.ds(pl.multiple_of((chip ^ mask) * width, width), width)
+        columns = pl.ds(pl.multiple_of((chip ^ chosen(mask)) * width, width), width)
         copies.append(
             pltpu.make_async_copy(tensor_ref.at[:, columns], block, semaphores.at[place])
         )
@@ -55,6 +61,7 @@
     half = width // 2
     starts = []
     for mask, block in zip(masks, blocks):
+        mask = chosen(mask)
         source = chip ^ mask
         place = pl.ds(pl.multiple_of(source * rows, rows), rows)
         held_ref[place, :] = block[...]
@@ -108,7 +115,7 @@
         far = exchange(value, both(a, b), both(c, d)).astype(f32)
         near = exchange(value, a, c).astype(f32)
         side = exchange(value, b, d).astype(f32)
-        value = (value.astype(f32) + near) + (side + far)
+        value = ((value.astype(f32) + near) + (side + far)).astype(value.dtype if len(even) else f32)
     if even:
         value = value.astype(f32) + exchange(value, even[0], odd[0]).astype(f32)
     return value
@@ -234,13 +241,6 @@
     )
 
 
-def in_chips(value, mask):
-    flipped = 2 * mask + (mask & 1)
-    return lax.ppermute(
-        value, "mode", [(i, i ^ flipped) for i in range(lax.axis_size("mode"))]
-    )
-
-
 def shards(tensor, start_block):
     row_count, slab_columns = tensor.shape
     modes = lax.axis_size("mode")
@@ -251,7 +251,10 @@
     held_rows = chips * row_count
     rank = start_block.shape[1]
 
-    masks = [0, far_mask] + [mask for mask in reversed(range(1, chips)) if mask != far_mask]
+    last_mask = chips - 1
+    masks = [(0, 0), (last_mask, far_mask), (far_mask, last_mask)]
+    masks += [(mask, mask) for mask in range(1, chips) if mask not in (far_mask, last_mask)]
+
     def split(source, some):
         return pl.pallas_call(
             functools.partial(split_kernel, some),
@@ -261,12 +264,13 @@
             scratch_shapes=[pltpu.SemaphoreType.DMA((len(some),))],
         )(source)
 
-    (far,) = split(tensor, [far_mask])
-    far, tensor = lax.optimization_barrier((far, tensor))
-    rest = split(tensor, [mask for mask in masks if mask != far_mask])
-    blocks = [rest[0], far, *rest[1:]]
+    (first,) = split(tensor, masks[1:2])
+    first, tensor = lax.optimization_barrier((first, tensor))
+    rest = split(tensor, masks[:1] + masks[2:])
+    blocks = [rest[0], first, *rest[1:]]
     for place in range(1, chips):
-        blocks[place] = in_chips(blocks[place], masks[place])
+        even_mask, odd_mask = masks[place]
+        blocks[place] = exchange(blocks[place], (0, even_mask), (0, odd_mask))
 
     inner, inner_low, held, own_half, away_half = pl.pallas_call(
         functools.partial(inner_kernel, masks),

time: 42.3 us -> 40.8 us (0.965)
  waiting for transfers between devices: 21.2 us -> 20.3 us
  starting transfers between devices: 12.5 us -> 11.9 us
    ppermute x3 -> x0, waiting for transfers between devices: 9.77 us -> none  [in_chips(): lax.ppermute(value, 'mode', [(i, i ^ flipped) for i in range(lax.axis_siz...]
    ppermute x6 -> x9, waiting for transfers between devices: 9.05 us -> 17.8 us  [exchange(): return lax.ppermute(value, ('slab', 'mode'), pairs)]
    ppermute x3 -> x0, starting transfers between devices: 4.98 us -> none  [in_chips(): lax.ppermute(value, 'mode', [(i, i ^ flipped) for i in range(lax.axis_siz...]
    ppermute x6 -> x9, starting transfers between devices: 6.85 us -> 11.8 us  [exchange(): return lax.ppermute(value, ('slab', 'mode'), pairs)]
    ppermute x3, starting transfers between devices: 0.69 us -> 0.14 us  [swap_cores(): lax.ppermute(value, 'mode', [(i, i ^ 1) for i in range(lax.axis_size('mod...]
where the time goes in v8:
time: 40.8 us; the launch traced here: 40.7 us
  waiting for transfers between devices  20.3 us (50%)
  starting transfers between devices  11.9 us (29%)
  Pallas kernels  7.65 us (19%)
  between operations  0.72 us (2%)
    ppermute x9, waiting for transfers between devices, exchange(): return lax.ppermute(value, ('slab', 'mode'), pairs)  17.8 us
    ppermute x9, starting transfers between devices, exchange(): return lax.ppermute(value, ('slab', 'mode'), pairs)  11.8 us
    pallas_call x1, Pallas kernels, shards(): pl.pallas_call(outputs_kernel, out_shape=(jax.ShapeDtypeStruct((row_count...  4.47 us
    ppermute x3, waiting for transfers between devices, swap_cores(): lax.ppermute(value, 'mode', [(i, i ^ 1) for i in range(lax.axis_size('mod...  2.53 us
    pallas_call x2, Pallas kernels, split(): pl.pallas_call(functools.partial(split_kernel, some), out_shape=[pltpu.VM...  1.99 us
  transfers between devices with their start and end apart: 12, of which 9 were waited for; matrix products, arithmetic and copies ran while one was open for 0% of the time, Pallas kernels for 3%

profile of v8, /device:TPU:0, one launch (start us, length us, event | category | flops | bytes accessed | tf_op | source)
XLA Modules:
  0.0 40.7 jit_solution(11967154443000957876)
XLA Ops:
  0.6 0.9 %shard_map.41 = bf16[64,1024]{1,0:T(8,128)(2,1)S(1)} custom-call(bf16[64,4096]{1,0:T(8,128)(2,1)} %tensor_ref.2), custom_call_target="tpu_custom_call" | custom-call | tf_op jit(solution)/shard_map/pallas_call | solution.py:259
  1.6 4.6 %collective-permute-start = (bf16[64,1024]{1,0:T(8,128)(2,1)S(1)}, bf16[64,1024]{1,0:T(8,128)(2,1)S(1)}, u32[]{:S(2)}, u32[]{:S(2)}) collective-permute-start(bf16[64,1024]{1,0:T(8,128)(2,1)S(1)} %shard_map.41), channel_id=1, source_target_pairs={{0,7},{1,5},{2,6},{3,4},{4,3},{5,1},{6,2},{7,0},{8,15},{9,13},{10,... | collective-permute-start | bytes 393224 | tf_op jit(solution)/shard_map/ppermute | solution.py:99
  6.1 1.1 %shard_map.42 = (bf16[64,1024]{1,0:T(8,128)(2,1)S(1)}, bf16[64,1024]{1,0:T(8,128)(2,1)S(1)}, bf16[64,1024]{1,0:T(8,128)(2,1)S(1)}) custom-call(bf16[64,4096]{1,0:T(8,128)(2,1)} %tensor_ref.2), custom_call_target="tpu_custom_call" | custom-call | tf_op jit(solution)/shard_map/pallas_call | solution.py:259
  7.3 0.3 collective-permute-start.2
  7.6 1.6 %collective-permute-done.refs_1_ = bf16[64,1024]{1,0:T(8,128)(2,1)S(1)} collective-permute-done((bf16[64,1024]{1,0:T(8,128)(2,1)S(1)}, bf16[64,1024]{1,0:T(8,128)(2,1)S(1)}, u32[]{:S(2)}, u32[]{:S(2)}) %collective-permute-start) | collective-permute-done | bytes 131104 | tf_op jit(solution)/shard_map/ppermute | solution.py:99
  9.1 8.5 %collective-permute-done.1.refs_2_ = bf16[64,1024]{1,0:T(8,128)(2,1)S(1)} collective-permute-done((bf16[64,1024]{1,0:T(8,128)(2,1)S(1)}, bf16[64,1024]{1,0:T(8,128)(2,1)S(1)}, u32[]{:S(2)}, u32[]{:S(2)}) %collective-permute-start.1) | collective-permute-done | bytes 131104 | tf_op jit(solution)/shard_map/ppermute | solution.py:99
  17.6 0.4 %shard_map.43 = (f32[128,1024]{1,0:T(8,128)S(1)}, bf16[128,1024]{1,0:T(8,128)(2,1)S(1)}, bf16[256,1024]{1,0:T(8,128)(2,1)S(1)}, bf16[256,512]{1,0:T(8,128)(2,1)S(1)}, bf16[256,512]{1,0:T(8,128)(2,1)S(1)}) custom-call(f32[512,128]{1,0:T(8,128)S(1)} %copy-done, bf16[64,1024]{1,0:T(8,128)(2,1)S(1)} %get-tuple-element.13.refs_0_, ...), custom_call_target="tpu_custom_call" | custom-call | tf_op jit(solution)/shard_map/pallas_call | solution.py:275
  18.1 0.1 collective-permute-start.3
  18.1 1.5 %collective-permute-done.3.other_ref = bf16[128,1024]{1,0:T(8,128)(2,1)S(1)} collective-permute-done((bf16[128,1024]{1,0:T(8,128)(2,1)S(1)}, bf16[128,1024]{1,0:T(8,128)(2,1)S(1)}, u32[]{:S(2)}, u32[]{:S(2)}) %collective-permute-start.3) | collective-permute-done | bytes 262176 | tf_op jit(solution)/shard_map/ppermute | solution.py:87
  19.7 0.4 %shard_map.44 = bf16[256,128]{1,0:T(8,128)(2,1)S(1)} custom-call(bf16[256,1024]{1,0:T(8,128)(2,1)S(1)} %get-tuple-element.17.held_ref, f32[128,1024]{1,0:T(8,128)S(1)} %get-tuple-element.18.own_ref, bf16[128,1024]{1,0:T(8,128)(2,1)S(1)} %collective-permute-done.3.other_ref), custom_call_target="tpu_custom_call" | custom-call | tf_op jit(solution)/shard_map/pallas_call | solution.py:290
  20.1 2.6 %collective-permute-start.6 = (bf16[256,128]{1,0:T(8,128)(2,1)S(1)}, bf16[256,128]{1,0:T(8,128)(2,1)S(1)}, u32[]{:S(2)}, u32[]{:S(2)}) collective-permute-start(bf16[256,128]{1,0:T(8,128)(2,1)S(1)} %shard_map.44), channel_id=1, source_target_pairs={{0,24},{1,5},{2,6},{3,27},{4,28},{5,1},{6,2},{7,31},{8,16},{9,13},... | collective-permute-start | bytes 196616 | tf_op jit(solution)/shard_map/ppermute | solution.py:99
  22.7 0.5 %collective-permute-start.5 = (bf16[256,128]{1,0:T(8,128)(2,1)S(1)}, bf16[256,128]{1,0:T(8,128)(2,1)S(1)}, u32[]{:S(2)}, u32[]{:S(2)}) collective-permute-start(bf16[256,128]{1,0:T(8,128)(2,1)S(1)} %shard_map.44), channel_id=1, source_target_pairs={{0,16},{1,6},{2,5},{3,19},{4,20},{5,2},{6,1},{7,23},{8,24},{9,14},... | collective-permute-start | bytes 196616 | tf_op jit(solution)/shard_map/ppermute | solution.py:99
  23.2 0.5 %collective-permute-start.4 = (bf16[256,128]{1,0:T(8,128)(2,1)S(1)}, bf16[256,128]{1,0:T(8,128)(2,1)S(1)}, u32[]{:S(2)}, u32[]{:S(2)}) collective-permute-start(bf16[256,128]{1,0:T(8,128)(2,1)S(1)} %shard_map.44), channel_id=1, source_target_pairs={{0,8},{1,2},{2,1},{3,11},{4,12},{5,6},{6,5},{7,15},{8,0},{9,10},{1... | collective-permute-start | bytes 196616 | tf_op jit(solution)/shard_map/ppermute | solution.py:99
  23.7 1.7 %collective-permute-done.6 = bf16[256,128]{1,0:T(8,128)(2,1)S(1)} collective-permute-done((bf16[256,128]{1,0:T(8,128)(2,1)S(1)}, bf16[256,128]{1,0:T(8,128)(2,1)S(1)}, u32[]{:S(2)}, u32[]{:S(2)}) %collective-permute-start.6) | collective-permute-done | bytes 65568 | tf_op jit(solution)/shard_map/ppermute | solution.py:99
  25.3 1.6 %collective-permute-done.5 = bf16[256,128]{1,0:T(8,128)(2,1)S(1)} collective-permute-done((bf16[256,128]{1,0:T(8,128)(2,1)S(1)}, bf16[256,128]{1,0:T(8,128)(2,1)S(1)}, u32[]{:S(2)}, u32[]{:S(2)}) %collective-permute-start.5) | collective-permute-done | bytes 65568 | tf_op jit(solution)/shard_map/ppermute | solution.py:99
  26.9 0.5 %collective-permute-done.4 = bf16[256,128]{1,0:T(8,128)(2,1)S(1)} collective-permute-done((bf16[256,128]{1,0:T(8,128)(2,1)S(1)}, bf16[256,128]{1,0:T(8,128)(2,1)S(1)}, u32[]{:S(2)}, u32[]{:S(2)}) %collective-permute-start.4) | collective-permute-done | bytes 65568 | tf_op jit(solution)/shard_map/ppermute | solution.py:99
  27.5 1.8 %collective-permute-start.9 = (bf16[256,128]{1,0:T(8,128)(2,1)S(1)}, bf16[256,128]{1,0:T(8,128)(2,1)S(1)}, u32[]{:S(2)}, u32[]{:S(2)}) collective-permute-start(bf16[256,128]{1,0:T(8,128)(2,1)S(1)} %add_convert_fusion), channel_id=1, source_target_pairs={{0,4},{1,25},{2,26},{3,7},{4,0},{5,29},{6,30},{7,3},{8,12},{9,17},... | collective-permute-start | bytes 196616 | tf_op jit(solution)/shard_map/ppermute | solution.py:99
  29.3 1.5 %collective-permute-start.7 = (bf16[256,128]{1,0:T(8,128)(2,1)S(1)}, bf16[256,128]{1,0:T(8,128)(2,1)S(1)}, u32[]{:S(2)}, u32[]{:S(2)}) collective-permute-start(bf16[256,128]{1,0:T(8,128)(2,1)S(1)} %add_convert_fusion), channel_id=1, source_target_pairs={{0,3},{1,9},{2,10},{3,0},{4,7},{5,13},{6,14},{7,4},{8,11},{9,1},{1... | collective-permute-start | bytes 196616 | tf_op jit(solution)/shard_map/ppermute | solution.py:99
  30.8 2.0 %collective-permute-done.9 = bf16[256,128]{1,0:T(8,128)(2,1)S(1)} collective-permute-done((bf16[256,128]{1,0:T(8,128)(2,1)S(1)}, bf16[256,128]{1,0:T(8,128)(2,1)S(1)}, u32[]{:S(2)}, u32[]{:S(2)}) %collective-permute-start.9) | collective-permute-done | bytes 65568 | tf_op jit(solution)/shard_map/ppermute | solution.py:99
  32.8 2.0 %collective-permute-done.8 = bf16[256,128]{1,0:T(8,128)(2,1)S(1)} collective-permute-done((bf16[256,128]{1,0:T(8,128)(2,1)S(1)}, bf16[256,128]{1,0:T(8,128)(2,1)S(1)}, u32[]{:S(2)}, u32[]{:S(2)}) %collective-permute-start.8) | collective-permute-done | bytes 65568 | tf_op jit(solution)/shard_map/ppermute | solution.py:99
  34.8 0.1 collective-permute-start.10
  34.9 0.3 shard_map.45.gram_ref
  35.2 1.0 %collective-permute-done.10.image_other_ref = f32[256,128]{1,0:T(8,128)S(1)} collective-permute-done((f32[256,128]{1,0:T(8,128)S(1)}, f32[256,128]{1,0:T(8,128)S(1)}, u32[]{:S(2)}, u32[]{:S(2)}) %collective-permute-start.10) | collective-permute-done | bytes 131104 | tf_op jit(solution)/shard_map/ppermute | solution.py:87
  36.2 4.5 %shard_map.46 = (f32[64,128]{1,0:T(8,128)}, f32[512,128]{1,0:T(8,128)}) custom-call(f32[128,128]{1,0:T(8,128)S(1)} %shard_map.45.gram_ref, f32[256,128]{1,0:T(8,128)S(1)} %add_add_fusion.image_ref, f32[256,128]{1,0:T(8,128)S(1)} %collective-permute-done.10.image_other_ref, bf16[256,512]{1,0:T(8,128)(2,1)S(1)} %get-tuple-element.20.own_ref, ...), custom_call_target="tpu_custom_call" | custom-call | tf_op jit(solution)/shard_map/pallas_call | solution.py:305
  (10 shorter events, 0.2 us)
Async XLA Ops:
  1.6 16.0 %copy-start = (f32[512,128]{1,0:T(8,128)S(1)}, f32[512,128]{1,0:T(8,128)}, u32[]{:S(2)}) copy-start(f32[512,128]{1,0:T(8,128)} %start_ref.1) | copy-start | bytes 786436
  1.6 7.5 %collective-permute-start = (bf16[64,1024]{1,0:T(8,128)(2,1)S(1)}, bf16[64,1024]{1,0:T(8,128)(2,1)S(1)}, u32[]{:S(2)}, u32[]{:S(2)}) collective-permute-start(bf16[64,1024]{1,0:T(8,128)(2,1)S(1)} %shard_map.41), channel_id=1, source_target_pairs={{0,7},{1,5},{2,6},{3,4},{4,3},{5,1},{6,2},{7,0},{8,15},{9,13},{10,... | collective-permute-start | bytes 393224 | tf_op jit(solution)/shard_map/ppermute | solution.py:99
  7.2 10.4 %collective-permute-start.1 = (bf16[64,1024]{1,0:T(8,128)(2,1)S(1)}, bf16[64,1024]{1,0:T(8,128)(2,1)S(1)}, u32[]{:S(2)}, u32[]{:S(2)}) collective-permute-start(bf16[64,1024]{1,0:T(8,128)(2,1)S(1)} %get-tuple-element.15), channel_id=1, source_target_pairs={{0,4},{1,6},{2,5},{3,7},{4,0},{5,2},{6,1},{7,3},{8,12},{9,14},{10,... | collective-permute-start | bytes 393224 | tf_op jit(solution)/shard_map/ppermute | solution.py:99
  7.3 10.3 %collective-permute-start.2 = (bf16[64,1024]{1,0:T(8,128)(2,1)S(1)}, bf16[64,1024]{1,0:T(8,128)(2,1)S(1)}, u32[]{:S(2)}, u32[]{:S(2)}) collective-permute-start(bf16[64,1024]{1,0:T(8,128)(2,1)S(1)} %get-tuple-element.16), channel_id=1, source_target_pairs={{0,3},{1,2},{2,1},{3,0},{4,7},{5,6},{6,5},{7,4},{8,11},{9,10},{10,... | collective-permute-start | bytes 393224 | tf_op jit(solution)/shard_map/ppermute | solution.py:99
  18.1 1.6 %collective-permute-start.3 = (bf16[128,1024]{1,0:T(8,128)(2,1)S(1)}, bf16[128,1024]{1,0:T(8,128)(2,1)S(1)}, u32[]{:S(2)}, u32[]{:S(2)}) collective-permute-start(bf16[128,1024]{1,0:T(8,128)(2,1)S(1)} %get-tuple-element.19), channel_id=1, source_target_pairs={{0,1},{1,0},{2,3},{3,2},{4,5},{5,4},{6,7},{7,6},{8,9},{9,8},{10,11... | collective-permute-start | bytes 786440 | tf_op jit(solution)/shard_map/ppermute | solution.py:87
  20.1 5.2 %collective-permute-start.6 = (bf16[256,128]{1,0:T(8,128)(2,1)S(1)}, bf16[256,128]{1,0:T(8,128)(2,1)S(1)}, u32[]{:S(2)}, u32[]{:S(2)}) collective-permute-start(bf16[256,128]{1,0:T(8,128)(2,1)S(1)} %shard_map.44), channel_id=1, source_target_pairs={{0,24},{1,5},{2,6},{3,27},{4,28},{5,1},{6,2},{7,31},{8,16},{9,13},... | collective-permute-start | bytes 196616 | tf_op jit(solution)/shard_map/ppermute | solution.py:99
  22.7 4.3 %collective-permute-start.5 = (bf16[256,128]{1,0:T(8,128)(2,1)S(1)}, bf16[256,128]{1,0:T(8,128)(2,1)S(1)}, u32[]{:S(2)}, u32[]{:S(2)}) collective-permute-start(bf16[256,128]{1,0:T(8,128)(2,1)S(1)} %shard_map.44), channel_id=1, source_target_pairs={{0,16},{1,6},{2,5},{3,19},{4,20},{5,2},{6,1},{7,23},{8,24},{9,14},... | collective-permute-start | bytes 196616 | tf_op jit(solution)/shard_map/ppermute | solution.py:99
  23.2 4.3 %collective-permute-start.4 = (bf16[256,128]{1,0:T(8,128)(2,1)S(1)}, bf16[256,128]{1,0:T(8,128)(2,1)S(1)}, u32[]{:S(2)}, u32[]{:S(2)}) collective-permute-start(bf16[256,128]{1,0:T(8,128)(2,1)S(1)} %shard_map.44), channel_id=1, source_target_pairs={{0,8},{1,2},{2,1},{3,11},{4,12},{5,6},{6,5},{7,15},{8,0},{9,10},{1... | collective-permute-start | bytes 196616 | tf_op jit(solution)/shard_map/ppermute | solution.py:99
  27.5 5.3 %collective-permute-start.9 = (bf16[256,128]{1,0:T(8,128)(2,1)S(1)}, bf16[256,128]{1,0:T(8,128)(2,1)S(1)}, u32[]{:S(2)}, u32[]{:S(2)}) collective-permute-start(bf16[256,128]{1,0:T(8,128)(2,1)S(1)} %add_convert_fusion), channel_id=1, source_target_pairs={{0,4},{1,25},{2,26},{3,7},{4,0},{5,29},{6,30},{7,3},{8,12},{9,17},... | collective-permute-start | bytes 196616 | tf_op jit(solution)/shard_map/ppermute | solution.py:99
  29.3 5.5 %collective-permute-start.8 = (bf16[256,128]{1,0:T(8,128)(2,1)S(1)}, bf16[256,128]{1,0:T(8,128)(2,1)S(1)}, u32[]{:S(2)}, u32[]{:S(2)}) collective-permute-start(bf16[256,128]{1,0:T(8,128)(2,1)S(1)} %add_convert_fusion), channel_id=1, source_target_pairs={{0,7},{1,17},{2,18},{3,4},{4,3},{5,21},{6,22},{7,0},{8,15},{9,25},... | collective-permute-start | bytes 196616 | tf_op jit(solution)/shard_map/ppermute | solution.py:99
  29.3 5.5 %collective-permute-start.7 = (bf16[256,128]{1,0:T(8,128)(2,1)S(1)}, bf16[256,128]{1,0:T(8,128)(2,1)S(1)}, u32[]{:S(2)}, u32[]{:S(2)}) collective-permute-start(bf16[256,128]{1,0:T(8,128)(2,1)S(1)} %add_convert_fusion), channel_id=1, source_target_pairs={{0,3},{1,9},{2,10},{3,0},{4,7},{5,13},{6,14},{7,4},{8,11},{9,1},{1... | collective-permute-start | bytes 196616 | tf_op jit(solution)/shard_map/ppermute | solution.py:99
  30.8 4.4 %collective-permute-start.11 = (bf16[256,512]{1,0:T(8,128)(2,1)S(1)}, bf16[256,512]{1,0:T(8,128)(2,1)S(1)}, u32[]{:S(2)}, u32[]{:S(2)}) collective-permute-start(bf16[256,512]{1,0:T(8,128)(2,1)S(1)} %get-tuple-element.21), channel_id=1, source_target_pairs={{0,1},{1,0},{2,3},{3,2},{4,5},{5,4},{6,7},{7,6},{8,9},{9,8},{10,11... | collective-permute-start | bytes 786440 | tf_op jit(solution)/shard_map/ppermute | solution.py:87
  34.8 1.4 %collective-permute-start.10 = (f32[256,128]{1,0:T(8,128)S(1)}, f32[256,128]{1,0:T(8,128)S(1)}, u32[]{:S(2)}, u32[]{:S(2)}) collective-permute-start(f32[256,128]{1,0:T(8,128)S(1)} %add_add_fusion.image_ref), channel_id=1, source_target_pairs={{0,1},{1,0},{2,3},{3,2},{4,5},{5,4},{6,7},{7,6},{8,9},{9,8},{10,11... | collective-permute-start | bytes 393224 | tf_op jit(solution)/shard_map/ppermute | solution.py:87

commit v9 on v8

--- a/solution.py
+++ b/solution.py
@@ -54,19 +54,16 @@
 
 
 def inner_kernel(masks, start_ref, *refs):
-    blocks, (inner_ref, inner_low_ref, held_ref, own_ref, away_ref) = refs[: len(masks)], refs[len(masks) :]
+    blocks, (inner_ref, inner_low_ref, held_ref) = refs[: len(masks)], refs[len(masks) :]
     mode_index = lax.axis_index("mode")
     chip, core = mode_index // 2, mode_index % 2
-    rows, width = blocks[0].shape
-    half = width // 2
+    rows = blocks[0].shape[0]
     starts = []
     for mask, block in zip(masks, blocks):
         mask = chosen(mask)
         source = chip ^ mask
         place = pl.ds(pl.multiple_of(source * rows, rows), rows)
         held_ref[place, :] = block[...]
-        own_ref[place, :] = block[:, pl.ds(pl.multiple_of(core * half, half), half)]
-        away_ref[place, :] = block[:, pl.ds(pl.multiple_of((1 - core) * half, half), half)]
         first = pl.multiple_of((source * 2 + (core ^ (mask & 1))) * rows, rows)
         starts.append(start_ref[pl.ds(first, rows), :])
     ordered = jnp.concatenate([block[...] for block in blocks], axis=0)
@@ -74,6 +71,12 @@
     inner = dot(high, ordered, contract_rows) + dot(low, ordered, contract_rows)
     inner_ref[...] = inner
     inner_low_ref[...] = inner.astype(bf16)
+
+
+def halves_kernel(held_ref, own_ref, away_ref):
+    core, half = lax.axis_index("mode") % 2, own_ref.shape[1]
+    own_ref[...] = held_ref[:, pl.ds(pl.multiple_of(core * half, half), half)]
+    away_ref[...] = held_ref[:, pl.ds(pl.multiple_of((1 - core) * half, half), half)]
 
 
 def image_kernel(held_ref, own_ref, other_ref, image_ref):
@@ -99,8 +102,17 @@
     return lax.ppermute(value, ("slab", "mode"), pairs)
 
 
-def both(first, second):
-    return (first[0] ^ second[0], first[1] ^ second[1])
+def add_kernel(value_ref, near_ref, side_ref, far_ref, total_ref):
+    value, near, side, far = [
+        ref[...].astype(f32) for ref in (value_ref, near_ref, side_ref, far_ref)
+    ]
+    total_ref[...] = ((value + near) + (side + far)).astype(total_ref.dtype)
+
+
+def three_ways(first, second):
+    sum_of_both = (first[0] ^ second[0], first[1] ^ second[1])
+    along_slab = not (first[1] or second[1])
+    return (second, first, sum_of_both) if along_slab else (first, sum_of_both, second)
 
 
 def sum_over_chips(value):
@@ -110,12 +122,15 @@
     along_mode = [(0, (2 << bit) - 1) for bit in range(chip_bits)]
     even, odd = along_slab + along_mode, along_mode + along_slab
     while len(even) >= 2:
-        (a, b), (c, d) = even[:2], odd[:2]
+        ways = zip(three_ways(*even[:2]), three_ways(*odd[:2]))
         even, odd = even[2:], odd[2:]
-        far = exchange(value, both(a, b), both(c, d)).astype(f32)
-        near = exchange(value, a, c).astype(f32)
-        side = exchange(value, b, d).astype(f32)
-        value = ((value.astype(f32) + near) + (side + far)).astype(value.dtype if len(even) else f32)
+        partners = [exchange(value, *masks) for masks in ways]
+        value = pl.pallas_call(
+            add_kernel,
+            out_shape=pltpu.VMEM(value.shape, value.dtype if even else f32),
+            in_specs=vmem_specs(4),
+            out_specs=vmem_specs(1)[0],
+        )(*in_vmem(value, *partners))
     if even:
         value = value.astype(f32) + exchange(value, even[0], odd[0]).astype(f32)
     return value
@@ -251,9 +266,8 @@
     held_rows = chips * row_count
     rank = start_block.shape[1]
 
-    last_mask = chips - 1
-    masks = [(0, 0), (last_mask, far_mask), (far_mask, last_mask)]
-    masks += [(mask, mask) for mask in range(1, chips) if mask not in (far_mask, last_mask)]
+    masks = [(0, 0), (far_mask, 1), (1, far_mask)] if far_mask > 1 else [(0, 0), (1, 1)]
+    masks += [(mask, mask) for mask in reversed(range(2, chips)) if mask != far_mask]
 
     def split(source, some):
         return pl.pallas_call(
@@ -272,19 +286,23 @@
         even_mask, odd_mask = masks[place]
         blocks[place] = exchange(blocks[place], (0, even_mask), (0, odd_mask))
 
-    inner, inner_low, held, own_half, away_half = pl.pallas_call(
+    inner, inner_low, held = pl.pallas_call(
         functools.partial(inner_kernel, masks),
         out_shape=(
             pltpu.VMEM((rank, chip_columns), f32),
             pltpu.VMEM((rank, chip_columns), bf16),
             pltpu.VMEM((held_rows, chip_columns), bf16),
-            pltpu.VMEM((held_rows, own_columns), bf16),
-            pltpu.VMEM((held_rows, own_columns), bf16),
         ),
         in_specs=vmem_specs(1 + chips),
-        out_specs=tuple(vmem_specs(5)),
+        out_specs=tuple(vmem_specs(3)),
     )(*in_vmem(start_block, *blocks))
     inner_other = swap_cores(inner_low)
+    own_half, away_half = pl.pallas_call(
+        halves_kernel,
+        out_shape=(pltpu.VMEM((held_rows, own_columns), bf16),) * 2,
+        in_specs=vmem_specs(1),
+        out_specs=tuple(vmem_specs(2)),
+    )(*in_vmem(held))
     other_half = swap_cores(away_half)
 
     image = pl.pallas_call(

time: 40.8 us -> 39.6 us (0.971)
  waiting for transfers between devices: 20.3 us -> 15.3 us
  starting transfers between devices: 11.9 us -> 15.7 us
    ppermute x9, waiting for transfers between devices: 17.8 us -> 13.1 us  [exchange(): return lax.ppermute(value, ('slab', 'mode'), pairs)]
    ppermute x3, starting transfers between devices: 0.14 us -> 2.29 us  [swap_cores(): lax.ppermute(value, 'mode', [(i, i ^ 1) for i in range(lax.axis_size('mod...]
    ppermute x9, starting transfers between devices: 11.8 us -> 13.5 us  [exchange(): return lax.ppermute(value, ('slab', 'mode'), pairs)]
  transfers between devices with their start and end apart: 12 -> 12, of which waited for: 9 -> 10; matrix products, arithmetic and copies ran while one was open for 0% -> 0% of each run, Pallas kernels for 3% -> 4%
where the time goes in v9:
time: 39.6 us; the launch traced here: 39.4 us
  starting transfers between devices  15.7 us (40%)
  waiting for transfers between devices  15.3 us (39%)
  Pallas kernels  7.71 us (19%)
  between operations  0.71 us (2%)
    ppermute x9, starting transfers between devices, exchange(): return lax.ppermute(value, ('slab', 'mode'), pairs)  13.5 us
    ppermute x9, waiting for transfers between devices, exchange(): return lax.ppermute(value, ('slab', 'mode'), pairs)  13.1 us
    pallas_call x1, Pallas kernels, shards(): pl.pallas_call(outputs_kernel, out_shape=(jax.ShapeDtypeStruct((row_count...  4.47 us
    ppermute x3, starting transfers between devices, swap_cores(): lax.ppermute(value, 'mode', [(i, i ^ 1) for i in range(lax.axis_size('mod...  2.29 us
    ppermute x3, waiting for transfers between devices, swap_cores(): lax.ppermute(value, 'mode', [(i, i ^ 1) for i in range(lax.axis_size('mod...  2.17 us
    pallas_call x2, Pallas kernels, split(): pl.pallas_call(functools.partial(split_kernel, some), out_shape=[pltpu.VM...  1.99 us
  transfers between devices with their start and end apart: 12, of which 10 were waited for; matrix products, arithmetic and copies ran while one was open for 0% of the time, Pallas kernels for 4%

profile of v9, /device:TPU:0, one launch (start us, length us, event | category | flops | bytes accessed | tf_op | source)
XLA Modules:
  0.0 39.4 jit_solution(16731425802847653595)
XLA Ops:
  0.6 0.9 %shard_map.41 = bf16[64,1024]{1,0:T(8,128)(2,1)S(1)} custom-call(bf16[64,4096]{1,0:T(8,128)(2,1)} %tensor_ref.2), custom_call_target="tpu_custom_call" | custom-call | tf_op jit(solution)/shard_map/pallas_call | solution.py:273
  1.6 4.1 %collective-permute-start = (bf16[64,1024]{1,0:T(8,128)(2,1)S(1)}, bf16[64,1024]{1,0:T(8,128)(2,1)S(1)}, u32[]{:S(2)}, u32[]{:S(2)}) collective-permute-start(bf16[64,1024]{1,0:T(8,128)(2,1)S(1)} %shard_map.41), channel_id=1, source_target_pairs={{0,4},{1,2},{2,1},{3,7},{4,0},{5,6},{6,5},{7,3},{8,12},{9,10},{10,... | collective-permute-start | bytes 393224 | tf_op jit(solution)/shard_map/ppermute | solution.py:102
  5.7 1.1 %shard_map.42 = (bf16[64,1024]{1,0:T(8,128)(2,1)S(1)}, bf16[64,1024]{1,0:T(8,128)(2,1)S(1)}, bf16[64,1024]{1,0:T(8,128)(2,1)S(1)}) custom-call(bf16[64,4096]{1,0:T(8,128)(2,1)} %tensor_ref.2), custom_call_target="tpu_custom_call" | custom-call | tf_op jit(solution)/shard_map/pallas_call | solution.py:273
  6.7 0.8 %collective-permute-start.1 = (bf16[64,1024]{1,0:T(8,128)(2,1)S(1)}, bf16[64,1024]{1,0:T(8,128)(2,1)S(1)}, u32[]{:S(2)}, u32[]{:S(2)}) collective-permute-start(bf16[64,1024]{1,0:T(8,128)(2,1)S(1)} %get-tuple-element.15), channel_id=1, source_target_pairs={{0,3},{1,5},{2,6},{3,0},{4,7},{5,1},{6,2},{7,4},{8,11},{9,13},{10,... | collective-permute-start | bytes 393224 | tf_op jit(solution)/shard_map/ppermute | solution.py:102
  7.5 0.5 %collective-permute-start.2 = (bf16[64,1024]{1,0:T(8,128)(2,1)S(1)}, bf16[64,1024]{1,0:T(8,128)(2,1)S(1)}, u32[]{:S(2)}, u32[]{:S(2)}) collective-permute-start(bf16[64,1024]{1,0:T(8,128)(2,1)S(1)} %get-tuple-element.16), channel_id=1, source_target_pairs={{0,7},{1,6},{2,5},{3,4},{4,3},{5,2},{6,1},{7,0},{8,15},{9,14},{10,... | collective-permute-start | bytes 393224 | tf_op jit(solution)/shard_map/ppermute | solution.py:102
  8.0 2.6 %collective-permute-done.refs_1_ = bf16[64,1024]{1,0:T(8,128)(2,1)S(1)} collective-permute-done((bf16[64,1024]{1,0:T(8,128)(2,1)S(1)}, bf16[64,1024]{1,0:T(8,128)(2,1)S(1)}, u32[]{:S(2)}, u32[]{:S(2)}) %collective-permute-start) | collective-permute-done | bytes 131104 | tf_op jit(solution)/shard_map/ppermute | solution.py:102
  10.7 2.5 %collective-permute-done.1.refs_2_ = bf16[64,1024]{1,0:T(8,128)(2,1)S(1)} collective-permute-done((bf16[64,1024]{1,0:T(8,128)(2,1)S(1)}, bf16[64,1024]{1,0:T(8,128)(2,1)S(1)}, u32[]{:S(2)}, u32[]{:S(2)}) %collective-permute-start.1) | collective-permute-done | bytes 131104 | tf_op jit(solution)/shard_map/ppermute | solution.py:102
  13.2 2.1 %collective-permute-done.2.refs_3_ = bf16[64,1024]{1,0:T(8,128)(2,1)S(1)} collective-permute-done((bf16[64,1024]{1,0:T(8,128)(2,1)S(1)}, bf16[64,1024]{1,0:T(8,128)(2,1)S(1)}, u32[]{:S(2)}, u32[]{:S(2)}) %collective-permute-start.2) | collective-permute-done | bytes 131104 | tf_op jit(solution)/shard_map/ppermute | solution.py:102
  15.3 0.4 shard_map.43
  15.7 0.5 %collective-permute-start.3 = (bf16[128,1024]{1,0:T(8,128)(2,1)S(1)}, bf16[128,1024]{1,0:T(8,128)(2,1)S(1)}, u32[]{:S(2)}, u32[]{:S(2)}) collective-permute-start(bf16[128,1024]{1,0:T(8,128)(2,1)S(1)} %get-tuple-element.19), channel_id=1, source_target_pairs={{0,1},{1,0},{2,3},{3,2},{4,5},{5,4},{6,7},{7,6},{8,9},{9,8},{10,11... | collective-permute-start | bytes 786440 | tf_op jit(solution)/shard_map/ppermute | solution.py:90
  16.3 1.2 %collective-permute-done.3.other_ref = bf16[128,1024]{1,0:T(8,128)(2,1)S(1)} collective-permute-done((bf16[128,1024]{1,0:T(8,128)(2,1)S(1)}, bf16[128,1024]{1,0:T(8,128)(2,1)S(1)}, u32[]{:S(2)}, u32[]{:S(2)}) %collective-permute-start.3) | collective-permute-done | bytes 262176 | tf_op jit(solution)/shard_map/ppermute | solution.py:90
  17.4 0.4 %shard_map.44.value_ref = bf16[256,128]{1,0:T(8,128)(2,1)S(1)} custom-call(bf16[256,1024]{1,0:T(8,128)(2,1)S(1)} %get-tuple-element.17.held_ref, f32[128,1024]{1,0:T(8,128)S(1)} %get-tuple-element.18.own_ref, bf16[128,1024]{1,0:T(8,128)(2,1)S(1)} %collective-permute-done.3.other_ref), custom_call_target="tpu_custom_call" | custom-call | tf_op jit(solution)/shard_map/pallas_call | solution.py:308
  17.9 2.8 %collective-permute-start.6 = (bf16[256,128]{1,0:T(8,128)(2,1)S(1)}, bf16[256,128]{1,0:T(8,128)(2,1)S(1)}, u32[]{:S(2)}, u32[]{:S(2)}) collective-permute-start(bf16[256,128]{1,0:T(8,128)(2,1)S(1)} %shard_map.44.value_ref), channel_id=1, source_target_pairs={{0,24},{1,6},{2,5},{3,27},{4,28},{5,2},{6,1},{7,31},{8,16},{9,14},... | collective-permute-start | bytes 196616 | tf_op jit(solution)/shard_map/ppermute | solution.py:102
  20.6 0.5 %collective-permute-start.5 = (bf16[256,128]{1,0:T(8,128)(2,1)S(1)}, bf16[256,128]{1,0:T(8,128)(2,1)S(1)}, u32[]{:S(2)}, u32[]{:S(2)}) collective-permute-start(bf16[256,128]{1,0:T(8,128)(2,1)S(1)} %shard_map.44.value_ref), channel_id=1, source_target_pairs={{0,8},{1,5},{2,6},{3,11},{4,12},{5,1},{6,2},{7,15},{8,0},{9,13},{1... | collective-permute-start | bytes 196616 | tf_op jit(solution)/shard_map/ppermute | solution.py:102
  21.5 1.7 %collective-permute-start.11 = (bf16[256,512]{1,0:T(8,128)(2,1)S(1)}, bf16[256,512]{1,0:T(8,128)(2,1)S(1)}, u32[]{:S(2)}, u32[]{:S(2)}) collective-permute-start(bf16[256,512]{1,0:T(8,128)(2,1)S(1)} %get-tuple-element.21), channel_id=1, source_target_pairs={{0,1},{1,0},{2,3},{3,2},{4,5},{5,4},{6,7},{7,6},{8,9},{9,8},{10,11... | collective-permute-start | bytes 786440 | tf_op jit(solution)/shard_map/ppermute | solution.py:90
  23.1 1.8 %collective-permute-done.5.side_ref = bf16[256,128]{1,0:T(8,128)(2,1)S(1)} collective-permute-done((bf16[256,128]{1,0:T(8,128)(2,1)S(1)}, bf16[256,128]{1,0:T(8,128)(2,1)S(1)}, u32[]{:S(2)}, u32[]{:S(2)}) %collective-permute-start.5) | collective-permute-done | bytes 65568 | tf_op jit(solution)/shard_map/ppermute | solution.py:102
  24.9 0.5 %collective-permute-done.4.near_ref = bf16[256,128]{1,0:T(8,128)(2,1)S(1)} collective-permute-done((bf16[256,128]{1,0:T(8,128)(2,1)S(1)}, bf16[256,128]{1,0:T(8,128)(2,1)S(1)}, u32[]{:S(2)}, u32[]{:S(2)}) %collective-permute-start.4) | collective-permute-done | bytes 65568 | tf_op jit(solution)/shard_map/ppermute | solution.py:102
  25.5 2.1 %collective-permute-start.9 = (bf16[256,128]{1,0:T(8,128)(2,1)S(1)}, bf16[256,128]{1,0:T(8,128)(2,1)S(1)}, u32[]{:S(2)}, u32[]{:S(2)}) collective-permute-start(bf16[256,128]{1,0:T(8,128)(2,1)S(1)} %shard_map.45.value_ref), channel_id=1, source_target_pairs={{0,7},{1,25},{2,26},{3,4},{4,3},{5,29},{6,30},{7,0},{8,15},{9,17},... | collective-permute-start | bytes 196616 | tf_op jit(solution)/shard_map/ppermute | solution.py:102
  27.6 2.3 %collective-permute-start.8 = (bf16[256,128]{1,0:T(8,128)(2,1)S(1)}, bf16[256,128]{1,0:T(8,128)(2,1)S(1)}, u32[]{:S(2)}, u32[]{:S(2)}) collective-permute-start(bf16[256,128]{1,0:T(8,128)(2,1)S(1)} %shard_map.45.value_ref), channel_id=1, source_target_pairs={{0,4},{1,9},{2,10},{3,7},{4,0},{5,13},{6,14},{7,3},{8,12},{9,1},{1... | collective-permute-start | bytes 196616 | tf_op jit(solution)/shard_map/ppermute | solution.py:102
  30.0 1.0 %collective-permute-done.9.far_ref = bf16[256,128]{1,0:T(8,128)(2,1)S(1)} collective-permute-done((bf16[256,128]{1,0:T(8,128)(2,1)S(1)}, bf16[256,128]{1,0:T(8,128)(2,1)S(1)}, u32[]{:S(2)}, u32[]{:S(2)}) %collective-permute-start.9) | collective-permute-done | bytes 65568 | tf_op jit(solution)/shard_map/ppermute | solution.py:102
  31.0 1.7 %collective-permute-done.8.side_ref = bf16[256,128]{1,0:T(8,128)(2,1)S(1)} collective-permute-done((bf16[256,128]{1,0:T(8,128)(2,1)S(1)}, bf16[256,128]{1,0:T(8,128)(2,1)S(1)}, u32[]{:S(2)}, u32[]{:S(2)}) %collective-permute-start.8) | collective-permute-done | bytes 65568 | tf_op jit(solution)/shard_map/ppermute | solution.py:102
  32.7 0.8 %collective-permute-done.7.near_ref = bf16[256,128]{1,0:T(8,128)(2,1)S(1)} collective-permute-done((bf16[256,128]{1,0:T(8,128)(2,1)S(1)}, bf16[256,128]{1,0:T(8,128)(2,1)S(1)}, u32[]{:S(2)}, u32[]{:S(2)}) %collective-permute-start.7) | collective-permute-done | bytes 65568 | tf_op jit(solution)/shard_map/ppermute | solution.py:102
  33.9 1.0 %collective-permute-done.10.image_other_ref = f32[256,128]{1,0:T(8,128)S(1)} collective-permute-done((f32[256,128]{1,0:T(8,128)S(1)}, f32[256,128]{1,0:T(8,128)S(1)}, u32[]{:S(2)}, u32[]{:S(2)}) %collective-permute-start.10) | collective-permute-done | bytes 131104 | tf_op jit(solution)/shard_map/ppermute | solution.py:90
  35.0 4.5 %shard_map.49 = (f32[64,128]{1,0:T(8,128)}, f32[512,128]{1,0:T(8,128)}) custom-call(f32[128,128]{1,0:T(8,128)S(1)} %shard_map.47.gram_ref, f32[256,128]{1,0:T(8,128)S(1)} %shard_map.46.image_ref, f32[256,128]{1,0:T(8,128)S(1)} %collective-permute-done.10.image_other_ref, bf16[256,512]{1,0:T(8,128)(2,1)S(1)} %get-tuple-element.20.own_ref, ...), custom_call_target="tpu_custom_call" | custom-call | tf_op jit(solution)/shard_map/pallas_call | solution.py:323
  (11 shorter events, 0.9 us)
Async XLA Ops:
  1.6 13.7 %copy-start = (f32[512,128]{1,0:T(8,128)S(1)}, f32[512,128]{1,0:T(8,128)}, u32[]{:S(2)}) copy-start(f32[512,128]{1,0:T(8,128)} %start_ref.1) | copy-start | bytes 786436
  1.6 9.1 %collective-permute-start = (bf16[64,1024]{1,0:T(8,128)(2,1)S(1)}, bf16[64,1024]{1,0:T(8,128)(2,1)S(1)}, u32[]{:S(2)}, u32[]{:S(2)}) collective-permute-start(bf16[64,1024]{1,0:T(8,128)(2,1)S(1)} %shard_map.41), channel_id=1, source_target_pairs={{0,4},{1,2},{2,1},{3,7},{4,0},{5,6},{6,5},{7,3},{8,12},{9,10},{10,... | collective-permute-start | bytes 393224 | tf_op jit(solution)/shard_map/ppermute | solution.py:102
  6.7 6.4 %collective-permute-start.1 = (bf16[64,1024]{1,0:T(8,128)(2,1)S(1)}, bf16[64,1024]{1,0:T(8,128)(2,1)S(1)}, u32[]{:S(2)}, u32[]{:S(2)}) collective-permute-start(bf16[64,1024]{1,0:T(8,128)(2,1)S(1)} %get-tuple-element.15), channel_id=1, source_target_pairs={{0,3},{1,5},{2,6},{3,0},{4,7},{5,1},{6,2},{7,4},{8,11},{9,13},{10,... | collective-permute-start | bytes 393224 | tf_op jit(solution)/shard_map/ppermute | solution.py:102
  7.5 7.8 %collective-permute-start.2 = (bf16[64,1024]{1,0:T(8,128)(2,1)S(1)}, bf16[64,1024]{1,0:T(8,128)(2,1)S(1)}, u32[]{:S(2)}, u32[]{:S(2)}) collective-permute-start(bf16[64,1024]{1,0:T(8,128)(2,1)S(1)} %get-tuple-element.16), channel_id=1, source_target_pairs={{0,7},{1,6},{2,5},{3,4},{4,3},{5,2},{6,1},{7,0},{8,15},{9,14},{10,... | collective-permute-start | bytes 393224 | tf_op jit(solution)/shard_map/ppermute | solution.py:102
  15.7 1.7 %collective-permute-start.3 = (bf16[128,1024]{1,0:T(8,128)(2,1)S(1)}, bf16[128,1024]{1,0:T(8,128)(2,1)S(1)}, u32[]{:S(2)}, u32[]{:S(2)}) collective-permute-start(bf16[128,1024]{1,0:T(8,128)(2,1)S(1)} %get-tuple-element.19), channel_id=1, source_target_pairs={{0,1},{1,0},{2,3},{3,2},{4,5},{5,4},{6,7},{7,6},{8,9},{9,8},{10,11... | collective-permute-start | bytes 786440 | tf_op jit(solution)/shard_map/ppermute | solution.py:90
  17.9 5.3 %collective-permute-start.6 = (bf16[256,128]{1,0:T(8,128)(2,1)S(1)}, bf16[256,128]{1,0:T(8,128)(2,1)S(1)}, u32[]{:S(2)}, u32[]{:S(2)}) collective-permute-start(bf16[256,128]{1,0:T(8,128)(2,1)S(1)} %shard_map.44.value_ref), channel_id=1, source_target_pairs={{0,24},{1,6},{2,5},{3,27},{4,28},{5,2},{6,1},{7,31},{8,16},{9,14},... | collective-permute-start | bytes 196616 | tf_op jit(solution)/shard_map/ppermute | solution.py:102
  20.6 4.3 %collective-permute-start.5 = (bf16[256,128]{1,0:T(8,128)(2,1)S(1)}, bf16[256,128]{1,0:T(8,128)(2,1)S(1)}, u32[]{:S(2)}, u32[]{:S(2)}) collective-permute-start(bf16[256,128]{1,0:T(8,128)(2,1)S(1)} %shard_map.44.value_ref), channel_id=1, source_target_pairs={{0,8},{1,5},{2,6},{3,11},{4,12},{5,1},{6,2},{7,15},{8,0},{9,13},{1... | collective-permute-start | bytes 196616 | tf_op jit(solution)/shard_map/ppermute | solution.py:102
  21.2 4.3 %collective-permute-start.4 = (bf16[256,128]{1,0:T(8,128)(2,1)S(1)}, bf16[256,128]{1,0:T(8,128)(2,1)S(1)}, u32[]{:S(2)}, u32[]{:S(2)}) collective-permute-start(bf16[256,128]{1,0:T(8,128)(2,1)S(1)} %shard_map.44.value_ref), channel_id=1, source_target_pairs={{0,16},{1,2},{2,1},{3,19},{4,20},{5,6},{6,5},{7,23},{8,24},{9,10},... | collective-permute-start | bytes 196616 | tf_op jit(solution)/shard_map/ppermute | solution.py:102
  21.5 12.5 %collective-permute-start.11 = (bf16[256,512]{1,0:T(8,128)(2,1)S(1)}, bf16[256,512]{1,0:T(8,128)(2,1)S(1)}, u32[]{:S(2)}, u32[]{:S(2)}) collective-permute-start(bf16[256,512]{1,0:T(8,128)(2,1)S(1)} %get-tuple-element.21), channel_id=1, source_target_pairs={{0,1},{1,0},{2,3},{3,2},{4,5},{5,4},{6,7},{7,6},{8,9},{9,8},{10,11... | collective-permute-start | bytes 786440 | tf_op jit(solution)/shard_map/ppermute | solution.py:90
  25.5 5.6 %collective-permute-start.9 = (bf16[256,128]{1,0:T(8,128)(2,1)S(1)}, bf16[256,128]{1,0:T(8,128)(2,1)S(1)}, u32[]{:S(2)}, u32[]{:S(2)}) collective-permute-start(bf16[256,128]{1,0:T(8,128)(2,1)S(1)} %shard_map.45.value_ref), channel_id=1, source_target_pairs={{0,7},{1,25},{2,26},{3,4},{4,3},{5,29},{6,30},{7,0},{8,15},{9,17},... | collective-permute-start | bytes 196616 | tf_op jit(solution)/shard_map/ppermute | solution.py:102
  27.6 5.2 %collective-permute-start.8 = (bf16[256,128]{1,0:T(8,128)(2,1)S(1)}, bf16[256,128]{1,0:T(8,128)(2,1)S(1)}, u32[]{:S(2)}, u32[]{:S(2)}) collective-permute-start(bf16[256,128]{1,0:T(8,128)(2,1)S(1)} %shard_map.45.value_ref), channel_id=1, source_target_pairs={{0,4},{1,9},{2,10},{3,7},{4,0},{5,13},{6,14},{7,3},{8,12},{9,1},{1... | collective-permute-start | bytes 196616 | tf_op jit(solution)/shard_map/ppermute | solution.py:102
  29.8 3.7 %collective-permute-start.7 = (bf16[256,128]{1,0:T(8,128)(2,1)S(1)}, bf16[256,128]{1,0:T(8,128)(2,1)S(1)}, u32[]{:S(2)}, u32[]{:S(2)}) collective-permute-start(bf16[256,128]{1,0:T(8,128)(2,1)S(1)} %shard_map.45.value_ref), channel_id=1, source_target_pairs={{0,3},{1,17},{2,18},{3,0},{4,7},{5,21},{6,22},{7,4},{8,11},{9,25},... | collective-permute-start | bytes 196616 | tf_op jit(solution)/shard_map/ppermute | solution.py:102
  33.5 1.4 %collective-permute-start.10 = (f32[256,128]{1,0:T(8,128)S(1)}, f32[256,128]{1,0:T(8,128)S(1)}, u32[]{:S(2)}, u32[]{:S(2)}) collective-permute-start(f32[256,128]{1,0:T(8,128)S(1)} %shard_map.46.image_ref), channel_id=1, source_target_pairs={{0,1},{1,0},{2,3},{3,2},{4,5},{5,4},{6,7},{7,6},{8,9},{9,8},{10,11... | collective-permute-start | bytes 393224 | tf_op jit(solution)/shard_map/ppermute | solution.py:90

commit v10 on v9

--- a/solution.py
+++ b/solution.py
@@ -42,11 +42,15 @@
     width = blocks[0].shape[1]
     chip = lax.axis_index("mode") // 2
     copies = []
-    for place, (mask, block) in enumerate(zip(masks, blocks)):
+    for mask, block in zip(masks, blocks):
         columns = pl.ds(pl.multiple_of((chip ^ chosen(mask)) * width, width), width)
-        copies.append(
-            pltpu.make_async_copy(tensor_ref.at[:, columns], block, semaphores.at[place])
-        )
+        for first in range(0, block.shape[0], 16):
+            rows = pl.ds(first, 16)
+            copies.append(
+                pltpu.make_async_copy(
+                    tensor_ref.at[rows, columns], block.at[rows], semaphores.at[len(copies)]
+                )
+            )
     for copy in copies:
         copy.start()
     for copy in copies:
@@ -54,16 +58,19 @@
 
 
 def inner_kernel(masks, start_ref, *refs):
-    blocks, (inner_ref, inner_low_ref, held_ref) = refs[: len(masks)], refs[len(masks) :]
+    blocks, (inner_ref, inner_low_ref, held_ref, own_ref, away_ref) = refs[: len(masks)], refs[len(masks) :]
     mode_index = lax.axis_index("mode")
     chip, core = mode_index // 2, mode_index % 2
-    rows = blocks[0].shape[0]
+    rows, width = blocks[0].shape
+    half = width // 2
     starts = []
     for mask, block in zip(masks, blocks):
         mask = chosen(mask)
         source = chip ^ mask
         place = pl.ds(pl.multiple_of(source * rows, rows), rows)
         held_ref[place, :] = block[...]
+        own_ref[place, :] = block[:, pl.ds(pl.multiple_of(core * half, half), half)]
+        away_ref[place, :] = block[:, pl.ds(pl.multiple_of((1 - core) * half, half), half)]
         first = pl.multiple_of((source * 2 + (core ^ (mask & 1))) * rows, rows)
         starts.append(start_ref[pl.ds(first, rows), :])
     ordered = jnp.concatenate([block[...] for block in blocks], axis=0)
@@ -71,12 +78,6 @@
     inner = dot(high, ordered, contract_rows) + dot(low, ordered, contract_rows)
     inner_ref[...] = inner
     inner_low_ref[...] = inner.astype(bf16)
-
-
-def halves_kernel(held_ref, own_ref, away_ref):
-    core, half = lax.axis_index("mode") % 2, own_ref.shape[1]
-    own_ref[...] = held_ref[:, pl.ds(pl.multiple_of(core * half, half), half)]
-    away_ref[...] = held_ref[:, pl.ds(pl.multiple_of((1 - core) * half, half), half)]
 
 
 def image_kernel(held_ref, own_ref, other_ref, image_ref):
@@ -275,7 +276,7 @@
             out_shape=[pltpu.VMEM((row_count, chip_columns), bf16)] * len(some),
             in_specs=[pl.BlockSpec(memory_space=pl.ANY)],
             out_specs=vmem_specs(len(some)),
-            scratch_shapes=[pltpu.SemaphoreType.DMA((len(some),))],
+            scratch_shapes=[pltpu.SemaphoreType.DMA((len(some) * row_count // 16,))],
         )(source)
 
     (first,) = split(tensor, masks[1:2])
@@ -286,23 +287,19 @@
         even_mask, odd_mask = masks[place]
         blocks[place] = exchange(blocks[place], (0, even_mask), (0, odd_mask))
 
-    inner, inner_low, held = pl.pallas_call(
+    inner, inner_low, held, own_half, away_half = pl.pallas_call(
         functools.partial(inner_kernel, masks),
         out_shape=(
             pltpu.VMEM((rank, chip_columns), f32),
             pltpu.VMEM((rank, chip_columns), bf16),
             pltpu.VMEM((held_rows, chip_columns), bf16),
+            pltpu.VMEM((held_rows, own_columns), bf16),
+            pltpu.VMEM((held_rows, own_columns), bf16),
         ),
         in_specs=vmem_specs(1 + chips),
-        out_specs=tuple(vmem_specs(3)),
+        out_specs=tuple(vmem_specs(5)),
     )(*in_vmem(start_block, *blocks))
     inner_other = swap_cores(inner_low)
-    own_half, away_half = pl.pallas_call(
-        halves_kernel,
-        out_shape=(pltpu.VMEM((held_rows, own_columns), bf16),) * 2,
-        in_specs=vmem_specs(1),
-        out_specs=tuple(vmem_specs(2)),
-    )(*in_vmem(held))
     other_half = swap_cores(away_half)
 
     image = pl.pallas_call(

time: 39.6 us -> 39.7 us (level)
  transfers between devices with their start and end apart: 12 -> 12, of which waited for: 10 -> 11; matrix products, arithmetic and copies ran while one was open for 0% -> 0% of each run, Pallas kernels for 4% -> 4%
where the time goes in v10:
time: 39.7 us; the launch traced here: 39.4 us
  starting transfers between devices  15.7 us (40%)
  waiting for transfers between devices  15.4 us (39%)
  Pallas kernels  7.62 us (19%)
  between operations  0.71 us (2%)
    ppermute x9, starting transfers between devices, exchange(): return lax.ppermute(value, ('slab', 'mode'), pairs)  13.5 us
    ppermute x9, waiting for transfers between devices, exchange(): return lax.ppermute(value, ('slab', 'mode'), pairs)  13.2 us
    pallas_call x1, Pallas kernels, shards(): pl.pallas_call(outputs_kernel, out_shape=(jax.ShapeDtypeStruct((row_count...  4.47 us
    ppermute x3, starting transfers between devices, swap_cores(): lax.ppermute(value, 'mode', [(i, i ^ 1) for i in range(lax.axis_size('mod...  2.24 us
    ppermute x3, waiting for transfers between devices, swap_cores(): lax.ppermute(value, 'mode', [(i, i ^ 1) for i in range(lax.axis_size('mod...  2.18 us
    pallas_call x2, Pallas kernels, split(): pl.pallas_call(functools.partial(split_kernel, some), out_shape=[pltpu.VM...  1.9 us
  transfers between devices with their start and end apart: 12, of which 11 were waited for; matrix products, arithmetic and copies ran while one was open for 0% of the time, Pallas kernels for 4%

profile of v10, /device:TPU:0, one launch (start us, length us, event | category | flops | bytes accessed | tf_op | source)
XLA Modules:
  0.0 39.4 jit_solution(16922323435510933806)
XLA Ops:
  0.6 0.9 %shard_map.41 = bf16[64,1024]{1,0:T(8,128)(2,1)S(1)} custom-call(bf16[64,4096]{1,0:T(8,128)(2,1)} %tensor_ref.2), custom_call_target="tpu_custom_call" | custom-call | tf_op jit(solution)/shard_map/pallas_call | solution.py:274
  1.5 4.1 %collective-permute-start = (bf16[64,1024]{1,0:T(8,128)(2,1)S(1)}, bf16[64,1024]{1,0:T(8,128)(2,1)S(1)}, u32[]{:S(2)}, u32[]{:S(2)}) collective-permute-start(bf16[64,1024]{1,0:T(8,128)(2,1)S(1)} %shard_map.41), channel_id=1, source_target_pairs={{0,4},{1,2},{2,1},{3,7},{4,0},{5,6},{6,5},{7,3},{8,12},{9,10},{10,... | collective-permute-start | bytes 393224 | tf_op jit(solution)/shard_map/ppermute | solution.py:103
  5.6 1.0 %shard_map.42 = (bf16[64,1024]{1,0:T(8,128)(2,1)S(1)}, bf16[64,1024]{1,0:T(8,128)(2,1)S(1)}, bf16[64,1024]{1,0:T(8,128)(2,1)S(1)}) custom-call(bf16[64,4096]{1,0:T(8,128)(2,1)} %tensor_ref.2), custom_call_target="tpu_custom_call" | custom-call | tf_op jit(solution)/shard_map/pallas_call | solution.py:274
  6.7 0.8 %collective-permute-start.1 = (bf16[64,1024]{1,0:T(8,128)(2,1)S(1)}, bf16[64,1024]{1,0:T(8,128)(2,1)S(1)}, u32[]{:S(2)}, u32[]{:S(2)}) collective-permute-start(bf16[64,1024]{1,0:T(8,128)(2,1)S(1)} %get-tuple-element.15), channel_id=1, source_target_pairs={{0,3},{1,5},{2,6},{3,0},{4,7},{5,1},{6,2},{7,4},{8,11},{9,13},{10,... | collective-permute-start | bytes 393224 | tf_op jit(solution)/shard_map/ppermute | solution.py:103
  7.5 0.5 %collective-permute-start.2 = (bf16[64,1024]{1,0:T(8,128)(2,1)S(1)}, bf16[64,1024]{1,0:T(8,128)(2,1)S(1)}, u32[]{:S(2)}, u32[]{:S(2)}) collective-permute-start(bf16[64,1024]{1,0:T(8,128)(2,1)S(1)} %get-tuple-element.16), channel_id=1, source_target_pairs={{0,7},{1,6},{2,5},{3,4},{4,3},{5,2},{6,1},{7,0},{8,15},{9,14},{10,... | collective-permute-start | bytes 393224 | tf_op jit(solution)/shard_map/ppermute | solution.py:103
  7.9 2.6 %collective-permute-done.refs_1_ = bf16[64,1024]{1,0:T(8,128)(2,1)S(1)} collective-permute-done((bf16[64,1024]{1,0:T(8,128)(2,1)S(1)}, bf16[64,1024]{1,0:T(8,128)(2,1)S(1)}, u32[]{:S(2)}, u32[]{:S(2)}) %collective-permute-start) | collective-permute-done | bytes 131104 | tf_op jit(solution)/shard_map/ppermute | solution.py:103
  10.6 2.5 %collective-permute-done.1.refs_2_ = bf16[64,1024]{1,0:T(8,128)(2,1)S(1)} collective-permute-done((bf16[64,1024]{1,0:T(8,128)(2,1)S(1)}, bf16[64,1024]{1,0:T(8,128)(2,1)S(1)}, u32[]{:S(2)}, u32[]{:S(2)}) %collective-permute-start.1) | collective-permute-done | bytes 131104 | tf_op jit(solution)/shard_map/ppermute | solution.py:103
  13.1 2.1 %collective-permute-done.2.refs_3_ = bf16[64,1024]{1,0:T(8,128)(2,1)S(1)} collective-permute-done((bf16[64,1024]{1,0:T(8,128)(2,1)S(1)}, bf16[64,1024]{1,0:T(8,128)(2,1)S(1)}, u32[]{:S(2)}, u32[]{:S(2)}) %collective-permute-start.2) | collective-permute-done | bytes 131104 | tf_op jit(solution)/shard_map/ppermute | solution.py:103
  15.2 0.4 %shard_map.43 = (f32[128,1024]{1,0:T(8,128)S(1)}, bf16[128,1024]{1,0:T(8,128)(2,1)S(1)}, bf16[256,1024]{1,0:T(8,128)(2,1)S(1)}, bf16[256,512]{1,0:T(8,128)(2,1)S(1)}, bf16[256,512]{1,0:T(8,128)(2,1)S(1)}) custom-call(f32[512,128]{1,0:T(8,128)S(1)} %copy-done, bf16[64,1024]{1,0:T(8,128)(2,1)S(1)} %get-tuple-element.13.refs_0_, ...), custom_call_target="tpu_custom_call" | custom-call | tf_op jit(solution)/shard_map/pallas_call | solution.py:290
  15.7 0.6 %collective-permute-start.3 = (bf16[128,1024]{1,0:T(8,128)(2,1)S(1)}, bf16[128,1024]{1,0:T(8,128)(2,1)S(1)}, u32[]{:S(2)}, u32[]{:S(2)}) collective-permute-start(bf16[128,1024]{1,0:T(8,128)(2,1)S(1)} %get-tuple-element.19), channel_id=1, source_target_pairs={{0,1},{1,0},{2,3},{3,2},{4,5},{5,4},{6,7},{7,6},{8,9},{9,8},{10,11... | collective-permute-start | bytes 786440 | tf_op jit(solution)/shard_map/ppermute | solution.py:91
  16.2 1.2 %collective-permute-done.3.other_ref = bf16[128,1024]{1,0:T(8,128)(2,1)S(1)} collective-permute-done((bf16[128,1024]{1,0:T(8,128)(2,1)S(1)}, bf16[128,1024]{1,0:T(8,128)(2,1)S(1)}, u32[]{:S(2)}, u32[]{:S(2)}) %collective-permute-start.3) | collective-permute-done | bytes 262176 | tf_op jit(solution)/shard_map/ppermute | solution.py:91
  17.4 0.4 %shard_map.44.value_ref = bf16[256,128]{1,0:T(8,128)(2,1)S(1)} custom-call(bf16[256,1024]{1,0:T(8,128)(2,1)S(1)} %get-tuple-element.17.held_ref, f32[128,1024]{1,0:T(8,128)S(1)} %get-tuple-element.18.own_ref, bf16[128,1024]{1,0:T(8,128)(2,1)S(1)} %collective-permute-done.3.other_ref), custom_call_target="tpu_custom_call" | custom-call | tf_op jit(solution)/shard_map/pallas_call | solution.py:305
  17.8 2.8 %collective-permute-start.6 = (bf16[256,128]{1,0:T(8,128)(2,1)S(1)}, bf16[256,128]{1,0:T(8,128)(2,1)S(1)}, u32[]{:S(2)}, u32[]{:S(2)}) collective-permute-start(bf16[256,128]{1,0:T(8,128)(2,1)S(1)} %shard_map.44.value_ref), channel_id=1, source_target_pairs={{0,24},{1,6},{2,5},{3,27},{4,28},{5,2},{6,1},{7,31},{8,16},{9,14},... | collective-permute-start | bytes 196616 | tf_op jit(solution)/shard_map/ppermute | solution.py:103
  20.6 0.5 %collective-permute-start.5 = (bf16[256,128]{1,0:T(8,128)(2,1)S(1)}, bf16[256,128]{1,0:T(8,128)(2,1)S(1)}, u32[]{:S(2)}, u32[]{:S(2)}) collective-permute-start(bf16[256,128]{1,0:T(8,128)(2,1)S(1)} %shard_map.44.value_ref), channel_id=1, source_target_pairs={{0,8},{1,5},{2,6},{3,11},{4,12},{5,1},{6,2},{7,15},{8,0},{9,13},{1... | collective-permute-start | bytes 196616 | tf_op jit(solution)/shard_map/ppermute | solution.py:103
  21.4 1.6 %collective-permute-start.11 = (bf16[256,512]{1,0:T(8,128)(2,1)S(1)}, bf16[256,512]{1,0:T(8,128)(2,1)S(1)}, u32[]{:S(2)}, u32[]{:S(2)}) collective-permute-start(bf16[256,512]{1,0:T(8,128)(2,1)S(1)} %get-tuple-element.21), channel_id=1, source_target_pairs={{0,1},{1,0},{2,3},{3,2},{4,5},{5,4},{6,7},{7,6},{8,9},{9,8},{10,11... | collective-permute-start | bytes 786440 | tf_op jit(solution)/shard_map/ppermute | solution.py:91
  23.1 1.8 %collective-permute-done.5.side_ref = bf16[256,128]{1,0:T(8,128)(2,1)S(1)} collective-permute-done((bf16[256,128]{1,0:T(8,128)(2,1)S(1)}, bf16[256,128]{1,0:T(8,128)(2,1)S(1)}, u32[]{:S(2)}, u32[]{:S(2)}) %collective-permute-start.5) | collective-permute-done | bytes 65568 | tf_op jit(solution)/shard_map/ppermute | solution.py:103
  24.9 0.5 %collective-permute-done.4.near_ref = bf16[256,128]{1,0:T(8,128)(2,1)S(1)} collective-permute-done((bf16[256,128]{1,0:T(8,128)(2,1)S(1)}, bf16[256,128]{1,0:T(8,128)(2,1)S(1)}, u32[]{:S(2)}, u32[]{:S(2)}) %collective-permute-start.4) | collective-permute-done | bytes 65568 | tf_op jit(solution)/shard_map/ppermute | solution.py:103
  25.5 2.1 %collective-permute-start.9 = (bf16[256,128]{1,0:T(8,128)(2,1)S(1)}, bf16[256,128]{1,0:T(8,128)(2,1)S(1)}, u32[]{:S(2)}, u32[]{:S(2)}) collective-permute-start(bf16[256,128]{1,0:T(8,128)(2,1)S(1)} %shard_map.45.value_ref), channel_id=1, source_target_pairs={{0,7},{1,25},{2,26},{3,4},{4,3},{5,29},{6,30},{7,0},{8,15},{9,17},... | collective-permute-start | bytes 196616 | tf_op jit(solution)/shard_map/ppermute | solution.py:103
  27.5 2.3 %collective-permute-start.8 = (bf16[256,128]{1,0:T(8,128)(2,1)S(1)}, bf16[256,128]{1,0:T(8,128)(2,1)S(1)}, u32[]{:S(2)}, u32[]{:S(2)}) collective-permute-start(bf16[256,128]{1,0:T(8,128)(2,1)S(1)} %shard_map.45.value_ref), channel_id=1, source_target_pairs={{0,4},{1,9},{2,10},{3,7},{4,0},{5,13},{6,14},{7,3},{8,12},{9,1},{1... | collective-permute-start | bytes 196616 | tf_op jit(solution)/shard_map/ppermute | solution.py:103
  30.0 1.0 %collective-permute-done.9.far_ref = bf16[256,128]{1,0:T(8,128)(2,1)S(1)} collective-permute-done((bf16[256,128]{1,0:T(8,128)(2,1)S(1)}, bf16[256,128]{1,0:T(8,128)(2,1)S(1)}, u32[]{:S(2)}, u32[]{:S(2)}) %collective-permute-start.9) | collective-permute-done | bytes 65568 | tf_op jit(solution)/shard_map/ppermute | solution.py:103
  31.0 1.7 %collective-permute-done.8.side_ref = bf16[256,128]{1,0:T(8,128)(2,1)S(1)} collective-permute-done((bf16[256,128]{1,0:T(8,128)(2,1)S(1)}, bf16[256,128]{1,0:T(8,128)(2,1)S(1)}, u32[]{:S(2)}, u32[]{:S(2)}) %collective-permute-start.8) | collective-permute-done | bytes 65568 | tf_op jit(solution)/shard_map/ppermute | solution.py:103
  32.7 0.8 %collective-permute-done.7.near_ref = bf16[256,128]{1,0:T(8,128)(2,1)S(1)} collective-permute-done((bf16[256,128]{1,0:T(8,128)(2,1)S(1)}, bf16[256,128]{1,0:T(8,128)(2,1)S(1)}, u32[]{:S(2)}, u32[]{:S(2)}) %collective-permute-start.7) | collective-permute-done | bytes 65568 | tf_op jit(solution)/shard_map/ppermute | solution.py:103
  33.9 1.0 %collective-permute-done.10.image_other_ref = f32[256,128]{1,0:T(8,128)S(1)} collective-permute-done((f32[256,128]{1,0:T(8,128)S(1)}, f32[256,128]{1,0:T(8,128)S(1)}, u32[]{:S(2)}, u32[]{:S(2)}) %collective-permute-start.10) | collective-permute-done | bytes 131104 | tf_op jit(solution)/shard_map/ppermute | solution.py:91
  34.9 4.5 %shard_map.48 = (f32[64,128]{1,0:T(8,128)}, f32[512,128]{1,0:T(8,128)}) custom-call(f32[128,128]{1,0:T(8,128)S(1)} %shard_map.47.gram_ref, f32[256,128]{1,0:T(8,128)S(1)} %shard_map.46.image_ref, f32[256,128]{1,0:T(8,128)S(1)} %collective-permute-done.10.image_other_ref, bf16[256,512]{1,0:T(8,128)(2,1)S(1)} %get-tuple-element.20.own_ref, ...), custom_call_target="tpu_custom_call" | custom-call | tf_op jit(solution)/shard_map/pallas_call | solution.py:320
  (10 shorter events, 1.0 us)
Async XLA Ops:
  1.5 13.7 %copy-start = (f32[512,128]{1,0:T(8,128)S(1)}, f32[512,128]{1,0:T(8,128)}, u32[]{:S(2)}) copy-start(f32[512,128]{1,0:T(8,128)} %start_ref.1) | copy-start | bytes 786436
  1.5 9.1 %collective-permute-start = (bf16[64,1024]{1,0:T(8,128)(2,1)S(1)}, bf16[64,1024]{1,0:T(8,128)(2,1)S(1)}, u32[]{:S(2)}, u32[]{:S(2)}) collective-permute-start(bf16[64,1024]{1,0:T(8,128)(2,1)S(1)} %shard_map.41), channel_id=1, source_target_pairs={{0,4},{1,2},{2,1},{3,7},{4,0},{5,6},{6,5},{7,3},{8,12},{9,10},{10,... | collective-permute-start | bytes 393224 | tf_op jit(solution)/shard_map/ppermute | solution.py:103
  6.7 6.5 %collective-permute-start.1 = (bf16[64,1024]{1,0:T(8,128)(2,1)S(1)}, bf16[64,1024]{1,0:T(8,128)(2,1)S(1)}, u32[]{:S(2)}, u32[]{:S(2)}) collective-permute-start(bf16[64,1024]{1,0:T(8,128)(2,1)S(1)} %get-tuple-element.15), channel_id=1, source_target_pairs={{0,3},{1,5},{2,6},{3,0},{4,7},{5,1},{6,2},{7,4},{8,11},{9,13},{10,... | collective-permute-start | bytes 393224 | tf_op jit(solution)/shard_map/ppermute | solution.py:103
  7.5 7.8 %collective-permute-start.2 = (bf16[64,1024]{1,0:T(8,128)(2,1)S(1)}, bf16[64,1024]{1,0:T(8,128)(2,1)S(1)}, u32[]{:S(2)}, u32[]{:S(2)}) collective-permute-start(bf16[64,1024]{1,0:T(8,128)(2,1)S(1)} %get-tuple-element.16), channel_id=1, source_target_pairs={{0,7},{1,6},{2,5},{3,4},{4,3},{5,2},{6,1},{7,0},{8,15},{9,14},{10,... | collective-permute-start | bytes 393224 | tf_op jit(solution)/shard_map/ppermute | solution.py:103
  15.7 1.7 %collective-permute-start.3 = (bf16[128,1024]{1,0:T(8,128)(2,1)S(1)}, bf16[128,1024]{1,0:T(8,128)(2,1)S(1)}, u32[]{:S(2)}, u32[]{:S(2)}) collective-permute-start(bf16[128,1024]{1,0:T(8,128)(2,1)S(1)} %get-tuple-element.19), channel_id=1, source_target_pairs={{0,1},{1,0},{2,3},{3,2},{4,5},{5,4},{6,7},{7,6},{8,9},{9,8},{10,11... | collective-permute-start | bytes 786440 | tf_op jit(solution)/shard_map/ppermute | solution.py:91
  17.8 5.2 %collective-permute-start.6 = (bf16[256,128]{1,0:T(8,128)(2,1)S(1)}, bf16[256,128]{1,0:T(8,128)(2,1)S(1)}, u32[]{:S(2)}, u32[]{:S(2)}) collective-permute-start(bf16[256,128]{1,0:T(8,128)(2,1)S(1)} %shard_map.44.value_ref), channel_id=1, source_target_pairs={{0,24},{1,6},{2,5},{3,27},{4,28},{5,2},{6,1},{7,31},{8,16},{9,14},... | collective-permute-start | bytes 196616 | tf_op jit(solution)/shard_map/ppermute | solution.py:103
  20.6 4.3 %collective-permute-start.5 = (bf16[256,128]{1,0:T(8,128)(2,1)S(1)}, bf16[256,128]{1,0:T(8,128)(2,1)S(1)}, u32[]{:S(2)}, u32[]{:S(2)}) collective-permute-start(bf16[256,128]{1,0:T(8,128)(2,1)S(1)} %shard_map.44.value_ref), channel_id=1, source_target_pairs={{0,8},{1,5},{2,6},{3,11},{4,12},{5,1},{6,2},{7,15},{8,0},{9,13},{1... | collective-permute-start | bytes 196616 | tf_op jit(solution)/shard_map/ppermute | solution.py:103
  21.2 4.3 %collective-permute-start.4 = (bf16[256,128]{1,0:T(8,128)(2,1)S(1)}, bf16[256,128]{1,0:T(8,128)(2,1)S(1)}, u32[]{:S(2)}, u32[]{:S(2)}) collective-permute-start(bf16[256,128]{1,0:T(8,128)(2,1)S(1)} %shard_map.44.value_ref), channel_id=1, source_target_pairs={{0,16},{1,2},{2,1},{3,19},{4,20},{5,6},{6,5},{7,23},{8,24},{9,10},... | collective-permute-start | bytes 196616 | tf_op jit(solution)/shard_map/ppermute | solution.py:103
  21.4 12.5 %collective-permute-start.11 = (bf16[256,512]{1,0:T(8,128)(2,1)S(1)}, bf16[256,512]{1,0:T(8,128)(2,1)S(1)}, u32[]{:S(2)}, u32[]{:S(2)}) collective-permute-start(bf16[256,512]{1,0:T(8,128)(2,1)S(1)} %get-tuple-element.21), channel_id=1, source_target_pairs={{0,1},{1,0},{2,3},{3,2},{4,5},{5,4},{6,7},{7,6},{8,9},{9,8},{10,11... | collective-permute-start | bytes 786440 | tf_op jit(solution)/shard_map/ppermute | solution.py:91
  25.5 5.6 %collective-permute-start.9 = (bf16[256,128]{1,0:T(8,128)(2,1)S(1)}, bf16[256,128]{1,0:T(8,128)(2,1)S(1)}, u32[]{:S(2)}, u32[]{:S(2)}) collective-permute-start(bf16[256,128]{1,0:T(8,128)(2,1)S(1)} %shard_map.45.value_ref), channel_id=1, source_target_pairs={{0,7},{1,25},{2,26},{3,4},{4,3},{5,29},{6,30},{7,0},{8,15},{9,17},... | collective-permute-start | bytes 196616 | tf_op jit(solution)/shard_map/ppermute | solution.py:103
  27.5 5.2 %collective-permute-start.8 = (bf16[256,128]{1,0:T(8,128)(2,1)S(1)}, bf16[256,128]{1,0:T(8,128)(2,1)S(1)}, u32[]{:S(2)}, u32[]{:S(2)}) collective-permute-start(bf16[256,128]{1,0:T(8,128)(2,1)S(1)} %shard_map.45.value_ref), channel_id=1, source_target_pairs={{0,4},{1,9},{2,10},{3,7},{4,0},{5,13},{6,14},{7,3},{8,12},{9,1},{1... | collective-permute-start | bytes 196616 | tf_op jit(solution)/shard_map/ppermute | solution.py:103
  29.8 3.7 %collective-permute-start.7 = (bf16[256,128]{1,0:T(8,128)(2,1)S(1)}, bf16[256,128]{1,0:T(8,128)(2,1)S(1)}, u32[]{:S(2)}, u32[]{:S(2)}) collective-permute-start(bf16[256,128]{1,0:T(8,128)(2,1)S(1)} %shard_map.45.value_ref), channel_id=1, source_target_pairs={{0,3},{1,17},{2,18},{3,0},{4,7},{5,21},{6,22},{7,4},{8,11},{9,25},... | collective-permute-start | bytes 196616 | tf_op jit(solution)/shard_map/ppermute | solution.py:103
  33.5 1.4 %collective-permute-start.10 = (f32[256,128]{1,0:T(8,128)S(1)}, f32[256,128]{1,0:T(8,128)S(1)}, u32[]{:S(2)}, u32[]{:S(2)}) collective-permute-start(f32[256,128]{1,0:T(8,128)S(1)} %shard_map.46.image_ref), channel_id=1, source_target_pairs={{0,1},{1,0},{2,3},{3,2},{4,5},{5,4},{6,7},{7,6},{8,9},{9,8},{10,11... | collective-permute-start | bytes 393224 | tf_op jit(solution)/shard_map/ppermute | solution.py:91
